TPU v7x, 32 devices: a whole 2x2x4 slice. The times are simulated.
32 devices in a mesh: dp: 8 (over z, x), mp: 4 (over y, core).
Axes of the slice: x: 2, y: 2, z: 4, core: 2. Of those that a mesh axis runs over, the one named last changes fastest.
Arguments:
- tokens: bfloat16 [1024, 2, 1024], P(('dp', 'mp')), may hold values from -6 to 6
- cotangent: bfloat16 [1024, 2, 1024], P(('dp', 'mp')), may hold values from -6 to 6
- char_start: int32 [1024, 2], P(('dp', 'mp')), may hold values 0 or 1
- lengths: int32 [2], replicated, may hold values from 768 to 1024, as said below
- norm_gain: float32 [2, 1024], replicated, may hold values from 0.1 to 1.9
- input_proj: bfloat16 [2, 2, 1024, 2048], P(None, None, None, 'mp'), may hold values from -0.1875 to 0.1875
- conv_kernel: bfloat16 [2, 4, 2048], P(None, None, 'mp'), may hold values from -3 to 3
- conv_bias: float32 [2, 2048], P(None, 'mp'), may hold values from -3 to 3
- state_proj: bfloat16 [2, 2048, 96], P(None, 'mp'), may hold values from -0.125 to 0.125
- step_proj: bfloat16 [2, 64, 2048], P(None, None, 'mp'), may hold values from -0.75 to 0.75
- step_bias: float32 [2, 2048], P(None, 'mp'), may hold values from -12 to -2.9
- decay_log: float32 [2, 16, 2048], P(None, None, 'mp'), may hold values from 0 to 2.77
- skip_gain: float32 [2, 2048], P(None, 'mp'), may hold values from 0.5 to 1.5
- output_proj: bfloat16 [2, 2048, 1024], P(None, 'mp'), may hold values from -0.25 to 0.25
Outputs:
- layer_output: bfloat16 [1024, 2, 1024], P(('dp', 'mp'))
- tokens_grad: float32 [1024, 2, 1024], P(('dp', 'mp'))
- norm_gain_grad: float32 [2, 1024], replicated
- input_proj_grad: float32 [2, 2, 1024, 2048], P(None, None, None, 'mp')
- conv_kernel_grad: float32 [2, 4, 2048], P(None, None, 'mp')
- conv_bias_grad: float32 [2, 2048], P(None, 'mp')
- state_proj_grad: float32 [2, 2048, 96], P(None, 'mp')
- step_proj_grad: float32 [2, 64, 2048], P(None, None, 'mp')
- step_bias_grad: float32 [2, 2048], P(None, 'mp')
- decay_log_grad: float32 [2, 16, 2048], P(None, None, 'mp')
- skip_gain_grad: float32 [2, 2048], P(None, 'mp')
- output_proj_grad: float32 [2, 2048, 1024], P(None, 'mp')
Inputs may be any that keep to these rules, and one draw needn't show every extreme that they name: `lengths`: at least one sequence uses all 1024 positions.
All inputs are finite; a program needn't handle non-finite values. No bound on the sum of `char_start` on one device may be relied on, other than what follows from the above.
Results may differ from a plain program's by a relative error of at most 0.015.
The roundings to bfloat16 on the way count: a program that leaves them out, or rounds other values in their place, can miss the bound.
Values may be sent and summed in bfloat16 or wider, within the bound.
A program may use at most 128 MiB of HBM per device.

v0:
```python
import functools
import math

import jax
import jax.numpy as jnp
from jax import lax
from jax.experimental import pallas as pl
from jax.experimental.pallas import tpu as pltpu
from jax.sharding import PartitionSpec as P

EPS = 1e-05


def from_behind(array, axis, by):
    peers = lax.axis_size(axis)
    pairs = [(i, i + by) for i in range(peers) if 0 <= i + by < peers]
    return lax.ppermute(array, axis, pairs)


def entering(part, axis, combine, reverse):
    count = lax.axis_size(axis)
    place = lax.axis_index(axis)
    ahead = count - 1 - place if reverse else place
    gathered = jax.tree.map(lambda a: lax.all_gather(a, axis), part)

    def one(step, state):
        source = count - 1 - step if reverse else step
        return combine(
            state, jax.tree.map(lambda a: lax.dynamic_index_in_dim(a, source, 0, False), gathered)
        )

    return lax.fori_loop(0, ahead, one, jnp.zeros_like(part[1]))


def silu_slope(value):
    sigma = jax.nn.sigmoid(value)
    return sigma * (1.0 + value * (1.0 - sigma))


GRP = 16

def spread(dst, part):
    for g in range(dst.shape[0]):
        dst[g] = part[:, g * GRP:(g + 1) * GRP]

def put(w, k, y):
    y = y[:8] + y[8:]
    for j in range(w.shape[0]):
        w[j, k * 8:(k + 1) * 8, :] = y[:, j * 128:(j + 1) * 128]

def take(out, base, w):
    for j in range(w.shape[0]):
        out[pl.ds(base, GRP), j * 128:(j + 1) * 128] = sum(w[j, pl.ds(i, GRP, stride=8), :] for i in range(8))

def totals_scan(dt, du, bg, a2, first):
    def step(g, hs):
        hs = list(hs)
        base = pl.multiple_of(g * GRP, GRP)
        bt = bg[g]
        for k in range(GRP):
            s = k % len(hs)
            d = dt[pl.ds(base + k, 1), :]
            x = du[pl.ds(base + k, 1), :]
            hs[s] = jnp.exp2(d * a2) * hs[s] + x * bt[:, k:k + 1]
        return tuple(hs)
    return lax.fori_loop(0, bg.shape[0], step, first)

def output_scan(dt, du, bg, cg, a2, first, h_all, w, ys):
    def step(g, hs):
        hs = list(hs)
        base = pl.multiple_of(g * GRP, GRP)
        bt = bg[g]
        ct = cg[g]
        for k in range(GRP):
            s = k % len(hs)
            d = dt[pl.ds(base + k, 1), :]
            x = du[pl.ds(base + k, 1), :]
            hs[s] = jnp.exp2(d * a2) * hs[s] + x * bt[:, k:k + 1]
            h_all[base + k] = hs[s]
            y = hs[s] * ct[:, k:k + 1]
            put(w, k, y)
        take(ys, base, w)
        return tuple(hs)
    return lax.fori_loop(0, bg.shape[0], step, first)

def adjoint_totals(dt, dy, cg, a2, first):
    def step(i, ks):
        g = cg.shape[0] - 1 - i
        ks = list(ks)
        base = pl.multiple_of(g * GRP, GRP)
        ct = cg[g]
        for k in reversed(range(GRP)):
            s = k % len(ks)
            d = dt[pl.ds(base + k, 1), :]
            y = dy[pl.ds(base + k, 1), :]
            ks[s] = jnp.exp2(d * a2) * (ks[s] + y * ct[:, k:k + 1])
        return tuple(ks)
    return lax.fori_loop(0, cg.shape[0], step, first)

def adjoint_scan(dt, du, dy, bg, cg, a2, an, first, h_all, q_all, w1, w2, s1, s2):
    groups = cg.shape[0]
    seqs = len(first)
    def step(i, carry):
        ks, acc = carry
        g = groups - 1 - i
        ks = list(ks)
        base = pl.multiple_of(g * GRP, GRP)
        bt = bg[g]
        ct = cg[g]
        for k in reversed(range(GRP)):
            s = k % seqs
            r = base + k
            d = dt[pl.ds(r, 1), :]
            y = dy[pl.ds(r, 1), :]
            q = ks[s] + y * ct[:, k:k + 1]
            q_all[r] = q.astype(q_all.dtype)
            kn = jnp.exp2(d * a2) * q
            ks[s] = kn
            fa = kn * h_all[r]
            acc = acc + fa * d
            put(w1, k, fa * an)
            put(w2, k, q * bt[:, k:k + 1])
        take(s1, base, w1)
        take(s2, base, w2)
        return tuple(ks), acc
    return lax.fori_loop(0, groups, step, (first, jnp.zeros_like(a2)))[1]

def state_sums(all_rows, skip, vec, out):
    states = all_rows.shape[1]
    wide = 128
    for j in range(0, vec.shape[0], wide):
        right = vec[j:j + wide, :].astype(jnp.bfloat16)
        total = jnp.zeros((states, wide), jnp.float32)
        lane = lax.broadcasted_iota(jnp.int32, (states, wide), 1)
        for b in range(0, wide, GRP):
            left = all_rows[skip + j + b:skip + j + b + GRP].astype(jnp.bfloat16).reshape(GRP * states, -1)
            both = lax.dot_general(left, right, (((1,), (1,)), ((), ())), preferred_element_type=jnp.float32)
            for k in range(GRP):
                total = total + jnp.where(lane == b + k, both[k * states:(k + 1) * states], 0.0)
        out[:, j:j + wide] = total


F32 = jnp.float32
VMEM = pltpu.VMEM
LOG2E = math.log2(math.e)


def rates(dlog):
    an = -jnp.exp(dlog[...])
    return an, an * LOG2E


def totals_kernel(dt, du, bt, dlog, out, bg):
    spread(bg, bt[...])
    an, a2 = rates(dlog)
    zero = jnp.zeros_like(a2)
    for s, h in enumerate(totals_scan(dt, du, bg, a2, (zero,) * out.shape[0])):
        out[s] = h


def output_kernel(dt, du, bt, ct, dlog, first, ys, bg, cg, h_all, w):
    spread(bg, bt[...])
    spread(cg, ct[...])
    an, a2 = rates(dlog)
    seqs = first.shape[0]
    output_scan(dt, du, bg, cg, a2, tuple(first[s] for s in range(seqs)), h_all, w, ys)


def back_totals_kernel(dt, dy, ct, dlog, out, cg):
    spread(cg, ct[...])
    an, a2 = rates(dlog)
    zero = jnp.zeros_like(a2)
    for s, h in enumerate(adjoint_totals(dt, dy, cg, a2, (zero,) * out.shape[0])):
        out[s] = h


def back_kernel(dt, du, dy, bt, ct, dlog, first, last, s1, s2, dbt, dct, acc, bg, cg, h_all, q_all, w1, w2):
    spread(bg, bt[...])
    spread(cg, ct[...])
    an, a2 = rates(dlog)
    seqs = first.shape[0]
    rows = dt.shape[0]
    for s in range(seqs):
        h_all[s] = first[s]
    begin = tuple(first[s] for s in range(seqs))
    output_scan(dt, du, bg, cg, a2, begin, h_all.at[pl.ds(seqs, rows)], w1, s1)
    end = tuple(last[s] for s in range(seqs))
    acc[...] = an * adjoint_scan(dt, du, dy, bg, cg, a2, an, end, h_all, q_all, w1, w2, s1, s2)
    state_sums(q_all, 0, du, dbt)
    state_sums(h_all, seqs, dy, dct)


def scan_call(kernel, outs, scratch, *args):
    return pl.pallas_call(
        kernel,
        out_shape=[jax.ShapeDtypeStruct(o, F32) for o in outs],
        scratch_shapes=[VMEM(s, t) for s, t in scratch],
        compiler_params=pltpu.CompilerParams(vmem_limit_bytes=50 * 2**20),
    )(*args)


def flat(value):
    return value.reshape((value.shape[0] * value.shape[1],) + value.shape[2:])


def segment_totals(stride_delta, b_part, u_float, dlog):
    dt = flat(stride_delta)
    rows, chans = dt.shape
    states = dlog.shape[0]
    seqs = stride_delta.shape[1]
    out = scan_call(
        totals_kernel, [(seqs, states, chans)], [((rows // GRP, states, GRP), F32)],
        dt, dt * flat(u_float), flat(b_part).T, dlog,
    )[0]
    return (jnp.sum(stride_delta, axis=0), out)


def segment_outputs(carried, stride_delta, b_part, c_part, u_float, dlog):
    dt = flat(stride_delta)
    rows, chans = dt.shape
    states = dlog.shape[0]
    small = ((rows // GRP, states, GRP), F32)
    out = scan_call(
        output_kernel, [(rows, chans)],
        [small, small, ((rows, states, chans), F32), ((chans // 128, GRP * 8, 128), F32)],
        dt, dt * flat(u_float), flat(b_part).T, flat(c_part).T, dlog, carried,
    )[0]
    return out.reshape(stride_delta.shape)


def adjoint_ends(stride_delta, c_part, dscan, dlog):
    dt = flat(stride_delta)
    rows, chans = dt.shape
    states = dlog.shape[0]
    seqs = stride_delta.shape[1]
    out = scan_call(
        back_totals_kernel, [(seqs, states, chans)], [((rows // GRP, states, GRP), F32)],
        dt, flat(dscan), flat(c_part).T, dlog,
    )[0]
    return (jnp.sum(stride_delta, axis=0), out)


def adjoint_grads(incoming, first, stride_delta, b_part, c_part, u_float, dscan, dlog):
    dt = flat(stride_delta)
    rows, chans = dt.shape
    states = dlog.shape[0]
    seqs = stride_delta.shape[1]
    small = ((rows // GRP, states, GRP), F32)
    work = ((chans // 128, GRP * 8, 128), F32)
    s1, s2, dbt, dct, acc = scan_call(
        back_kernel,
        [(rows, chans), (rows, chans), (states, rows), (states, rows), (states, chans)],
        [small, small, ((rows + seqs, states, chans), F32), ((rows, states, chans), jnp.bfloat16), work, work],
        dt, dt * flat(u_float), flat(dscan), flat(b_part).T, flat(c_part).T, dlog, first, incoming,
    )
    shape = stride_delta.shape
    s1, s2 = s1.reshape(shape), s2.reshape(shape)
    narrow = shape[:2] + (states,)
    return (s1 + s2 * u_float, s2 * stride_delta, dbt.T.reshape(narrow), dct.T.reshape(narrow), acc)


def joined(totals, decay, reverse):
    def combine(state, new):
        return new[1] + jnp.exp(new[0][:, None, :] * decay) * state
    return entering(totals, "dp", combine, reverse)


def conv_apply(earlier_rows, conv_in, kernel, cbias):
    width = kernel.shape[0]
    seg_rows = conv_in.shape[0]
    extended = jnp.concatenate([earlier_rows, conv_in], axis=0).astype(jnp.float32)
    kern = kernel.astype(jnp.float32)
    conv_pre = cbias + sum((extended[tap : tap + seg_rows] * kern[tap] for tap in range(width)))
    return (extended, kern, conv_pre)


def scan_inputs(projection_totals, timestep_projector, timestep_bias, dlog):
    rank = timestep_projector.shape[0]
    nstate = dlog.shape[0]
    reduced_rank = projection_totals[..., :rank].astype(jnp.bfloat16)
    b_part = projection_totals[..., rank : rank + nstate]
    c_part = projection_totals[..., rank + nstate :]
    pre_step = (
        jnp.einsum(
            "psr,rc->psc", reduced_rank, timestep_projector, preferred_element_type=jnp.float32
        )
        + timestep_bias
    )
    return (reduced_rank, b_part, c_part, pre_step, jax.nn.softplus(pre_step), -jnp.exp(dlog))


def forward_layer(
    resid,
    gain,
    in_proj,
    kernel,
    cbias,
    state_projector,
    timestep_projector,
    timestep_bias,
    dlog,
    skipg,
    oproj,
):
    inv_rms = lax.rsqrt(jnp.mean(resid * resid, axis=-1, keepdims=True) + EPS)
    normed = (resid * inv_rms * gain).astype(jnp.bfloat16)
    full_normed = lax.all_gather(normed, "mp", axis=0, tiled=True)
    mixed_in = jnp.einsum("psd,kdc->pskc", full_normed, in_proj, preferred_element_type=jnp.float32)
    conv_in = mixed_in[:, :, 0].astype(jnp.bfloat16)
    gate_in = mixed_in[:, :, 1]
    width = kernel.shape[0]
    earlier_rows = from_behind(conv_in[conv_in.shape[0] - (width - 1) :], "dp", 1)
    extended, kern, conv_pre = conv_apply(earlier_rows, conv_in, kernel, cbias)
    signal_reduced = jax.nn.silu(conv_pre).astype(jnp.bfloat16)
    projection_totals = lax.psum(
        jnp.einsum(
            "psc,cr->psr", signal_reduced, state_projector, preferred_element_type=jnp.float32
        ),
        "mp",
    )
    reduced_rank, b_part, c_part, pre_step, stride_delta, decay = scan_inputs(
        projection_totals, timestep_projector, timestep_bias, dlog
    )
    u_float = signal_reduced.astype(jnp.float32)
    carried = joined(segment_totals(stride_delta, b_part, u_float, dlog), decay, False)
    scan_out = (
        segment_outputs(carried, stride_delta, b_part, c_part, u_float, dlog) + skipg * u_float
    )
    gated = (scan_out * jax.nn.silu(gate_in)).astype(jnp.bfloat16)
    branch = lax.psum_scatter(
        jnp.einsum("psc,cd->psd", gated, oproj, preferred_element_type=jnp.float32),
        "mp",
        scatter_dimension=0,
        tiled=True,
    )
    saved = (
        resid,
        inv_rms,
        normed,
        full_normed,
        conv_in,
        earlier_rows,
        gate_in,
        signal_reduced,
        projection_totals,
        carried,
        scan_out,
        gated,
    )
    return (resid + branch, saved)


def backward_layer(
    grad_resid,
    saved,
    gain,
    in_proj,
    kernel,
    cbias,
    state_projector,
    timestep_projector,
    timestep_bias,
    dlog,
    skipg,
    oproj,
):
    (
        resid,
        inv_rms,
        normed,
        full_normed,
        conv_in,
        earlier_rows,
        gate_in,
        signal_reduced,
        projection_totals,
        carried,
        scan_out,
        gated,
    ) = saved
    out_low = grad_resid.astype(jnp.bfloat16)
    piece = lax.all_gather(out_low, "mp", axis=0, tiled=True)
    rows_grad = jnp.einsum("psd,cd->psc", piece, oproj, preferred_element_type=jnp.float32)
    dgated = rows_grad
    oacc = jnp.einsum("psc,psd->cd", gated, piece, preferred_element_type=jnp.float32)
    dgated, oproj_grad = (dgated, oacc)
    dscan = dgated * jax.nn.silu(gate_in)
    dgate_in = dgated * scan_out * silu_slope(gate_in)
    u_float = signal_reduced.astype(jnp.float32)
    skip_grad = jnp.sum(dscan * u_float, axis=(0, 1))
    reduced_rank, b_part, c_part, pre_step, stride_delta, decay = scan_inputs(
        projection_totals, timestep_projector, timestep_bias, dlog
    )
    incoming = joined(adjoint_ends(stride_delta, c_part, dscan, dlog), decay, True)
    dstep, du_piece, db_part, dc_part, dlog_grad = adjoint_grads(
        incoming, carried, stride_delta, b_part, c_part, u_float, dscan, dlog
    )
    du_scan = du_piece + skipg * dscan
    dpre_low = (dstep * jax.nn.sigmoid(pre_step)).astype(jnp.bfloat16)
    tbias_grad = jnp.sum(dpre_low.astype(jnp.float32), axis=(0, 1))
    tproj_grad = jnp.einsum(
        "psr,psc->rc", reduced_rank, dpre_low, preferred_element_type=jnp.float32
    )
    drank = jnp.einsum(
        "psc,rc->psr", dpre_low, timestep_projector, preferred_element_type=jnp.float32
    )
    dproj = lax.psum(jnp.concatenate([drank, db_part, dc_part], axis=-1), "mp")
    dproj_low = dproj.astype(jnp.bfloat16)
    sproj_grad = jnp.einsum(
        "psc,psr->cr", signal_reduced, dproj_low, preferred_element_type=jnp.float32
    )
    du_total = du_scan + jnp.einsum(
        "psr,cr->psc", dproj_low, state_projector, preferred_element_type=jnp.float32
    )
    extended, kern, conv_pre = conv_apply(earlier_rows, conv_in, kernel, cbias)
    dconv = du_total * silu_slope(conv_pre)
    width = kernel.shape[0]
    seg_rows = conv_in.shape[0]
    cbias_grad = jnp.sum(dconv, axis=(0, 1))
    kernel_grad = jnp.stack(
        [jnp.sum(dconv * extended[tap : tap + seg_rows], axis=(0, 1)) for tap in range(width)]
    )
    dextended = sum(
        (
            jnp.pad(dconv * kern[tap], ((tap, width - 1 - tap), (0, 0), (0, 0)))
            for tap in range(width)
        )
    )
    from_later = from_behind(dextended[: width - 1], "dp", -1)
    dconv_in = dextended[width - 1 :] + jnp.pad(
        from_later, ((seg_rows - width + 1, 0), (0, 0), (0, 0))
    )
    dmixed = jnp.stack([dconv_in, dgate_in], axis=2).astype(jnp.bfloat16)
    in_grad = jnp.einsum("psd,pskc->kdc", full_normed, dmixed, preferred_element_type=jnp.float32)
    dnormed = lax.psum_scatter(
        jnp.einsum("pskc,kdc->psd", dmixed, in_proj, preferred_element_type=jnp.float32),
        "mp",
        scatter_dimension=0,
        tiled=True,
    )
    gain_part = jnp.sum(dnormed * resid * inv_rms, axis=(0, 1))
    dnorm_in = dnormed * gain
    cubed = inv_rms * inv_rms * inv_rms
    grad_next = (
        grad_resid
        + inv_rms * dnorm_in
        - resid * cubed * jnp.mean(dnorm_in * resid, axis=-1, keepdims=True)
    )
    grads = (
        in_grad,
        kernel_grad,
        cbias_grad,
        sproj_grad,
        tproj_grad,
        tbias_grad,
        dlog_grad,
        skip_grad,
        oproj_grad,
    )
    return (grad_next, grads, gain_part)


def body(
    tokens,
    cotangent,
    char_start,
    lengths,
    norm_gain,
    input_proj,
    conv_kernel,
    conv_bias,
    state_proj,
    step_proj,
    step_bias,
    decay_log,
    skip_gain,
    output_proj,
):
    layers = norm_gain.shape[0]
    resid = tokens.astype(jnp.float32)
    saves = []
    for index in range(layers):
        resid, saved = forward_layer(
            resid,
            norm_gain[index],
            input_proj[index],
            conv_kernel[index],
            conv_bias[index],
            state_proj[index],
            step_proj[index],
            step_bias[index],
            decay_log[index],
            skip_gain[index],
            output_proj[index],
        )
        saves.append(saved)
    layer_output = resid.astype(jnp.bfloat16)
    rows = tokens.shape[0]
    position = lax.axis_index(("dp", "mp")) * rows + lax.broadcasted_iota(
        jnp.int32, (rows, tokens.shape[1]), 0
    )
    weight = jnp.where(position < lengths[None, :], 0.5 + char_start.astype(jnp.float32), 0.0)
    grad_resid = cotangent.astype(jnp.float32) * weight[:, :, None]
    ordered = []
    gain_parts = []
    for index in reversed(range(layers)):
        grad_resid, layer_grads, gain_part = backward_layer(
            grad_resid,
            saves[index],
            norm_gain[index],
            input_proj[index],
            conv_kernel[index],
            conv_bias[index],
            state_proj[index],
            step_proj[index],
            step_bias[index],
            decay_log[index],
            skip_gain[index],
            output_proj[index],
        )
        (
            grad_in,
            grad_kernel,
            grad_cbias,
            grad_sproj,
            grad_tproj,
            grad_tbias,
            grad_dlog,
            grad_skip,
            grad_oproj,
        ) = layer_grads
        layer_grads = lax.psum(
            (
                grad_in,
                grad_kernel,
                grad_cbias,
                grad_sproj,
                grad_tproj,
                grad_tbias,
                grad_dlog,
                grad_skip,
                grad_oproj,
            ),
            "dp",
        )
        ordered.insert(0, layer_grads)
        gain_parts.insert(0, gain_part)
    stacked = [jnp.stack([entry[slot] for entry in ordered]) for slot in range(9)]
    gain_grad = lax.psum(jnp.stack(gain_parts), ("dp", "mp"))
    return (
        layer_output,
        grad_resid,
        gain_grad,
        stacked[0],
        stacked[1],
        stacked[2],
        stacked[3],
        stacked[4],
        stacked[5],
        stacked[6],
        stacked[7],
        stacked[8],
    )


def solution(mesh):
    return jax.shard_map(
        body,
        mesh=mesh,
        in_specs=(
            P(("dp", "mp"), None, None),
            P(("dp", "mp"), None, None),
            P(("dp", "mp"), None),
            P(),
            P(),
            P(None, None, None, "mp"),
            P(None, None, "mp"),
            P(None, "mp"),
            P(None, "mp", None),
            P(None, None, "mp"),
            P(None, "mp"),
            P(None, None, "mp"),
            P(None, "mp"),
            P(None, "mp", None),
        ),
        out_specs=(
            P(("dp", "mp"), None, None),
            P(("dp", "mp"), None, None),
            P(),
            P(None, None, None, "mp"),
            P(None, None, "mp"),
            P(None, "mp"),
            P(None, "mp", None),
            P(None, None, "mp"),
            P(None, "mp"),
            P(None, None, "mp"),
            P(None, "mp"),
            P(None, "mp", None),
        ),
        check_vma=False,
    )
```

profile of v0, /device:TPU:0, one launch (start us, length us, event | category | flops | bytes accessed | tf_op | source)
XLA Modules:
  0.0 1066.0 jit_solution(16486336982279701594)
XLA Ops:
  10.7 8.6 all_gather.52
  19.3 2.5 fusion.6
  21.9 3.5 collective-permute-start
  30.2 31.7 %all-reduce.17.cloned.1.call-done = f32[128,2,96]{0,2,1:T(8,128)} async-done(((f32[128,2,96]{0,2,1:T(8,128)}), f32[128,2,96]{0,2,1:T(8,128)}) %all-reduce.17.cloned.1.call-update) | async-done | bytes 98320 | tf_op jit(solution)/shard_map/psum | solution.py:315
  64.6 30.5 %all-gather.6 = f32[8,2,512]{2,1,0:T(2,128)S(1)} all-gather(f32[1,2,512]{2,1,0:T(2,128)S(1)} %bitcast.317), channel_id=3, replica_groups=mesh['dp'=8,'mp'=4] {'dp'}, dimensions={0}, use_global_device_ids=true | all-gather | bytes 36864 | tf_op jit(solution)/shard_map/all_gather | solution.py:24
  95.9 2.1 shard_map.229
  98.1 31.5 %all-gather = f32[16,16,512]{2,1,0:T(8,128)S(1)} all-gather(f32[2,16,512]{2,1,0:T(8,128)S(1)} %shard_map.229), channel_id=2, replica_groups=mesh['dp'=8,'mp'=4] {'dp'}, dimensions={0}, use_global_device_ids=true | all-gather | bytes 589824 | tf_op jit(solution)/shard_map/all_gather | solution.py:24
  129.7 3.3 shard_map.230
  133.3 1.4 multiply_convert_fusion.4
  134.7 2.7 fusion.26
  137.8 6.5 all_gather.62
  144.3 18.5 %reduce-scatter.5.cloned.1.call-done = f32[32,2,1024]{2,0,1:T(8,128)} async-done(((f32[128,2,1024]{2,0,1:T(8,128)}), f32[32,2,1024]{2,0,1:T(8,128)}) %reduce-scatter.5.cloned.1.call-update) | async-done | bytes 262160 | tf_op jit(solution)/shard_map/reduce_scatter | solution.py:330
  164.8 6.8 all_gather.57
  171.6 2.5 fusion.104
  174.1 3.4 collective-permute-start.1
  177.5 1.3 collective-permute-done.1
  179.0 2.5 multiply_reduce_fusion
  182.8 1.4 copy.125
  185.0 30.1 %all-reduce.19.cloned.1.call-done = f32[128,2,96]{0,2,1:T(8,128)} async-done(((f32[128,2,96]{0,2,1:T(8,128)}), f32[128,2,96]{0,2,1:T(8,128)}) %all-reduce.19.cloned.1.call-update) | async-done | bytes 98320 | tf_op jit(solution)/shard_map/psum | solution.py:315
  218.6 30.7 %all-gather.7 = f32[8,2,512]{2,1,0:T(2,128)S(1)} all-gather(f32[1,2,512]{2,1,0:T(2,128)S(1)} %bitcast.318), channel_id=5, replica_groups=mesh['dp'=8,'mp'=4] {'dp'}, dimensions={0}, use_global_device_ids=true | all-gather | bytes 36864 | tf_op jit(solution)/shard_map/all_gather | solution.py:24
  250.1 2.2 shard_map.233
  252.3 31.7 %all-gather.4 = f32[16,16,512]{2,1,0:T(8,128)S(1)} all-gather(f32[2,16,512]{2,1,0:T(8,128)S(1)} %shard_map.233), channel_id=6, replica_groups=mesh['dp'=8,'mp'=4] {'dp'}, dimensions={0}, use_global_device_ids=true | all-gather | bytes 589824 | tf_op jit(solution)/shard_map/all_gather | solution.py:24
  284.5 2.1 shard_map.231
  286.6 31.2 %all-gather.2 = f32[16,16,512]{2,1,0:T(8,128)S(1)} all-gather(f32[2,16,512]{2,1,0:T(8,128)S(1)} %shard_map.231), channel_id=4, replica_groups=mesh['dp'=8,'mp'=4] {'dp'}, dimensions={0}, use_global_device_ids=true | all-gather | bytes 589824 | tf_op jit(solution)/shard_map/all_gather | solution.py:24
  317.9 3.3 shard_map.232
  321.2 12.0 %shard_map.234 = (f32[256,512]{1,0:T(8,128)S(1)}, f32[256,512]{1,0:T(8,128)S(1)}, f32[16,256]{1,0:T(8,128)S(1)}, f32[16,256]{1,0:T(8,128)S(1)}, f32[16,512]{1,0:T(8,128)}) custom-call(f32[256,512]{1,0:T(8,128)S(1)} %reshape.197.dt, f32[256,512]{1,0:T(8,128)S(1)} %mul.633.du, f32[256,512]{1,0:T(8,128)S(1)} %reshape.202.dy, f32[16,256]{1,0:T(8,128)S(1)} %bitcast.293, ...), custom_call_target="tpu_custom_call" | custom-call | tf_op jit(solution)/shard_map/pallas_call | solution.py:194
  334.8 1.4 reshape.203
  336.9 1.4 reshape.204
  338.3 3.3 convert_reduce_fusion
  341.8 11.1 %psum.163 = bf16[128,2,96]{0,2,1:T(8,128)(2,1)S(1)} all-reduce(f32[128,2,96]{0,2,1:T(8,128)S(1)} %pad_maximum_fusion.10), channel_id=1, replica_groups=mesh['dp'=8,'mp'=4] {'mp'}, use_global_device_ids=true, to_apply=%region_14.15 | all-reduce | flops 24576 | bytes 147456 | tf_op jit(solution)/shard_map/psum | solution.py:407
  353.0 3.7 multiply_reduce_fusion.5
  356.8 1.6 collective-permute-start.2
  358.7 4.0 collective-permute-done.2
  362.8 1.7 fusion.12
  365.2 22.6 %reduce-scatter.9.cloned.1.call-done = f32[32,2,1024]{2,0,1:T(8,128)} async-done(((f32[128,2,1024]{2,0,1:T(8,128)}), f32[32,2,1024]{2,0,1:T(8,128)}) %reduce-scatter.9.cloned.1.call-update) | async-done | bytes 262160 | tf_op jit(solution)/shard_map/reduce_scatter | solution.py:435
  387.8 1.7 multiply_reduce_fusion.10
  390.6 6.8 all_gather.65
  397.4 3.5 multiply_reduce_fusion.1
  402.5 2.2 shard_map.235
  404.7 33.2 %all-gather.5 = f32[16,16,512]{2,1,0:T(8,128)} all-gather(f32[2,16,512]{2,1,0:T(8,128)S(1)} %shard_map.235), channel_id=7, replica_groups=mesh['dp'=8,'mp'=4] {'dp'}, dimensions={0}, use_global_device_ids=true | all-gather | bytes 589824 | tf_op jit(solution)/shard_map/all_gather | solution.py:24
  438.0 11.3 %while.47 = (s32[]{:T(128)}, f32[2,16,512]{2,1,0:T(8,128)S(1)}, s32[]{:T(128)}, f32[8,2,16,512]{3,2,1,0:T(8,128)}, f32[8,2,512]{2,1,0:T(2,128)}, /*index=5*/f32[...) while((s32[]{:T(128)}, f32[2,16,512]{2,1,0:T(8,128)S(1)}, s32[]{:T(128)}, ...), condition=%wide.region_18.19_spmd, body=%wide.region_17.18_spmd.sunk | while | flops 49158 | bytes 241827 | solution.py:32
  450.0 12.8 %shard_map.236 = (f32[256,512]{1,0:T(8,128)S(1)}, f32[256,512]{1,0:T(8,128)S(1)}, f32[16,256]{1,0:T(8,128)S(1)}, f32[16,256]{1,0:T(8,128)S(1)}, f32[16,512]{1,0:T(8,128)}) custom-call(f32[256,512]{1,0:T(8,128)S(1)} %reshape.192.dt, f32[256,512]{1,0:T(8,128)S(1)} %mul.608.du, f32[256,512]{1,0:T(8,128)S(1)} %reshape.207.dy, f32[16,256]{1,0:T(8,128)S(1)} %bitcast.287, ...), custom_call_target="tpu_custom_call" | custom-call | tf_op jit(solution)/shard_map/pallas_call | solution.py:194
  463.8 1.9 convert_reduce_fusion.1
  466.7 11.0 %psum.164 = bf16[128,2,96]{0,2,1:T(8,128)(2,1)S(1)} all-reduce(f32[128,2,96]{0,2,1:T(8,128)S(1)} %pad_maximum_fusion.11), channel_id=1, replica_groups=mesh['dp'=8,'mp'=4] {'mp'}, use_global_device_ids=true, to_apply=%region_19.20 | all-reduce | flops 24576 | bytes 147456 | tf_op jit(solution)/shard_map/psum | solution.py:407
  477.8 2.7 multiply_reduce_fusion.9
  480.8 1.3 collective-permute-start.3
  482.8 3.6 collective-permute-done.3
  486.6 3.4 fusion.15
  490.1 2.7 fusion.22
  494.6 1.8 convolution_bitcast_fusion.2
  496.4 2.8 convolution_bitcast_fusion
  500.9 1.8 convolution_bitcast_fusion.3
  502.7 2.8 convolution_bitcast_fusion.1
  505.6 48.5 %all-reduce.21.cloned.1.call-done = (f32[1,4,512]{2,1,0:T(4,128)}, f32[1,4,512]{2,1,0:T(4,128)}, f32[1,512]{1,0:T(1,128)}, f32[1,512]{1,0:T(1,128)}, f32[1,512]{...) async-done(((f32[1,4,512]{2,1,0:T(4,128)}, f32[1,4,512]{2,1,0:T(4,128)}, ...) | async-done | bytes 94224 | tf_op jit(solution)/shard_map/psum | solution.py:532
  554.1 1.3 pad_maximum_fusion.15
  557.9 1.3 pad_maximum_fusion.13
  559.2 1.4 pad_maximum_fusion.12
  560.6 20.1 %reduce-scatter.11.cloned.1.call-done = f32[32,2,1024]{2,0,1:T(8,128)} async-done(((f32[128,2,1024]{2,0,1:T(8,128)}), f32[32,2,1024]{2,0,1:T(8,128)}) %reduce-scatter.11.cloned.1.call-update) | async-done | bytes 262160 | tf_op jit(solution)/shard_map/reduce_scatter | solution.py:435
  581.8 26.5 %reduce-scatter.7.cloned.1.call-done = f32[32,2,1024]{2,0,1:T(8,128)} async-done(((f32[128,2,1024]{2,0,1:T(8,128)}), f32[32,2,1024]{2,0,1:T(8,128)}) %reduce-scatter.7.cloned.1.call-update) | async-done | bytes 262160 | tf_op jit(solution)/shard_map/reduce_scatter | solution.py:330
  611.3 44.2 %psum.165 = f32[2,1024]{1,0:T(2,128)} all-reduce(f32[2,1024]{1,0:T(2,128)S(1)} %pad_maximum_fusion.14), channel_id=1, replica_groups=mesh['dp'=8,'mp'=4] {'dp','mp'}, use_global_device_ids=true, to_apply=%region_24.25 | all-reduce | flops 2048 | bytes 16384 | tf_op jit(solution)/shard_map/psum | solution.py:549
  655.5 380.8 %all-reduce.23.cloned.1.call-done = (f32[1,2,1024,512]{2,3,1,0:T(8,128)}, f32[1,2,1024,512]{2,3,1,0:T(8,128)}, f32[1,512,96]{1,2,0:T(8,128)}, f32[1,512,96]{1,2,...) async-done(((f32[1,2,1024,512]{2,3,1,0:T(8,128)}, f32[1,2,1024,512]{2,3,1,0:T(8,128)}, ...) | async-done | bytes 13238288 | tf_op jit(solution)/shard_map/psum | solution.py:532
  1036.3 8.4 pad_maximum_fusion
  1044.7 8.8 copy.147
  1055.1 4.0 pad_maximum_fusion.1
  (337 shorter events, 53.9 us)
Async XLA Ops:
  7.2 18.2 %copy-start.54 = (f32[2,16,512]{2,1,0:T(8,128)S(1)}, f32[2,16,512]{2,1,0:T(8,128)}, u32[]{:S(2)}) copy-start(f32[2,16,512]{2,1,0:T(8,128)} %param.33) | copy-start | bytes 196612
  7.2 18.3 %copy-start.81 = (f32[2,512]{1,0:T(2,128)S(1)}, f32[2,512]{1,0:T(2,128)}, u32[]{:S(2)}) copy-start(f32[2,512]{1,0:T(2,128)} %param.29) | copy-start | bytes 12292
  7.2 18.9 %copy-start.79 = (bf16[2,4,512]{2,1,0:T(4,128)(2,1)S(1)}, bf16[2,4,512]{2,1,0:T(4,128)(2,1)}, u32[]{:S(2)}) copy-start(bf16[2,4,512]{2,1,0:T(4,128)(2,1)} %param.28) | copy-start | bytes 24580
  7.2 19.5 %copy-start.82 = (f32[2,512]{1,0:T(2,128)S(1)}, f32[2,512]{1,0:T(2,128)}, u32[]{:S(2)}) copy-start(f32[2,512]{1,0:T(2,128)} %param.32) | copy-start | bytes 12292
  7.2 54.7 %all-reduce.17.cloned.1.call-start = ((), (), s32[]{:S(2)}) async-start(), calls=%async_computation.4 | async-start | bytes 196608 | tf_op jit(solution)/shard_map/psum | solution.py:315
  19.3 9.6 copy-start.83
  21.8 41.2 %copy-start.47 = (bf16[2,64,512]{2,1,0:T(8,128)(2,1)S(1)}, bf16[2,64,512]{2,1,0:T(8,128)(2,1)}, u32[]{:S(2)}) copy-start(bf16[2,64,512]{2,1,0:T(8,128)(2,1)} %param.31) | copy-start | bytes 393220
  21.9 4.9 collective-permute-start
  26.7 37.5 %copy-start.73 = (f32[1,1,512]{2,1,0:T(1,128)}, f32[1,1,512]{2,1,0:T(1,128)S(1)}, u32[]{:S(2)}) copy-start(f32[1,1,512]{2,1,0:T(1,128)S(1)} %get-tuple-element.448) | copy-start | bytes 6148
  26.7 152.3 %copy-start.84 = (f32[1,1,512]{2,1,0:T(1,128)}, f32[1,1,512]{2,1,0:T(1,128)S(1)}, u32[]{:S(2)}) copy-start(f32[1,1,512]{2,1,0:T(1,128)S(1)} %get-tuple-element.419) | copy-start | bytes 6148
  26.7 152.3 %copy-start.86 = (f32[1,1,512]{2,1,0:T(1,128)}, f32[1,1,512]{2,1,0:T(1,128)S(1)}, u32[]{:S(2)}) copy-start(f32[1,1,512]{2,1,0:T(1,128)S(1)} %get-tuple-element.420) | copy-start | bytes 6148
  26.7 152.3 %copy-start.88 = (f32[1,1,512]{2,1,0:T(1,128)}, f32[1,1,512]{2,1,0:T(1,128)S(1)}, u32[]{:S(2)}) copy-start(f32[1,1,512]{2,1,0:T(1,128)S(1)} %get-tuple-element.421) | copy-start | bytes 6148
  26.8 35.9 %copy-start.2 = (f32[131,2,512]{2,0,1:T(8,128)}, f32[131,2,512]{2,0,1:T(8,128)S(1)}, u32[]{:S(2)}) copy-start(f32[131,2,512]{2,0,1:T(8,128)S(1)} %maximum_convert_fusion) | copy-start | bytes 1609732
  28.0 105.3 %copy-start.4 = (bf16[128,2,512]{2,0,1:T(8,128)(2,1)}, bf16[128,2,512]{2,0,1:T(8,128)(2,1)S(1)}, u32[]{:S(2)}) copy-start(bf16[128,2,512]{2,0,1:T(8,128)(2,1)S(1)} %get-tuple-element.394) | copy-start | bytes 786436
  28.9 133.9 %reduce-scatter.5.cloned.1.call-start = ((), (), s32[]{:S(2)}) async-start(), calls=%async_computation.5 | async-start | bytes 1310720 | tf_op jit(solution)/shard_map/reduce_scatter | solution.py:330
  29.5 103.8 %copy-start.77 = (f32[1,512]{1,0:T(1,128)}, f32[1,512]{1,0:T(1,128)S(1)}, u32[]{:S(2)}) copy-start(f32[1,512]{1,0:T(1,128)S(1)} %get-tuple-element.432) | copy-start | bytes 6148
  64.2 30.9 %copy-start.9 = (f32[128,2,512]{2,0,1:T(8,128)}, f32[128,2,512]{2,0,1:T(8,128)S(1)}, u32[]{:S(2)}) copy-start(f32[128,2,512]{2,0,1:T(8,128)S(1)} %get-tuple-element.442) | copy-start | bytes 1572868
  64.6 30.9 %copy-start.28 = (f32[128,2,512]{2,0,1:T(8,128)}, f32[128,2,512]{2,0,1:T(8,128)S(1)}, u32[]{:S(2)}) copy-start(f32[128,2,512]{2,0,1:T(8,128)S(1)} %get-tuple-element.393) | copy-start | bytes 1572868
  129.6 14.7 %copy-start.11 = (f32[2,16,512]{2,1,0:T(8,128)}, f32[2,16,512]{2,1,0:T(8,128)S(1)}, u32[]{:S(2)}) copy-start(f32[2,16,512]{2,1,0:T(8,128)S(1)} %get-tuple-element.248.first) | copy-start | bytes 196612
  129.6 14.7 %copy-start.61 = (f32[8,2,512]{2,1,0:T(2,128)}, f32[8,2,512]{2,1,0:T(2,128)S(1)}, u32[]{:S(2)}) copy-start(f32[8,2,512]{2,1,0:T(2,128)S(1)} %get-tuple-element.796) | copy-start | bytes 98308
  129.7 33.1 %copy-start.14 = (bf16[32,2,1024]{2,1,0:T(2,128)(2,1)S(1)}, bf16[32,2,1024]{2,1,0:T(2,128)(2,1)}, u32[]{:S(2)}) copy-start(bf16[32,2,1024]{2,1,0:T(2,128)(2,1)} %param.22) | copy-start | bytes 393220
  134.7 39.4 %copy-start.21 = (bf16[128,2,512]{2,0,1:T(8,128)(2,1)}, bf16[128,2,512]{2,0,1:T(8,128)(2,1)S(1)}, u32[]{:S(2)}) copy-start(bf16[128,2,512]{2,0,1:T(8,128)(2,1)S(1)} %multiply_convert_fusion.4) | copy-start | bytes 786436
  137.5 77.6 %all-reduce.19.cloned.1.call-start = ((), (), s32[]{:S(2)}) async-start(), calls=%async_computation.6 | async-start | bytes 196608 | tf_op jit(solution)/shard_map/psum | solution.py:315
  137.5 41.5 %copy-start.90 = (f32[1,1,512]{2,1,0:T(1,128)S(1)}, f32[1,1,512]{2,1,0:T(1,128)}, u32[]{:S(2)}) copy-start(f32[1,1,512]{2,1,0:T(1,128)} %get-tuple-element.422) | copy-start | bytes 6148
  137.6 41.5 %copy-start.92 = (f32[1,512]{1,0:T(1,128)S(1)}, f32[1,512]{1,0:T(1,128)}, u32[]{:S(2)}) copy-start(f32[1,512]{1,0:T(1,128)} %get-tuple-element.435) | copy-start | bytes 6148
  137.7 26.3 %copy-start.64 = (f32[32,2]{0,1:T(2,128)}, f32[32,2]{0,1:T(2,128)S(1)}, u32[]{:S(2)}) copy-start(f32[32,2]{0,1:T(2,128)S(1)} %compare_select_fusion) | copy-start | bytes 772
  144.3 37.3 %copy-start.29 = (bf16[128,2,1024]{2,0,1:T(8,128)(2,1)}, bf16[128,2,1024]{2,0,1:T(8,128)(2,1)S(1)}, u32[]{:S(2)}) copy-start(bf16[128,2,1024]{2,0,1:T(8,128)(2,1)S(1)} %all_gather.62) | copy-start | bytes 1572868
  162.8 16.2 %copy-start.27 = (bf16[2,512,1024]{2,1,0:T(8,128)(2,1)S(1)}, bf16[2,512,1024]{2,1,0:T(8,128)(2,1)}, u32[]{:S(2)}) copy-start(bf16[2,512,1024]{2,1,0:T(8,128)(2,1)} %param.35) | copy-start | bytes 6291460
  174.1 4.7 collective-permute-start.1
  182.5 205.4 %reduce-scatter.9.cloned.1.call-start = ((), (), s32[]{:S(2)}) async-start(), calls=%async_computation.8 | async-start | bytes 1310720 | tf_op jit(solution)/shard_map/reduce_scatter | solution.py:435
  218.6 30.7 %copy-start.35 = (f32[128,2,512]{2,0,1:T(8,128)}, f32[128,2,512]{2,0,1:T(8,128)S(1)}, u32[]{:S(2)}) copy-start(f32[128,2,512]{2,0,1:T(8,128)S(1)} %get-tuple-element.389) | copy-start | bytes 1572868
  334.8 18.2 %copy-start.72 = (f32[1,512]{1,0:T(1,128)S(1)}, f32[1,512]{1,0:T(1,128)}, u32[]{:S(2)}) copy-start(f32[1,512]{1,0:T(1,128)} %get-tuple-element.431) | copy-start | bytes 6148
  334.8 18.2 %copy-start.85 = (f32[1,1,512]{2,1,0:T(1,128)S(1)}, f32[1,1,512]{2,1,0:T(1,128)}, u32[]{:S(2)}) copy-start(f32[1,1,512]{2,1,0:T(1,128)} %copy-done.84) | copy-start | bytes 6148
  334.8 18.2 %copy-start.87 = (f32[1,1,512]{2,1,0:T(1,128)S(1)}, f32[1,1,512]{2,1,0:T(1,128)}, u32[]{:S(2)}) copy-start(f32[1,1,512]{2,1,0:T(1,128)} %copy-done.86) | copy-start | bytes 6148
  334.8 18.2 %copy-start.89 = (f32[1,1,512]{2,1,0:T(1,128)S(1)}, f32[1,1,512]{2,1,0:T(1,128)}, u32[]{:S(2)}) copy-start(f32[1,1,512]{2,1,0:T(1,128)} %copy-done.88) | copy-start | bytes 6148
  334.8 18.2 %copy-start.91 = (f32[1,1,512]{2,1,0:T(1,128)S(1)}, f32[1,1,512]{2,1,0:T(1,128)}, u32[]{:S(2)}) copy-start(f32[1,1,512]{2,1,0:T(1,128)} %get-tuple-element.422) | copy-start | bytes 6148
  341.6 15.1 %copy-start.17 = (bf16[128,2,512]{2,0,1:T(8,128)(2,1)}, bf16[128,2,512]{2,0,1:T(8,128)(2,1)S(1)}, u32[]{:S(2)}) copy-start(bf16[128,2,512]{2,0,1:T(8,128)(2,1)S(1)} %get-tuple-element.387) | copy-start | bytes 786436
  356.8 31.1 %copy-start.7 = (f32[32,2,1024]{2,0,1:T(8,128)S(1)}, f32[32,2,1024]{2,0,1:T(8,128)}, u32[]{:S(2)}) copy-start(f32[32,2,1024]{2,0,1:T(8,128)} %copy-done.6) | copy-start | bytes 786436
  356.8 32.7 %copy-start.38 = (bf16[32,2,1024]{2,1,0:T(2,128)(2,1)S(1)}, bf16[32,2,1024]{2,1,0:T(2,128)(2,1)}, u32[]{:S(2)}) copy-start(bf16[32,2,1024]{2,1,0:T(2,128)(2,1)} %param.23) | copy-start | bytes 393220
  356.8 32.7 %copy-start.65 = (f32[32,2]{0,1:T(2,128)S(1)}, f32[32,2]{0,1:T(2,128)}, u32[]{:S(2)}) copy-start(f32[32,2]{0,1:T(2,128)} %copy-done.64) | copy-start | bytes 772
  356.8 32.7 %copy-start.68 = (f32[32,2]{0,1:T(2,128)S(1)}, f32[32,2]{0,1:T(2,128)}, u32[]{:S(2)}) copy-start(f32[32,2]{0,1:T(2,128)} %get-tuple-element.439) | copy-start | bytes 772
  356.8 5.9 collective-permute-start.2
  358.6 38.8 %copy-start.5 = (bf16[128,2,512]{2,0,1:T(8,128)(2,1)S(1)}, bf16[128,2,512]{2,0,1:T(8,128)(2,1)}, u32[]{:S(2)}) copy-start(bf16[128,2,512]{2,0,1:T(8,128)(2,1)} %copy-done.4) | copy-start | bytes 786436
  358.6 38.8 %copy-start.32 = (f32[128,2,512]{2,1,0:T(2,128)S(1)}, f32[128,2,512]{2,1,0:T(2,128)}, u32[]{:S(2)}) copy-start(f32[128,2,512]{2,1,0:T(2,128)} %copy-done.31) | copy-start | bytes 1572868
  358.6 38.8 %copy-start.78 = (f32[1,512]{1,0:T(1,128)S(1)}, f32[1,512]{1,0:T(1,128)}, u32[]{:S(2)}) copy-start(f32[1,512]{1,0:T(1,128)} %copy-done.77) | copy-start | bytes 6148
  362.8 26.7 %copy-start.42 = (bf16[128,2,1,512]{3,0,1,2:T(8,128)(2,1)}, bf16[128,2,1,512]{3,0,1,2:T(8,128)(2,1)S(1)}, u32[]{:S(2)}) copy-start(bf16[128,2,1,512]{3,0,1,2:T(8,128)(2,1)S(1)} %fusion.44) | copy-start | bytes 786436
  364.5 189.5 %all-reduce.21.cloned.1.call-start = ((), (), s32[]{:S(2)}) async-start(), calls=%async_computation.10 | async-start | bytes 188416 | tf_op jit(solution)/shard_map/psum | solution.py:532
  389.5 12.6 %copy-start.70 = (f32[32,2]{0,1:T(2,128)}, f32[32,2]{0,1:T(2,128)S(1)}, u32[]{:S(2)}) copy-start(f32[32,2]{0,1:T(2,128)S(1)} %broadcast_multiply_fusion.9) | copy-start | bytes 772
  438.0 39.7 %copy-start.3 = (f32[131,2,512]{2,0,1:T(8,128)S(1)}, f32[131,2,512]{2,0,1:T(8,128)}, u32[]{:S(2)}) copy-start(f32[131,2,512]{2,0,1:T(8,128)} %copy-done.2) | copy-start | bytes 1609732
  480.8 5.6 collective-permute-start.3
  482.7 98.0 %reduce-scatter.11.cloned.1.call-start = ((), (), s32[]{:S(2)}) async-start(), calls=%async_computation.9 | async-start | bytes 1310720 | tf_op jit(solution)/shard_map/reduce_scatter | solution.py:435
  490.0 118.3 %reduce-scatter.7.cloned.1.call-start = ((), (), s32[]{:S(2)}) async-start(), calls=%async_computation.7 | async-start | bytes 1310720 | tf_op jit(solution)/shard_map/reduce_scatter | solution.py:330
  492.8 543.5 %all-reduce.23.cloned.1.call-start = ((), (), s32[]{:S(2)}) async-start(), calls=%async_computation.11 | async-start | bytes 26476544 | tf_op jit(solution)/shard_map/psum | solution.py:532
  505.5 75.2 %copy-start.15 = (bf16[32,2,1024]{2,1,0:T(2,128)(2,1)S(1)}, bf16[32,2,1024]{2,1,0:T(2,128)(2,1)}, u32[]{:S(2)}) copy-start(bf16[32,2,1024]{2,1,0:T(2,128)(2,1)} %param.22) | copy-start | bytes 393220
  505.5 102.8 %copy-start.8 = (f32[32,2,1024]{2,0,1:T(8,128)S(1)}, f32[32,2,1024]{2,0,1:T(8,128)}, u32[]{:S(2)}) copy-start(f32[32,2,1024]{2,0,1:T(8,128)} %copy-done.6) | copy-start | bytes 786436
  505.5 102.8 %copy-start.19 = (f32[32,2,1024]{2,0,1:T(8,128)S(1)}, f32[32,2,1024]{2,0,1:T(8,128)}, u32[]{:S(2)}) copy-start(f32[32,2,1024]{2,0,1:T(8,128)} %reduce-scatter.9.cloned.1.call-done) | copy-start | bytes 786436
  505.5 102.8 %copy-start.39 = (bf16[32,2,1024]{2,1,0:T(2,128)(2,1)S(1)}, bf16[32,2,1024]{2,1,0:T(2,128)(2,1)}, u32[]{:S(2)}) copy-start(bf16[32,2,1024]{2,1,0:T(2,128)(2,1)} %param.23) | copy-start | bytes 393220
  505.5 102.8 %copy-start.66 = (f32[32,2]{0,1:T(2,128)S(1)}, f32[32,2]{0,1:T(2,128)}, u32[]{:S(2)}) copy-start(f32[32,2]{0,1:T(2,128)} %copy-done.64) | copy-start | bytes 772
  505.5 102.8 %copy-start.69 = (f32[32,2]{0,1:T(2,128)S(1)}, f32[32,2]{0,1:T(2,128)}, u32[]{:S(2)}) copy-start(f32[32,2]{0,1:T(2,128)} %get-tuple-element.439) | copy-start | bytes 772
  505.5 102.8 %copy-start.71 = (f32[32,2]{0,1:T(2,128)S(1)}, f32[32,2]{0,1:T(2,128)}, u32[]{:S(2)}) copy-start(f32[32,2]{0,1:T(2,128)} %copy-done.70) | copy-start | bytes 772
  505.5 102.8 %copy-start.80 = (f32[32,2]{0,1:T(2,128)S(1)}, f32[32,2]{0,1:T(2,128)}, u32[]{:S(2)}) copy-start(f32[32,2]{0,1:T(2,128)} %get-tuple-element.437) | copy-start | bytes 772
  505.5 105.8 %copy-start.67 = (f32[1024]{0:T(1024)S(1)}, f32[1024]{0:T(1024)}, u32[]{:S(2)}) copy-start(f32[1024]{0:T(1024)} %get-tuple-element.308) | copy-start | bytes 12292
  1044.7 9.6 copy-start.58
  1044.7 10.4 copy-start.36
  (44 other events, 243.1 us)
Sparse Core Ops, SparseCore 0:
  29.0 32.8 all-reduce.16
  137.6 25.1 reduce-scatter.4
  182.6 32.4 all-reduce.18
  364.7 23.1 reduce-scatter.8
  482.8 71.1 all-reduce.20
  556.4 24.2 reduce-scatter.10
  583.4 24.8 reduce-scatter.6
  615.2 420.9 all-reduce.22
where the time goes:
time: 1070 us
  waiting for transfers between devices  588 us (55%)
  blocking collectives  284 us (27%)
  other arithmetic  47.4 us (4%)
  matrix products  45.8 us (4%)
  Pallas kernels  40 us (4%)
  local copies, waits for them, and re-layouts  34.7 us (3%)
  between operations  15.5 us (1%)
    psum x2, waiting for transfers between devices, body(): lax.psum((grad_in, grad_kernel, grad_cbias, grad_sproj, grad_tproj, grad_...  429 us
    all_gather x6, blocking collectives, entering(): gathered = jax.tree.map(lambda a: lax.all_gather(a, axis), part)  189 us
    psum x2, waiting for transfers between devices, forward_layer(): lax.psum(jnp.einsum('psc,cr->psr', signal_reduced, state_projector, prefe...  61.8 us
    reduce_scatter x2, waiting for transfers between devices, forward_layer(): lax.psum_scatter(jnp.einsum('psc,cd->psd', gated, oproj, preferred_elemen...  45 us
    psum x1, blocking collectives, body(): gain_grad = lax.psum(jnp.stack(gain_parts), ('dp', 'mp'))  44.2 us
    reduce_scatter x2, waiting for transfers between devices, backward_layer(): lax.psum_scatter(jnp.einsum('pskc,kdc->psd', dmixed, in_proj, preferred_e...  42.7 us
    pallas_call x8, Pallas kernels, scan_call(): pl.pallas_call(kernel, out_shape=[jax.ShapeDtypeStruct(o, F32) for o in o...  40 us
    psum x2, blocking collectives, backward_layer(): dproj = lax.psum(jnp.concatenate([drank, db_part, dc_part], axis=-1), 'mp')  22.1 us
  transfers between devices with their start and end apart: 12, of which 11 were waited for; matrix products, arithmetic and copies ran while one was open for 3% of the time, Pallas kernels for 0%

commit v1 on v0

v1 whole, which is shorter than its diff:
```python
import functools
import math

import jax
import jax.numpy as jnp
from jax import lax
from jax.experimental import pallas as pl
from jax.experimental.pallas import tpu as pltpu
from jax.sharding import PartitionSpec as P

EPS = 1e-05
F32 = jnp.float32
BF16 = jnp.bfloat16
LOG2E = math.log2(math.e)
MESH = pl.DeviceIdType.MESH
VMEM = pltpu.VMEM
EDGE = 16

GRP = 16

def spread(dst, part):
    for g in range(dst.shape[0]):
        dst[g] = part[:, g * GRP:(g + 1) * GRP]

def put(w, k, y):
    y = y[:8] + y[8:]
    for j in range(w.shape[0]):
        w[j, k * 8:(k + 1) * 8, :] = y[:, j * 128:(j + 1) * 128]

def take(out, base, w):
    for j in range(w.shape[0]):
        out[pl.ds(base, GRP), j * 128:(j + 1) * 128] = sum(w[j, pl.ds(i, GRP, stride=8), :] for i in range(8))

def totals_scan(dt, du, bg, a2, first):
    def step(g, hs):
        hs = list(hs)
        base = pl.multiple_of(g * GRP, GRP)
        bt = bg[g]
        for k in range(GRP):
            s = k % len(hs)
            d = dt[pl.ds(base + k, 1), :]
            x = du[pl.ds(base + k, 1), :]
            hs[s] = jnp.exp2(d * a2) * hs[s] + x * bt[:, k:k + 1]
        return tuple(hs)
    return lax.fori_loop(0, bg.shape[0], step, first)

def output_scan(dt, du, bg, cg, a2, first, h_all, w, ys):
    def step(g, hs):
        hs = list(hs)
        base = pl.multiple_of(g * GRP, GRP)
        bt = bg[g]
        ct = cg[g]
        for k in range(GRP):
            s = k % len(hs)
            d = dt[pl.ds(base + k, 1), :]
            x = du[pl.ds(base + k, 1), :]
            hs[s] = jnp.exp2(d * a2) * hs[s] + x * bt[:, k:k + 1]
            h_all[base + k] = hs[s].astype(h_all.dtype)
            y = hs[s] * ct[:, k:k + 1]
            put(w, k, y)
        take(ys, base, w)
        return tuple(hs)
    return lax.fori_loop(0, bg.shape[0], step, first)

def adjoint_totals(dt, dy, cg, a2, first):
    def step(i, ks):
        g = cg.shape[0] - 1 - i
        ks = list(ks)
        base = pl.multiple_of(g * GRP, GRP)
        ct = cg[g]
        for k in reversed(range(GRP)):
            s = k % len(ks)
            d = dt[pl.ds(base + k, 1), :]
            y = dy[pl.ds(base + k, 1), :]
            ks[s] = jnp.exp2(d * a2) * (ks[s] + y * ct[:, k:k + 1])
        return tuple(ks)
    return lax.fori_loop(0, cg.shape[0], step, first)

def adjoint_scan(dt, du, dy, bg, cg, a2, an, first, h_all, q_all, w1, w2, s1, s2):
    groups = cg.shape[0]
    seqs = len(first)
    def step(i, carry):
        ks, acc = carry
        g = groups - 1 - i
        ks = list(ks)
        base = pl.multiple_of(g * GRP, GRP)
        bt = bg[g]
        ct = cg[g]
        for k in reversed(range(GRP)):
            s = k % seqs
            r = base + k
            d = dt[pl.ds(r, 1), :]
            y = dy[pl.ds(r, 1), :]
            q = ks[s] + y * ct[:, k:k + 1]
            q_all[r] = q.astype(q_all.dtype)
            kn = jnp.exp2(d * a2) * q
            ks[s] = kn
            fa = kn * h_all[r].astype(jnp.float32)
            acc = acc + fa * d
            put(w1, k, fa * an)
            put(w2, k, q * bt[:, k:k + 1])
        take(s1, base, w1)
        take(s2, base, w2)
        return tuple(ks), acc
    return lax.fori_loop(0, groups, step, (first, jnp.zeros_like(a2)))[1]

def state_sums(all_rows, skip, vec, out):
    states = all_rows.shape[1]
    wide = 128
    for j in range(0, vec.shape[0], wide):
        right = vec[j:j + wide, :].astype(jnp.bfloat16)
        total = jnp.zeros((states, wide), jnp.float32)
        lane = lax.broadcasted_iota(jnp.int32, (states, wide), 1)
        for b in range(0, wide, GRP):
            left = all_rows[skip + j + b:skip + j + b + GRP].astype(jnp.bfloat16).reshape(GRP * states, -1)
            both = lax.dot_general(left, right, (((1,), (1,)), ((), ())), preferred_element_type=jnp.float32)
            for k in range(GRP):
                total = total + jnp.where(lane == b + k, both[k * states:(k + 1) * states], 0.0)
        out[:, j:j + wide] = total


def dot(a, b, ca, cb):
    return lax.dot_general(a, b, (((ca,), (cb,)), ((), ())), preferred_element_type=F32)


def silu_slope(v, s):
    return s * (1.0 + v * (1.0 - s))


def softplus(v):
    return jnp.maximum(v, 0.0) + jnp.log1p(jnp.exp(-jnp.abs(v)))


class Place:
    def __init__(self, blocks, lanes):
        self.blocks, self.lanes = blocks, lanes
        self.dp, self.mp = lax.axis_index("dp"), lax.axis_index("mp")
        self.outer, self.inner = self.dp // 2, self.dp % 2
        self.outers = blocks // 2
        self.core = self.mp + 1 - 2 * (self.mp % 2)
        self.chip = (self.mp + 2) % 4
        self.twin = self.dp + 1 - 2 * self.inner

    def at(self, dp=None, mp=None):
        return {"dp": self.dp if dp is None else dp, "mp": self.mp if mp is None else mp}

    def ahead(self, k):
        return (self.outer + k) % self.outers

    def behind(self, k):
        return (self.outer + self.outers - k) % self.outers


class Net:
    def __init__(self, send, recv):
        self.send, self.recv, self.used = send, recv, 0

    def slots(self, count=1):
        first = self.used
        self.used += count
        assert self.used <= self.send.shape[0], self.used
        return first

    def copy(self, src, dst, device, slot):
        return pltpu.make_async_remote_copy(
            src_ref=src,
            dst_ref=dst,
            send_sem=self.send.at[slot],
            recv_sem=self.recv.at[slot],
            device_id=device,
            device_id_type=MESH,
        )


def start(copy):
    copy.start()
    return copy


def others(count, body):
    if count <= 4:
        for k in range(1, count):
            body(k)
    else:
        lax.fori_loop(1, count, lambda k, c: (body(k), c)[1], 0)


def entry_barrier(me):
    sem = pltpu.get_barrier_semaphore()

    def greet(dp, mp):
        pl.semaphore_signal(sem, inc=1, device_id=me.at(dp, mp), device_id_type=MESH)

    greet(None, me.core)
    greet(None, me.chip)
    others(me.blocks, lambda k: greet((me.dp + k) % me.blocks, None))
    top = me.lanes - 1

    @pl.when((me.mp == top) & (me.dp < me.blocks - 1))
    def _():
        for t in range(top):
            greet(me.dp + 1, t)

    @pl.when((me.mp < top) & (me.dp > 0))
    def _():
        greet(me.dp - 1, top)

    greeted = jnp.where(me.mp == top, jnp.where(me.dp < me.blocks - 1, top, 0), jnp.where(me.dp > 0, 1, 0))
    pl.semaphore_wait(sem, 2 + me.blocks - 1 + greeted)


def gather_rows(net, me, full, base, rows):
    slot = net.slots(3)

    def block(mp):
        return full.at[pl.ds(pl.multiple_of(base + mp * rows, 16), rows)]

    mine = block(me.mp)
    far = start(net.copy(mine, mine, me.at(mp=me.chip), slot))
    near = start(net.copy(mine, mine, me.at(mp=me.core), slot + 1))
    far.wait_recv()
    theirs = block(me.chip)
    passed = start(net.copy(theirs, theirs, me.at(mp=me.core), slot + 2))

    def finish():
        near.wait()
        passed.wait()
        far.wait_send()

    return finish


def sum_lanes(net, me, own, got1, got2):
    slot = net.slots(2)
    near = start(net.copy(own, got1, me.at(mp=me.core), slot))

    def second():
        near.wait()
        own[...] = own[...] + got1[...]
        far = start(net.copy(own, got2, me.at(mp=me.chip), slot + 1))

        def finish():
            far.wait()
            return own[...] + got2[...]

        return finish

    return second


def scatter_sum(net, me, part, rows, send1, got1, send2, got2):
    slot = net.slots(3)

    def block(mp):
        return part[pl.ds(pl.multiple_of(mp * rows, 16), rows), :]

    far_core = (me.core + 2) % 4
    copies = []
    for i, mp in enumerate((far_core, me.core)):
        send1[i] = block(mp).astype(send1.dtype)
        copies.append(start(net.copy(send1.at[i], got1.at[i], me.at(mp=me.core), slot + i)))

    def second():
        copies[0].wait_recv()
        send2[...] = (block(me.chip) + got1[0].astype(F32)).astype(send2.dtype)
        far = start(net.copy(send2, got2, me.at(mp=me.chip), slot + 2))

        def finish():
            copies[1].wait_recv()
            total = block(me.mp) + got1[1].astype(F32)
            far.wait()
            copies[0].wait_send()
            copies[1].wait_send()
            return total + got2[...].astype(F32)

        return finish

    return second


def share_sums(net, me, sums):
    slot = net.slots(me.blocks)

    def copy(k):
        mine = sums.at[me.dp]
        return net.copy(mine, mine, me.at(dp=(me.dp + k) % me.blocks), slot + k)

    others(me.blocks, lambda k: copy(k).start())

    def finish():
        others(me.blocks, lambda k: copy(k).wait())

    return finish


def entering_state(net, me, own, sums, a2, send1, got1, send2, got2, forward):
    seqs = len(own)
    slot = net.slots(1 + me.outers)
    early = 0 if forward else 1
    am_early = me.inner == early

    def decay(dp, s):
        tile = sums[dp]
        width = a2.shape[1] // 128
        row = jnp.concatenate([tile[s * width + j : s * width + j + 1, :] for j in range(width)], axis=1)
        return row

    for s in range(seqs):
        send1[s] = own[s].astype(send1.dtype)
    pair = start(net.copy(send1, got1, me.at(dp=me.twin), slot))

    def to(k):
        return me.outer + k if forward else me.outer - k

    def copy(k):
        dp = to(k) * 2 + me.inner
        return net.copy(send2, got2.at[me.outer], me.at(dp=dp), slot + k)

    def reaches(k):
        return (to(k) < me.outers) if forward else (to(k) >= 0)

    def second():
        pair.wait()
        late_block = me.outer * 2 + 1 - early
        for s in range(seqs):
            theirs = got1[s].astype(F32)
            mine = own[s]
            first = jnp.where(am_early, mine, theirs)
            last = jnp.where(am_early, theirs, mine)
            send2[s] = (last + jnp.exp2(a2 * decay(late_block, s)) * first).astype(send2.dtype)

        def send(k):
            @pl.when(reaches(k))
            def _():
                copy(k).start()

        others(me.outers, send)

        def finish():
            count = me.outer if forward else me.outers - 1 - me.outer

            def add(i, state):
                source = i if forward else me.outers - 1 - i
                away = me.outer - source if forward else source - me.outer
                net.copy(send2, got2.at[source], me.at(dp=me.twin), slot + away).wait_recv()
                both = [decay(2 * source, s) + decay(2 * source + 1, s) for s in range(seqs)]
                return tuple(got2[source, s].astype(F32) + jnp.exp2(a2 * both[s]) * state[s] for s in range(seqs))

            state = lax.fori_loop(0, count, add, tuple(jnp.zeros_like(own[s]) for s in range(seqs)))
            result = []
            for s in range(seqs):
                after = got1[s].astype(F32) + jnp.exp2(a2 * decay(me.twin, s)) * state[s]
                result.append(jnp.where(am_early, state[s], after))

            def sent(k):
                @pl.when(reaches(k))
                def _():
                    copy(k).wait_send()

            others(me.outers, sent)
            return tuple(result)

        return finish

    return second


def reduce_chunk(net, me, local, out, row, n, fill, bufs):
    half = n // 2
    piece = half // me.outers
    gs, gm, zs, sh, xr, zr = bufs
    slot = net.slots(3 + 3 * me.outers)
    s_z, s_a, s_f = slot + 2, slot + 2 + me.outers, slot + 2 + 2 * me.outers
    fill(1 - me.inner, gs)
    pair = start(net.copy(gs, xr, me.at(dp=me.twin), slot))
    fill(me.inner, gm)
    yield

    pair.wait()
    gm[...] = gm[...] + xr[...].astype(F32)
    zs[...] = gm[...].astype(zs.dtype)

    def rows_of(o):
        return pl.ds(pl.multiple_of(o * piece, 16), piece)

    def give(k):
        o = me.ahead(k)
        return net.copy(zs.at[rows_of(o)], zr.at[k], me.at(dp=o * 2 + me.inner), s_z + k)

    others(me.outers, lambda k: give(k).start())
    yield

    total = gm[rows_of(me.outer), :]
    if me.outers <= 4:
        for k in range(1, me.outers):
            give(k).wait()
            total = total + zr[k].astype(F32)
    else:
        def more(k, acc):
            give(k).wait()
            return acc + zr[k].astype(F32)
        total = lax.fori_loop(1, me.outers, more, total)
    sh[...] = total.astype(sh.dtype)

    def place(o, inner):
        return out.at[pl.ds(pl.multiple_of(row + inner * half + o * piece, 16), piece)]

    keep = pltpu.make_async_copy(sh, place(me.outer, me.inner), local)
    keep.start()
    across = start(net.copy(sh, place(me.outer, me.inner), me.at(dp=me.twin), slot + 1))

    def spread_to(k):
        return net.copy(sh, place(me.outer, me.inner), me.at(dp=me.ahead(k) * 2 + me.inner), s_a + k)

    others(me.outers, lambda k: spread_to(k).start())
    yield

    def hand_on(k):
        there = place(me.behind(k), me.inner)
        return net.copy(there, there, me.at(dp=me.twin), s_f + k)

    def forward(k):
        spread_to(k).wait_recv()
        hand_on(k).start()

    others(me.outers, forward)
    yield

    across.wait()
    keep.wait()

    def close(k):
        spread_to(k).wait_send()
        hand_on(k).wait()

    others(me.outers, close)


def rms(x):
    return lax.rsqrt(jnp.mean(x * x, axis=-1, keepdims=True) + EPS)


def forward_layer(net, me, l, s):
    own_rows = s.x.shape[1]
    rows = s.dt.shape[1]
    seqs = s.seqs
    chans = s.dt.shape[2]
    states = s.dlog.shape[1]
    rank = s.stp.shape[1]
    taps = s.ck.shape[1]

    x = s.x[l]
    hn = (x * rms(x) * s.gain[l : l + 1, :]).astype(BF16)
    at = pl.multiple_of(EDGE + me.mp * own_rows, 16)
    s.hn[l, pl.ds(at, own_rows), :] = hn
    edge_slot = net.slots(me.lanes)
    last = me.mp == me.lanes - 1

    def edge(t):
        src = s.hn.at[l, pl.ds(rows, EDGE)]
        return net.copy(src, s.hn.at[l, pl.ds(0, EDGE)], me.at(dp=me.dp + 1, mp=t), edge_slot + t)

    @pl.when(last & (me.dp < me.blocks - 1))
    def _():
        for t in range(me.lanes):
            edge(t).start()

    @pl.when(me.dp == 0)
    def _():
        s.hn[l, 0:EDGE, :] = jnp.zeros((EDGE, s.hn.shape[2]), BF16)

    gather_rows(net, me, s.hn.at[l], EDGE, own_rows)()

    @pl.when(me.dp > 0)
    def _():
        pltpu.make_async_remote_copy(
            src_ref=s.hn.at[l, pl.ds(rows, EDGE)], dst_ref=s.hn.at[l, pl.ds(0, EDGE)],
            send_sem=net.send.at[edge_slot], recv_sem=net.recv.at[edge_slot + me.mp],
            device_id=me.at(dp=me.twin), device_id_type=MESH,
        ).wait_recv()

    s.xi[l] = dot(s.hn[l], s.win[l, 0], 1, 0).astype(BF16).astype(F32)
    conv = s.cb[l : l + 1, :]
    for k in range(taps):
        off = EDGE - seqs * (taps - 1 - k)
        conv = conv + s.xi[l, off : off + rows, :] * s.ck[l, k : k + 1, :].astype(F32)
    s.xc[l] = conv
    u = (conv * jax.nn.sigmoid(conv)).astype(BF16)
    s.u[l] = u

    p = 2 * l
    s.xd[p] = dot(s.stt[l], u, 1, 1)
    second = sum_lanes(net, me, s.xd.at[p], s.xd1.at[p], s.xd2.at[p])
    s.z[l] = dot(s.hn[l, EDGE : EDGE + rows, :], s.win[l, 1], 1, 0)
    xd = second()()
    s.dtr[l] = xd[:rank].astype(BF16)
    spread(s.bg.at[l], xd[rank : rank + states])
    spread(s.cg.at[l], xd[rank + states :])
    pre = dot(s.dtr[l], s.stp[l], 0, 0) + s.sb[l : l + 1, :]
    s.pre[l] = pre
    dt = softplus(pre)
    s.dt[l] = dt
    s.du[...] = dt * s.u[l].astype(F32)

    odd = lax.broadcasted_iota(jnp.int32, (rows, 1), 0) % seqs
    for q in range(seqs):
        total = jnp.sum(jnp.where(odd == q, dt, 0.0), axis=0, keepdims=True)
        for j in range(chans // 128):
            i = q * (chans // 128) + j
            s.sums[l, me.dp, i : i + 1, :] = total[:, j * 128 : (j + 1) * 128]
    shared = share_sums(net, me, s.sums.at[l])
    a2 = -jnp.exp(s.dlog[l]) * LOG2E
    zero = jnp.zeros_like(a2)
    own = totals_scan(s.dt.at[l], s.du, s.bg.at[l], a2, (zero,) * seqs)
    shared()
    first = entering_state(
        net, me, own, s.sums.at[l], a2, s.st1.at[p], s.got1.at[p], s.st2.at[p], s.got2.at[p], True
    )()()
    for q in range(seqs):
        s.h[l, q] = first[q].astype(s.h.dtype)
    output_scan(
        s.dt.at[l], s.du, s.bg.at[l], s.cg.at[l], a2, first, s.h.at[l, pl.ds(seqs, rows)], s.w1, s.ys.at[l]
    )

    ys = s.ys[l] + s.skip[l : l + 1, :] * s.u[l].astype(F32)
    s.ys[l] = ys
    z = s.z[l]
    s.go[l] = (ys * z * jax.nn.sigmoid(z)).astype(BF16)
    s.part[...] = dot(s.go[l], s.wout[l], 1, 0)
    total = scatter_sum(net, me, s.part, own_rows, s.rs1, s.rs2.at[p], s.rs3, s.rs4.at[p])()()
    s.x[l + 1] = s.x[l] + total

    @pl.when(last & (me.dp < me.blocks - 1))
    def _():
        for t in range(me.lanes):
            edge(t).wait_send()


def gradient_chunks(net, me, l, s):
    rows = s.dt.shape[1]
    chans = s.dt.shape[2]
    width = s.x.shape[2]
    big = max(512, EDGE * me.blocks)
    made = []

    def bufs(first, n):
        half, piece = n // 2, n // 2 // me.outers
        r = pl.ds(first // 2, half)
        return (
            s.gs.at[r], s.gm.at[r], s.zs.at[r], s.sh.at[pl.ds(first // 2 // me.outers, piece)],
            s.xr.at[l, r], s.zr.at[l, pl.ds(0, me.outers), pl.ds(first // 2 // me.outers, piece)],
        )

    def add(first, n, fill):
        made.append(reduce_chunk(net, me, s.local.at[l, len(made)], s.gout.at[l], first, n, fill, bufs(first, n)))

    def out_rows(first, n):
        def fill(h, ref):
            begin = first + h * (n // 2)
            d0 = pl.multiple_of(begin // chans * chans, chans)
            c0 = pl.multiple_of(begin % chans, min(n // 2, chans))
            left = s.go[l, :, pl.ds(c0, n // 2)]
            right = s.do[l, :, pl.ds(d0, chans)]
            ref[...] = dot(left, right, 0, 0).astype(ref.dtype)
        return fill

    def in_rows(first, n, ref2):
        def fill(h, ref):
            d0 = pl.multiple_of(first + h * (n // 2), n // 2)
            left = s.hn[l, EDGE : EDGE + rows, pl.ds(d0, n // 2)]
            ref[...] = dot(left, ref2[...], 0, 0).astype(ref.dtype)
        return fill

    def small_rows(n):
        def fill(h, ref):
            ref[...] = s.small[pl.ds(pl.multiple_of(h * (n // 2), 16), n // 2), :].astype(ref.dtype)
        return fill

    groups = []
    for which in range(3):
        names = []
        for first in range(0, width, big):
            base = which * width + first
            names.append(len(made))
            if which == 0:
                add(base, big, out_rows(first, big))
            else:
                add(base, big, in_rows(first, big, s.dxi if which == 1 else s.dz.at[l]))
        groups.append([made[i] for i in names])
    n = s.small.shape[0]
    add(3 * width, n, small_rows(n))
    out, conv, gate = groups
    return out, gate, conv, [made[-1]]


def advance(chunks):
    for c in chunks:
        next(c, None)


def backward_layer(net, me, l, s, before):
    own_rows = s.x.shape[1]
    rows = s.dt.shape[1]
    seqs = s.seqs
    chans = s.dt.shape[2]
    states = s.dlog.shape[1]
    rank = s.stp.shape[1]
    taps = s.ck.shape[1]
    p = 2 * l + 1
    out, gate, conv, small = gradient_chunks(net, me, l, s)

    at = pl.multiple_of(me.mp * own_rows, 16)
    s.do[l, pl.ds(at, own_rows), :] = s.g[...].astype(BF16)
    gathered = gather_rows(net, me, s.do.at[l], 0, own_rows)
    advance(before)
    gathered()
    dgo = dot(s.do[l], s.wout[l], 1, 1)
    z = s.z[l]
    sg = jax.nn.sigmoid(z)
    s.dy[...] = dgo * z * sg
    s.dz[l] = (dgo * s.ys[l] * silu_slope(z, sg)).astype(BF16)

    s.du[...] = s.dt[l] * s.u[l].astype(F32)
    an = -jnp.exp(s.dlog[l])
    a2 = an * LOG2E
    zero = jnp.zeros_like(a2)
    own = adjoint_totals(s.dt.at[l], s.dy, s.cg.at[l], a2, (zero,) * seqs)
    second = entering_state(
        net, me, own, s.sums.at[l], a2, s.st1.at[p], s.got1.at[p], s.st2.at[p], s.got2.at[p], False
    )
    advance(out)
    finish = second()
    advance(gate)
    advance(before)
    last = finish()
    acc = adjoint_scan(
        s.dt.at[l], s.du, s.dy, s.bg.at[l], s.cg.at[l], a2, an, last, s.h.at[l], s.q, s.w1, s.w2, s.s1, s.s2
    )
    advance(out + gate + before)
    x0 = s.xd.shape[1] - 2 * states
    state_sums(s.q, 0, s.du, s.xd.at[p, pl.ds(x0, states)])
    state_sums(s.h.at[l], seqs, s.dy, s.xd.at[p, pl.ds(x0 + states, states)])

    u = s.u[l].astype(F32)
    dpre = ((s.s1[...] + s.s2[...] * u) * jax.nn.sigmoid(s.pre[l])).astype(BF16)
    s.s2[...] = s.s2[...] * s.dt[l] + s.skip[l : l + 1, :] * s.dy[...]
    s.xd[p, 0:rank, :] = dot(s.stp[l], dpre, 1, 1)
    second = sum_lanes(net, me, s.xd.at[p], s.xd1.at[p], s.xd2.at[p])
    xw = s.xd.shape[1]
    s.small[xw : xw + rank, :] = dot(s.dtr[l], dpre, 1, 0)
    s.small[xw + rank : xw + rank + states, :] = an * acc
    v0 = xw + rank + states
    s.small[v0 + taps + 2 : v0 + taps + 3, :] = jnp.sum(dpre.astype(F32), axis=0, keepdims=True)
    s.small[v0 + taps + 1 : v0 + taps + 2, :] = jnp.sum(s.dy[...] * u, axis=0, keepdims=True)
    finish = second()
    advance(out + gate + before)
    dxr = finish().astype(BF16)
    xc = s.xc[l]
    du = s.s2[...] + dot(dxr, s.stt[l], 0, 0)
    dxc = du * silu_slope(xc, jax.nn.sigmoid(xc))
    s.dxc[l, 0:rows, :] = dxc

    slot = net.slots()
    edge = net.copy(s.dxc.at[l, pl.ds(0, 8)], s.dxc.at[l, pl.ds(rows, 8)], me.at(dp=me.dp - 1), slot)

    @pl.when(me.dp > 0)
    def _():
        edge.start()

    @pl.when(me.dp == me.blocks - 1)
    def _():
        s.dxc[l, rows : rows + 8, :] = jnp.zeros((8, chans), F32)

    s.small[0:xw, :] = dot(dxr, s.u[l], 1, 0)
    s.small[v0 + taps : v0 + taps + 1, :] = jnp.sum(dxc, axis=0, keepdims=True)
    for k in range(taps):
        off = EDGE - seqs * (taps - 1 - k)
        s.small[v0 + k : v0 + k + 1, :] = jnp.sum(dxc * s.xi[l, off : off + rows, :], axis=0, keepdims=True)
    s.part[...] = dot(s.dz[l], s.win[l, 1], 1, 1)

    @pl.when(me.dp < me.blocks - 1)
    def _():
        net.copy(s.dxc.at[l, pl.ds(0, 8)], s.dxc.at[l, pl.ds(rows, 8)], me.at(dp=me.twin), slot).wait_recv()

    dxi = jnp.zeros((rows, chans), F32)
    for k in range(taps):
        off = seqs * (taps - 1 - k)
        dxi = dxi + s.ck[l, k : k + 1, :].astype(F32) * s.dxc[l, off : off + rows, :]
    s.dxi[...] = dxi.astype(BF16)

    s.part[...] = s.part[...] + dot(s.dxi[...], s.win[l, 0], 1, 1)
    second = scatter_sum(net, me, s.part, own_rows, s.rs1, s.rs2.at[p], s.rs3, s.rs4.at[p])
    advance(conv)
    finish = second()
    advance(out + gate + before)
    dhn = finish()
    x = s.x[l]
    inv = rms(x)
    part = jnp.sum(dhn * x * inv, axis=0, keepdims=True)
    g0 = v0 + 8
    s.gg[l] = jnp.zeros_like(s.gg[l])
    for j in range(x.shape[1] // chans):
        s.gg[l, j : j + 1, :] = part[:, j * chans : (j + 1) * chans]
    dr = dhn * s.gain[l : l + 1, :]
    s.g[...] = s.g[...] + inv * dr - x * (inv * inv * inv) * jnp.mean(dr * x, axis=-1, keepdims=True)

    @pl.when(me.dp > 0)
    def _():
        edge.wait_send()

    s.small[g0 : g0 + 8, :] = sum_lanes(net, me, s.gg.at[l], s.gg1.at[l], s.gg2.at[l])()()
    if s.small.shape[0] > g0 + 8:
        s.small[g0 + 8 :, :] = jnp.zeros((s.small.shape[0] - g0 - 8, chans), F32)
    s.small[v0 + taps + 3 : g0, :] = jnp.zeros((g0 - v0 - taps - 3, chans), F32)
    advance(small)
    return out + gate + conv + small


class Refs:
    pass


def kernel(names, seqs, blocks, lanes, *refs):
    s = Refs()
    for name, ref in zip(names, refs, strict=True):
        setattr(s, name, ref)
    s.seqs = seqs
    me = Place(blocks, lanes)
    net = Net(s.send, s.recv)
    entry_barrier(me)
    layers = s.gain.shape[0]
    s.x[0] = s.tok[...].astype(F32)
    for l in range(layers):
        forward_layer(net, me, l, s)
    s.lout[...] = s.x[layers].astype(s.lout.dtype)
    s.g[...] = s.g0[...]
    before = []
    for l in reversed(range(layers)):
        done = backward_layer(net, me, l, s, before)
        if before:
            for c in before:
                for _ in c:
                    pass
        before = done
    s.tgrad[...] = s.g[...]
    for _ in range(6):
        advance(before)


def layers_call(mesh, tokens, grad, gain, win, ck, cb, stt, stp, sb, dlog, skip, wout):
    blocks, lanes = mesh.shape["dp"], mesh.shape["mp"]
    seg, seqs, width = tokens.shape
    own_rows = seg * seqs
    rows = own_rows * lanes
    layers, chans = skip.shape
    states, rank, xw, taps = dlog.shape[1], stp.shape[1], stt.shape[1], ck.shape[1]
    outers = blocks // 2
    small = -(-(xw + rank + states + 16) // (EDGE * blocks)) * EDGE * blocks
    grads = 3 * width + small
    groups = rows // GRP
    slots = layers * (3 * 2 + 2 * 3 + 3 * 2 + lanes + blocks + 2 * (1 + outers) + 1)
    chunks = 3 * (width // max(512, EDGE * blocks)) + 1
    slots += layers * chunks * (3 + 3 * outers)
    two = 2 * layers
    ins = ["tok", "g0", "gain", "win", "ck", "cb", "stt", "stp", "sb", "dlog", "skip", "wout"]
    outs = {
        "lout": ((own_rows, width), BF16),
        "tgrad": ((own_rows, width), F32),
        "gout": ((layers, grads, chans), BF16),
    }
    half = grads // 2
    piece = half // outers
    scratch = {
        "x": ((layers + 1, own_rows, width), F32),
        "g": ((own_rows, width), F32),
        "hn": ((layers, EDGE + rows, width), BF16),
        "xi": ((layers, EDGE + rows, chans), F32),
        "xc": ((layers, rows, chans), F32),
        "u": ((layers, rows, chans), BF16),
        "z": ((layers, rows, chans), F32),
        "pre": ((layers, rows, chans), F32),
        "dt": ((layers, rows, chans), F32),
        "du": ((rows, chans), F32),
        "ys": ((layers, rows, chans), F32),
        "go": ((layers, rows, chans), BF16),
        "dtr": ((layers, rank, rows), BF16),
        "bg": ((layers, groups, states, GRP), F32),
        "cg": ((layers, groups, states, GRP), F32),
        "h": ((layers, rows + seqs, states, chans), BF16),
        "q": ((rows, states, chans), BF16),
        "w1": ((chans // 128, GRP * 8, 128), F32),
        "w2": ((chans // 128, GRP * 8, 128), F32),
        "do": ((layers, rows, width), BF16),
        "dy": ((rows, chans), F32),
        "dz": ((layers, rows, chans), BF16),
        "s1": ((rows, chans), F32),
        "s2": ((rows, chans), F32),
        "dxc": ((layers, rows + 8, chans), F32),
        "dxi": ((rows, chans), BF16),
        "part": ((rows, width), F32),
        "rs1": ((2, own_rows, width), BF16),
        "rs2": ((two, 2, own_rows, width), BF16),
        "rs3": ((own_rows, width), BF16),
        "rs4": ((two, own_rows, width), BF16),
        "xd": ((two, xw, rows), F32),
        "xd1": ((two, xw, rows), F32),
        "xd2": ((two, xw, rows), F32),
        "sums": ((layers, blocks, seqs * chans // 128, 128), F32),
        "st1": ((two, seqs, states, chans), BF16),
        "got1": ((two, seqs, states, chans), BF16),
        "st2": ((two, seqs, states, chans), BF16),
        "got2": ((two, outers, seqs, states, chans), BF16),
        "small": ((small, chans), F32),
        "gg": ((layers, 8, chans), F32),
        "gg1": ((layers, 8, chans), F32),
        "gg2": ((layers, 8, chans), F32),
        "gs": ((half, chans), BF16),
        "gm": ((half, chans), F32),
        "zs": ((half, chans), BF16),
        "sh": ((piece, chans), BF16),
        "xr": ((layers, half, chans), BF16),
        "zr": ((layers, outers, piece, chans), BF16),
    }
    names = ins + list(outs) + list(scratch) + ["local", "send", "recv"]
    any_space = pl.BlockSpec(memory_space=pl.ANY)
    vmem = pl.BlockSpec(memory_space=VMEM)
    sems = [pltpu.SemaphoreType.DMA((layers, chunks)), pltpu.SemaphoreType.DMA((slots,)), pltpu.SemaphoreType.DMA((slots,))]
    return pl.pallas_call(
        functools.partial(kernel, names, seqs, blocks, lanes),
        out_shape=[jax.ShapeDtypeStruct(a, t) for a, t in outs.values()],
        in_specs=[vmem] * len(ins),
        out_specs=[vmem, vmem, any_space],
        scratch_shapes=[VMEM(a, t) for a, t in scratch.values()] + sems,
        compiler_params=pltpu.CompilerParams(
            collective_id=0, has_side_effects=True, vmem_limit_bytes=63 * 2**20
        ),
    )(tokens.reshape(own_rows, width), grad, gain, win, ck, cb, stt, stp, sb, dlog, skip, wout)


def body(
    mesh,
    tokens,
    cotangent,
    char_start,
    lengths,
    norm_gain,
    input_proj,
    conv_kernel,
    conv_bias,
    state_proj,
    step_proj,
    step_bias,
    decay_log,
    skip_gain,
    output_proj,
):
    seg, seqs, width = tokens.shape
    position = lax.axis_index(("dp", "mp")) * seg + lax.broadcasted_iota(jnp.int32, (seg, seqs), 0)
    weight = jnp.where(position < lengths[None, :], 0.5 + char_start.astype(F32), 0.0)
    grad = (cotangent.astype(F32) * weight[:, :, None]).reshape(seg * seqs, width)
    lout, tgrad, gout = layers_call(
        mesh, tokens, grad, norm_gain, input_proj, conv_kernel, conv_bias,
        state_proj.transpose(0, 2, 1), step_proj, step_bias, decay_log, skip_gain, output_proj,
    )
    layers, chans = skip_gain.shape
    xw, rank, states, taps = state_proj.shape[2], step_proj.shape[1], decay_log.shape[1], conv_kernel.shape[1]
    gout = gout.astype(F32)
    out = gout[:, :width].reshape(layers, width // chans, chans, chans).transpose(0, 2, 1, 3).reshape(layers, chans, width)
    inp = gout[:, width : 3 * width].reshape(layers, 2, width, chans)
    rest = gout[:, 3 * width :]
    v0 = xw + rank + states
    return (
        lout.reshape(tokens.shape),
        tgrad.reshape(tokens.shape),
        rest[:, v0 + 8 : v0 + 8 + width // chans].reshape(layers, width),
        inp,
        rest[:, v0 : v0 + taps],
        rest[:, v0 + taps],
        rest[:, :xw].transpose(0, 2, 1),
        rest[:, xw : xw + rank],
        rest[:, v0 + taps + 2],
        rest[:, xw + rank : v0],
        rest[:, v0 + taps + 1],
        out,
    )


def solution(mesh):
    return jax.shard_map(
        functools.partial(body, mesh),
        mesh=mesh,
        in_specs=(
            P(("dp", "mp"), None, None),
            P(("dp", "mp"), None, None),
            P(("dp", "mp"), None),
            P(),
            P(),
            P(None, None, None, "mp"),
            P(None, None, "mp"),
            P(None, "mp"),
            P(None, "mp", None),
            P(None, None, "mp"),
            P(None, "mp"),
            P(None, None, "mp"),
            P(None, "mp"),
            P(None, "mp", None),
        ),
        out_specs=(
            P(("dp", "mp"), None, None),
            P(("dp", "mp"), None, None),
            P(),
            P(None, None, None, "mp"),
            P(None, None, "mp"),
            P(None, "mp"),
            P(None, "mp", None),
            P(None, None, "mp"),
            P(None, "mp"),
            P(None, None, "mp"),
            P(None, "mp"),
            P(None, "mp", None),
        ),
        check_vma=False,
    )
```

time: 1070 us -> 332 us (0.31)
  waiting for transfers between devices: 588 us -> 0 us
  blocking collectives: 284 us -> 0 us
  Pallas kernels: 40 us -> 300 us
  matrix products: 45.8 us -> 0 us
  other arithmetic: 47.4 us -> 11.7 us
  local copies, waits for them, and re-layouts: 34.7 us -> 19.1 us
  between operations: 15.5 us -> 0.7 us
    psum x4 -> x0, waiting for transfers between devices: 491 us -> none  [the longest x2 429 us: body(): lax.psum((grad_in, grad_kernel, grad_cbias, grad_sproj, grad_tproj, grad_...]
    pallas_call x8 -> x1, Pallas kernels: 40 us -> 300 us  [layers_call(): pl.pallas_call(functools.partial(kernel, names, seqs, blocks, lanes), out...]
    all_gather x10 -> x0, blocking collectives: 218 us -> none  [the longest x6 189 us: entering(): gathered = jax.tree.map(lambda a: lax.all_gather(a, axis), part)]
    reduce_scatter x4 -> x0, waiting for transfers between devices: 87.7 us -> none  [the longest x2 45 us: forward_layer(): lax.psum_scatter(jnp.einsum('psc,cd->psd', gated, oproj, preferred_elemen...]
    psum x3 -> x0, blocking collectives: 66.3 us -> none  [the longest x1 44.2 us: body(): gain_grad = lax.psum(jnp.stack(gain_parts), ('dp', 'mp'))]
    dot_general x24 -> x0, matrix products: 45.8 us -> none  [the longest x2 6.45 us: backward_layer(): jnp.einsum('psr,cr->psc', dproj_low, state_projector, preferred_element_t...]
    another operation x14 -> x0, other arithmetic: 21.9 us -> none  [the longest x11 21.8 us: body(): jnp.stack([entry[slot] for entry in ordered])]
    unnamed x195 -> x10, local copies, waits for them, and re-layouts: 14.9 us -> 2.57 us
  transfers between devices with their start and end apart: 12 -> 0, of which waited for: 11 -> 0; matrix products, arithmetic and copies ran while one was open for 3% -> 0% of each run, Pallas kernels for 0% -> 0%
where the time goes in v1:
time: 332 us
  Pallas kernels  300 us (90%)
  local copies, waits for them, and re-layouts  19.1 us (6%)
  other arithmetic  11.7 us (4%)
    pallas_call x1, Pallas kernels, layers_call(): pl.pallas_call(functools.partial(kernel, names, seqs, blocks, lanes), out...  300 us
    convert_element_type x1, other arithmetic, body(): gout = gout.astype(F32)  9.92 us

profile of v1, /device:TPU:0, one launch (start us, length us, event | category | flops | bytes accessed | tf_op | source)
XLA Modules:
  0.0 331.9 jit_solution(10328026364506971812)
XLA Ops:
  0.7 0.8 compare_select_fusion
  1.4 0.1 copy.26
  1.5 1.0 convert_multiply_fusion
  2.5 0.9 reshape.51.refs_1_
  3.4 1.6 reshape.50.refs_0_
  5.0 300.4 %shard_map.229 = (bf16[64,1024]{1,0:T(8,128)(2,1)}, f32[64,1024]{1,0:T(8,128)}, bf16[2,3328,512]{2,1,0:T(8,128)(2,1)}) custom-call(bf16[64,1024]{1,0:T(8,128)(2,1)} %reshape.50.refs_0_, f32[64,1024]{1,0:T(8,128)} %reshape.51.refs_1_, f32[2,1024]{1,0:T(2,128)} %refs_2_.1, bf16[2,2,1024,512]{3,2,1,0:T(8,128)(2,1)} %refs_3_.1, bf16[2,4,512]{2,1,0:T(4,128)(2,1)} %refs_4_.1, ...), custom_call_target="tpu_custom_call" | custom-call | tf_op jit(solution)/shard_map/pallas_call | solution.py:828
  305.4 0.8 fusion
  306.3 0.6 copy_bitcast_fusion
  306.9 0.6 copy.36
  307.5 0.0 copy-start
  307.5 9.9 %convert_element_type.11 = f32[2,3328,512]{2,1,0:T(8,128)} convert(bf16[2,3328,512]{2,1,0:T(8,128)(2,1)} %get-tuple-element.17) | non-fusion elementwise | flops 3407872 | bytes 20447232 | tf_op jit(solution)/shard_map/convert_element_type | solution.py:867
  317.4 1.8 slice_bitcast_fusion
  319.2 0.8 slice_bitcast_fusion.1
  319.9 0.6 copy.32
  320.5 0.0 copy-done
  320.5 4.6 %slice.50 = f32[2,2048,512]{2,1,0:T(8,128)} slice(bf16[2,3328,512]{2,1,0:T(8,128)(2,1)S(1)} %copy-done), slice={[0:2], [1024:3072], [0:512]} | slice | bytes 16777216 | tf_op jit(solution)/shard_map/slice | solution.py:869
  325.1 0.0 copy-start.1
  325.1 0.6 slice.58
  325.7 0.0 copy-start.2
  325.7 2.7 copy.31
  328.4 0.7 slice.54
  329.1 0.6 slice.56
  329.8 0.6 slice.51
  330.4 0.0 copy-done.1
  330.4 0.8 reshape.53
  331.2 0.0 copy-done.2
  331.2 0.7 reshape.52
  (1 shorter events, 0.0 us)
Async XLA Ops:
  307.5 13.1 %copy-start = (bf16[2,3328,512]{2,1,0:T(8,128)(2,1)S(1)}, bf16[2,3328,512]{2,1,0:T(8,128)(2,1)}, u32[]{:S(2)}) copy-start(bf16[2,3328,512]{2,1,0:T(8,128)(2,1)} %get-tuple-element.17) | copy-start | bytes 20447236
  325.1 5.2 %copy-start.1 = (f32[64,1024]{1,0:T(8,128)S(1)}, f32[64,1024]{1,0:T(8,128)}, u32[]{:S(2)}) copy-start(f32[64,1024]{1,0:T(8,128)} %get-tuple-element.16) | copy-start | bytes 786436
  325.7 5.5 %copy-start.2 = (bf16[64,1024]{1,0:T(8,128)(2,1)S(1)}, bf16[64,1024]{1,0:T(8,128)(2,1)}, u32[]{:S(2)}) copy-start(bf16[64,1024]{1,0:T(8,128)(2,1)} %get-tuple-element.15) | copy-start | bytes 393220

commit v2 on v1

--- a/solution.py
+++ b/solution.py
@@ -76,7 +76,7 @@
         return tuple(ks)
     return lax.fori_loop(0, cg.shape[0], step, first)
 
-def adjoint_scan(dt, du, dy, bg, cg, a2, an, first, h_all, q_all, w1, w2, s1, s2):
+def adjoint_scan(dt, du, dy, bg, cg, a2, an, first, h_all, q_all, w1, w2, s1, s2, between, parts):
     groups = cg.shape[0]
     seqs = len(first)
     def step(i, carry):
@@ -102,7 +102,11 @@
         take(s1, base, w1)
         take(s2, base, w2)
         return tuple(ks), acc
-    return lax.fori_loop(0, groups, step, (first, jnp.zeros_like(a2)))[1]
+    carry = (first, jnp.zeros_like(a2))
+    for part in range(parts):
+        carry = lax.fori_loop(part * groups // parts, (part + 1) * groups // parts, step, carry)
+        between()
+    return carry[1]
 
 def state_sums(all_rows, skip, vec, out):
     states = all_rows.shape[1]
@@ -131,6 +135,10 @@
     return jnp.maximum(v, 0.0) + jnp.log1p(jnp.exp(-jnp.abs(v)))
 
 
+def softplus_slope(dt):
+    return jnp.where(dt < 0.02, dt * (1.0 - dt * (1.0 / 2 - dt * (1.0 / 6 - dt / 24.0))), 1.0 - jnp.exp(-dt))
+
+
 class Place:
     def __init__(self, blocks, lanes):
         self.blocks, self.lanes = blocks, lanes
@@ -365,75 +373,87 @@
     return second
 
 
-def reduce_chunk(net, me, local, out, row, n, fill, bufs):
-    half = n // 2
-    piece = half // me.outers
-    gs, gm, zs, sh, xr, zr = bufs
-    slot = net.slots(3 + 3 * me.outers)
-    s_z, s_a, s_f = slot + 2, slot + 2 + me.outers, slot + 2 + 2 * me.outers
-    fill(1 - me.inner, gs)
-    pair = start(net.copy(gs, xr, me.at(dp=me.twin), slot))
-    fill(me.inner, gm)
-    yield
-
-    pair.wait()
-    gm[...] = gm[...] + xr[...].astype(F32)
-    zs[...] = gm[...].astype(zs.dtype)
-
-    def rows_of(o):
-        return pl.ds(pl.multiple_of(o * piece, 16), piece)
-
-    def give(k):
-        o = me.ahead(k)
-        return net.copy(zs.at[rows_of(o)], zr.at[k], me.at(dp=o * 2 + me.inner), s_z + k)
-
-    others(me.outers, lambda k: give(k).start())
-    yield
-
-    total = gm[rows_of(me.outer), :]
-    if me.outers <= 4:
-        for k in range(1, me.outers):
-            give(k).wait()
-            total = total + zr[k].astype(F32)
-    else:
-        def more(k, acc):
-            give(k).wait()
-            return acc + zr[k].astype(F32)
-        total = lax.fori_loop(1, me.outers, more, total)
-    sh[...] = total.astype(sh.dtype)
-
-    def place(o, inner):
-        return out.at[pl.ds(pl.multiple_of(row + inner * half + o * piece, 16), piece)]
-
-    keep = pltpu.make_async_copy(sh, place(me.outer, me.inner), local)
+class Pump:
+    def __init__(self):
+        self.now, self.free, self.active = 0.0, {}, []
+
+    def add(self, chunks):
+        self.active += [[c, self.now] for c in chunks]
+        self.poll()
+
+    def spend(self, us):
+        self.now += us
+        self.poll()
+
+    def poll(self):
+        for entry in list(self.active):
+            if entry[1] <= self.now:
+                self.step(entry)
+
+    def step(self, entry):
+        issued = next(entry[0], None)
+        if issued is None:
+            self.active.remove(entry)
+            return
+        link, us = issued
+        begin = max(self.now, self.free.get(link, 0.0))
+        self.free[link] = begin + us
+        entry[1] = begin + us + 2.0
+        self.now += 0.4
+
+    def drain(self):
+        while self.active:
+            entry = min(self.active, key=lambda e: e[1])
+            self.now = max(self.now, entry[1])
+            self.step(entry)
+
+
+def transfer(bit, ref):
+    us = 2e-5 * math.prod(ref.shape) * 2
+    return ("x", us) if bit == 0 else ("z", us * bit)
+
+
+def reduce_chunk(net, me, local, out, row, half, fill, bufs):
+    gm, sends, gots, sh = bufs
+    levels = len(sends) + 1
+    slot = net.slots(2 * levels)
+    yield from fill(gm)
+    off, size = 0, half
+
+    def bit_of(b):
+        return (me.dp // 2**b) % 2
+
+    def peer(b):
+        return me.at(dp=me.dp + (1 - 2 * bit_of(b)) * 2**b)
+
+    def part(ref, first, count):
+        return ref.at[pl.ds(pl.multiple_of(first, 16), count)]
+
+    for b in range(1, levels):
+        size //= 2
+        sends[b - 1][...] = part(gm, off + (1 - bit_of(b)) * size, size)[...].astype(BF16)
+        copy = start(net.copy(sends[b - 1], gots[b - 1], peer(b), slot + b))
+        yield transfer(b, sends[b - 1])
+        copy.wait()
+        off = off + bit_of(b) * size
+        mine = part(gm, off, size)
+        mine[...] = mine[...] + gots[b - 1][...].astype(F32)
+    sh[...] = part(gm, off, size)[...].astype(BF16)
+    base = row + me.inner * half
+    held = part(out, base + off, size)
+    keep = pltpu.make_async_copy(sh, held, local)
     keep.start()
-    across = start(net.copy(sh, place(me.outer, me.inner), me.at(dp=me.twin), slot + 1))
-
-    def spread_to(k):
-        return net.copy(sh, place(me.outer, me.inner), me.at(dp=me.ahead(k) * 2 + me.inner), s_a + k)
-
-    others(me.outers, lambda k: spread_to(k).start())
-    yield
-
-    def hand_on(k):
-        there = place(me.behind(k), me.inner)
-        return net.copy(there, there, me.at(dp=me.twin), s_f + k)
-
-    def forward(k):
-        spread_to(k).wait_recv()
-        hand_on(k).start()
-
-    others(me.outers, forward)
-    yield
-
-    across.wait()
-    keep.wait()
-
-    def close(k):
-        spread_to(k).wait_send()
-        hand_on(k).wait()
-
-    others(me.outers, close)
+    source = sh
+    for b in reversed(range(levels)):
+        copy = start(net.copy(source, held, peer(b), slot + levels + b))
+        yield transfer(b, held)
+        copy.wait()
+        if b == levels - 1:
+            keep.wait()
+        if b > 0:
+            off = off - bit_of(b) * size
+            size *= 2
+            source = held = part(out, base + off, size)
 
 
 def rms(x):
@@ -478,6 +498,13 @@
             send_sem=net.send.at[edge_slot], recv_sem=net.recv.at[edge_slot + me.mp],
             device_id=me.at(dp=me.twin), device_id_type=MESH,
         ).wait_recv()
+
+    @pl.when(last & (me.dp < me.blocks - 1))
+    def _():
+        for t in range(me.lanes):
+            edge(t).wait_send()
+
+    s.pending[l] = [start(net.copy(s.hn.at[l, pl.ds(EDGE, rows)], s.hnt.at[l], me.at(dp=me.twin), net.slots()))]
 
     s.xi[l] = dot(s.hn[l], s.win[l, 0], 1, 0).astype(BF16).astype(F32)
     conv = s.cb[l : l + 1, :]
@@ -497,7 +524,6 @@
     spread(s.bg.at[l], xd[rank : rank + states])
     spread(s.cg.at[l], xd[rank + states :])
     pre = dot(s.dtr[l], s.stp[l], 0, 0) + s.sb[l : l + 1, :]
-    s.pre[l] = pre
     dt = softplus(pre)
     s.dt[l] = dt
     s.du[...] = dt * s.u[l].astype(F32)
@@ -514,7 +540,7 @@
     own = totals_scan(s.dt.at[l], s.du, s.bg.at[l], a2, (zero,) * seqs)
     shared()
     first = entering_state(
-        net, me, own, s.sums.at[l], a2, s.st1.at[p], s.got1.at[p], s.st2.at[p], s.got2.at[p], True
+        net, me, own, s.sums.at[l], a2, s.st1, s.got1.at[p], s.st2, s.got2.at[p], True
     )()()
     for q in range(seqs):
         s.h[l, q] = first[q].astype(s.h.dtype)
@@ -526,79 +552,83 @@
     s.ys[l] = ys
     z = s.z[l]
     s.go[l] = (ys * z * jax.nn.sigmoid(z)).astype(BF16)
+    s.pending[l].append(start(net.copy(s.go.at[l], s.got.at[l], me.at(dp=me.twin), net.slots())))
     s.part[...] = dot(s.go[l], s.wout[l], 1, 0)
     total = scatter_sum(net, me, s.part, own_rows, s.rs1, s.rs2.at[p], s.rs3, s.rs4.at[p])()()
     s.x[l + 1] = s.x[l] + total
 
-    @pl.when(last & (me.dp < me.blocks - 1))
-    def _():
-        for t in range(me.lanes):
-            edge(t).wait_send()
+
+def small_rows(rows, blocks):
+    return -(-(rows + 16) // (8 * blocks)) * 8 * blocks
+
+
+def chunk_table(width, chans, blocks, small):
+    wide = chans // 2
+    half = max(512, 8 * blocks)
+    table, base = [], 0
+    for kind, rows, places in (("out", chans, width // chans), ("gate", width, 1), ("conv", width, 1), ("small", small, 1)):
+        step = min(half, rows)
+        for place in range(places):
+            for first in range(0, rows, step):
+                table.append((kind, first, place * wide, base, step))
+                base += 2 * step
+    return table, base
 
 
 def gradient_chunks(net, me, l, s):
     rows = s.dt.shape[1]
     chans = s.dt.shape[2]
     width = s.x.shape[2]
-    big = max(512, EDGE * me.blocks)
-    made = []
-
-    def bufs(first, n):
-        half, piece = n // 2, n // 2 // me.outers
-        r = pl.ds(first // 2, half)
-        return (
-            s.gs.at[r], s.gm.at[r], s.zs.at[r], s.sh.at[pl.ds(first // 2 // me.outers, piece)],
-            s.xr.at[l, r], s.zr.at[l, pl.ds(0, me.outers), pl.ds(first // 2 // me.outers, piece)],
-        )
-
-    def add(first, n, fill):
-        made.append(reduce_chunk(net, me, s.local.at[l, len(made)], s.gout.at[l], first, n, fill, bufs(first, n)))
-
-    def out_rows(first, n):
-        def fill(h, ref):
-            begin = first + h * (n // 2)
-            d0 = pl.multiple_of(begin // chans * chans, chans)
-            c0 = pl.multiple_of(begin % chans, min(n // 2, chans))
-            left = s.go[l, :, pl.ds(c0, n // 2)]
-            right = s.do[l, :, pl.ds(d0, chans)]
-            ref[...] = dot(left, right, 0, 0).astype(ref.dtype)
+    wide = chans // 2
+    table, _ = chunk_table(width, chans, me.blocks, s.small.shape[1])
+    levels = me.blocks.bit_length() - 1
+    hn = s.hn.at[l, pl.ds(EDGE, rows)]
+
+    def bufs(base, half):
+        first, sends, gots, size = base // 2, [], [], half
+        for b in range(1, levels):
+            size //= 2
+            r = pl.ds((base // 2) // 2**b, size)
+            sends.append(s.zs.at[b - 1, r])
+            gots.append(s.zr.at[l, b - 1, r])
+        return s.gm.at[pl.ds(first, half)], sends, gots, s.sh.at[pl.ds((base // 2) // 2 ** (levels - 1), size)]
+
+    def out_fill(first, place, half):
+        def fill(gm):
+            d0 = pl.multiple_of(me.inner * (width // 2) + place, wide)
+            mine = dot(s.go[l, :, first : first + half], s.do[:, pl.ds(d0, wide)], 0, 0)
+            gm[...] = mine + dot(s.got[l, :, first : first + half], s.dor[l, :, place : place + wide], 0, 0)
+            yield from ()
         return fill
 
-    def in_rows(first, n, ref2):
-        def fill(h, ref):
-            d0 = pl.multiple_of(first + h * (n // 2), n // 2)
-            left = s.hn[l, EDGE : EDGE + rows, pl.ds(d0, n // 2)]
-            ref[...] = dot(left, ref2[...], 0, 0).astype(ref.dtype)
+    def in_fill(first, half, own, other):
+        def fill(gm):
+            mine = dot(hn[:, first : first + half], own[me.inner], 0, 0)
+            gm[...] = mine + dot(s.hnt[l, :, first : first + half], other[...], 0, 0)
+            yield from ()
         return fill
 
-    def small_rows(n):
-        def fill(h, ref):
-            ref[...] = s.small[pl.ds(pl.multiple_of(h * (n // 2), 16), n // 2), :].astype(ref.dtype)
-        return fill
-
-    groups = []
-    for which in range(3):
-        names = []
-        for first in range(0, width, big):
-            base = which * width + first
-            names.append(len(made))
-            if which == 0:
-                add(base, big, out_rows(first, big))
-            else:
-                add(base, big, in_rows(first, big, s.dxi if which == 1 else s.dz.at[l]))
-        groups.append([made[i] for i in names])
-    n = s.small.shape[0]
-    add(3 * width, n, small_rows(n))
-    out, conv, gate = groups
-    return out, gate, conv, [made[-1]]
-
-
-def advance(chunks):
-    for c in chunks:
-        next(c, None)
-
-
-def backward_layer(net, me, l, s, before):
+    def small_fill(gm):
+        slot = net.slots()
+        s.smalls[...] = s.small[1 - me.inner].astype(BF16)
+        pair = start(net.copy(s.smalls, s.smallr.at[l], me.at(dp=me.twin), slot))
+        yield transfer(0, s.smalls)
+        pair.wait()
+        gm[...] = s.small[me.inner] + s.smallr[l].astype(F32)
+
+    made = {"out": [], "gate": [], "conv": [], "small": []}
+    for i, (kind, first, place, base, half) in enumerate(table):
+        fill = {
+            "out": lambda: out_fill(first, place, half),
+            "gate": lambda: in_fill(first, half, s.dzh, s.dzr.at[l]),
+            "conv": lambda: in_fill(first, half, s.dxh, s.dxr.at[l]),
+            "small": lambda: small_fill,
+        }[kind]()
+        made[kind].append(reduce_chunk(net, me, s.local.at[l, i], s.gout.at[l], base, half, fill, bufs(base, half)))
+    return made["out"], made["gate"], made["conv"], made["small"]
+
+
+def backward_layer(net, me, l, s, pump):
     own_rows = s.x.shape[1]
     rows = s.dt.shape[1]
     seqs = s.seqs
@@ -610,15 +640,24 @@
     out, gate, conv, small = gradient_chunks(net, me, l, s)
 
     at = pl.multiple_of(me.mp * own_rows, 16)
-    s.do[l, pl.ds(at, own_rows), :] = s.g[...].astype(BF16)
-    gathered = gather_rows(net, me, s.do.at[l], 0, own_rows)
-    advance(before)
+    s.do[pl.ds(at, own_rows), :] = s.tgrad[...].astype(BF16)
+    gathered = gather_rows(net, me, s.do, 0, own_rows)
+    pump.spend(4)
     gathered()
-    dgo = dot(s.do[l], s.wout[l], 1, 1)
+    half = s.do.shape[1] // 2
+    theirs = pl.ds(pl.multiple_of((1 - me.inner) * half, 128), half)
+    do_sent = start(net.copy(s.do.at[:, theirs], s.dor.at[l], me.at(dp=me.twin), net.slots()))
+    pump.spend(1.5)
+    dgo = dot(s.do[...], s.wout[l], 1, 1)
     z = s.z[l]
     sg = jax.nn.sigmoid(z)
     s.dy[...] = dgo * z * sg
-    s.dz[l] = (dgo * s.ys[l] * silu_slope(z, sg)).astype(BF16)
+    dz = (dgo * s.ys[l] * silu_slope(z, sg)).astype(BF16)
+    s.dz[...] = dz
+    for i in range(2):
+        s.dzh[i] = dz[:, i * chans // 2 : (i + 1) * chans // 2]
+    dz_sent = start(net.copy(s.dzh.at[1 - me.inner], s.dzr.at[l], me.at(dp=me.twin), net.slots()))
+    pump.spend(1.5)
 
     s.du[...] = s.dt[l] * s.u[l].astype(F32)
     an = -jnp.exp(s.dlog[l])
@@ -626,42 +665,58 @@
     zero = jnp.zeros_like(a2)
     own = adjoint_totals(s.dt.at[l], s.dy, s.cg.at[l], a2, (zero,) * seqs)
     second = entering_state(
-        net, me, own, s.sums.at[l], a2, s.st1.at[p], s.got1.at[p], s.st2.at[p], s.got2.at[p], False
+        net, me, own, s.sums.at[l], a2, s.st1, s.got1.at[p], s.st2, s.got2.at[p], False
     )
-    advance(out)
+    pump.spend(2.8)
+    hn_sent, go_sent = s.pending[l]
+    do_sent.wait()
+    go_sent.wait()
+    pump.add(out)
     finish = second()
-    advance(gate)
-    advance(before)
+    hn_sent.wait()
+    dz_sent.wait()
+    pump.add(gate)
+    pump.spend(1)
     last = finish()
+    pump.spend(2.5)
     acc = adjoint_scan(
-        s.dt.at[l], s.du, s.dy, s.bg.at[l], s.cg.at[l], a2, an, last, s.h.at[l], s.q, s.w1, s.w2, s.s1, s.s2
+        s.dt.at[l], s.du, s.dy, s.bg.at[l], s.cg.at[l], a2, an, last, s.h.at[l], s.q, s.w1, s.w2, s.s1, s.s2,
+        lambda: pump.spend(1.5), 4,
     )
-    advance(out + gate + before)
     x0 = s.xd.shape[1] - 2 * states
     state_sums(s.q, 0, s.du, s.xd.at[p, pl.ds(x0, states)])
     state_sums(s.h.at[l], seqs, s.dy, s.xd.at[p, pl.ds(x0 + states, states)])
 
+    pump.spend(2)
+
     u = s.u[l].astype(F32)
-    dpre = ((s.s1[...] + s.s2[...] * u) * jax.nn.sigmoid(s.pre[l])).astype(BF16)
+    dpre = ((s.s1[...] + s.s2[...] * u) * softplus_slope(s.dt[l])).astype(BF16)
     s.s2[...] = s.s2[...] * s.dt[l] + s.skip[l : l + 1, :] * s.dy[...]
     s.xd[p, 0:rank, :] = dot(s.stp[l], dpre, 1, 1)
     second = sum_lanes(net, me, s.xd.at[p], s.xd1.at[p], s.xd2.at[p])
     xw = s.xd.shape[1]
-    s.small[xw : xw + rank, :] = dot(s.dtr[l], dpre, 1, 0)
-    s.small[xw + rank : xw + rank + states, :] = an * acc
     v0 = xw + rank + states
-    s.small[v0 + taps + 2 : v0 + taps + 3, :] = jnp.sum(dpre.astype(F32), axis=0, keepdims=True)
-    s.small[v0 + taps + 1 : v0 + taps + 2, :] = jnp.sum(s.dy[...] * u, axis=0, keepdims=True)
+
+    def keep(first, value):
+        for i in range(2):
+            s.small[i, first : first + value.shape[0], :] = value[:, i * chans // 2 : (i + 1) * chans // 2]
+
+    keep(xw, dot(s.dtr[l], dpre, 1, 0))
+    keep(xw + rank, an * acc)
+    keep(v0 + taps + 2, jnp.sum(dpre.astype(F32), axis=0, keepdims=True))
+    keep(v0 + taps + 1, jnp.sum(s.dy[...] * u, axis=0, keepdims=True))
+    pump.spend(1)
     finish = second()
-    advance(out + gate + before)
+    pump.spend(3.5)
     dxr = finish().astype(BF16)
+    pump.spend(0.5)
     xc = s.xc[l]
     du = s.s2[...] + dot(dxr, s.stt[l], 0, 0)
     dxc = du * silu_slope(xc, jax.nn.sigmoid(xc))
-    s.dxc[l, 0:rows, :] = dxc
+    s.dxc[0:rows, :] = dxc
 
     slot = net.slots()
-    edge = net.copy(s.dxc.at[l, pl.ds(0, 8)], s.dxc.at[l, pl.ds(rows, 8)], me.at(dp=me.dp - 1), slot)
+    edge = net.copy(s.dxc.at[pl.ds(0, 8)], s.tail.at[l], me.at(dp=me.dp - 1), slot)
 
     @pl.when(me.dp > 0)
     def _():
@@ -669,51 +724,64 @@
 
     @pl.when(me.dp == me.blocks - 1)
     def _():
-        s.dxc[l, rows : rows + 8, :] = jnp.zeros((8, chans), F32)
-
-    s.small[0:xw, :] = dot(dxr, s.u[l], 1, 0)
-    s.small[v0 + taps : v0 + taps + 1, :] = jnp.sum(dxc, axis=0, keepdims=True)
+        s.tail[l] = jnp.zeros((8, chans), F32)
+
+    keep(0, dot(dxr, s.u[l], 1, 0))
+    keep(v0 + taps, jnp.sum(dxc, axis=0, keepdims=True))
     for k in range(taps):
         off = EDGE - seqs * (taps - 1 - k)
-        s.small[v0 + k : v0 + k + 1, :] = jnp.sum(dxc * s.xi[l, off : off + rows, :], axis=0, keepdims=True)
-    s.part[...] = dot(s.dz[l], s.win[l, 1], 1, 1)
+        keep(v0 + k, jnp.sum(dxc * s.xi[l, off : off + rows, :], axis=0, keepdims=True))
+    s.part[...] = dot(s.dz[...], s.win[l, 1], 1, 1)
+    pump.spend(1.5)
 
     @pl.when(me.dp < me.blocks - 1)
     def _():
-        net.copy(s.dxc.at[l, pl.ds(0, 8)], s.dxc.at[l, pl.ds(rows, 8)], me.at(dp=me.twin), slot).wait_recv()
-
+        net.copy(s.dxc.at[pl.ds(0, 8)], s.tail.at[l], me.at(dp=me.twin), slot).wait_recv()
+
+    s.dxc[rows : rows + 8, :] = s.tail[l]
     dxi = jnp.zeros((rows, chans), F32)
     for k in range(taps):
         off = seqs * (taps - 1 - k)
-        dxi = dxi + s.ck[l, k : k + 1, :].astype(F32) * s.dxc[l, off : off + rows, :]
-    s.dxi[...] = dxi.astype(BF16)
-
-    s.part[...] = s.part[...] + dot(s.dxi[...], s.win[l, 0], 1, 1)
+        dxi = dxi + s.ck[l, k : k + 1, :].astype(F32) * s.dxc[off : off + rows, :]
+    dxi = dxi.astype(BF16)
+    for i in range(2):
+        s.dxh[i] = dxi[:, i * chans // 2 : (i + 1) * chans // 2]
+    dxi_sent = start(net.copy(s.dxh.at[1 - me.inner], s.dxr.at[l], me.at(dp=me.twin), net.slots()))
+
+    s.part[...] = s.part[...] + dot(dxi, s.win[l, 0], 1, 1)
     second = scatter_sum(net, me, s.part, own_rows, s.rs1, s.rs2.at[p], s.rs3, s.rs4.at[p])
-    advance(conv)
+    pump.spend(2)
     finish = second()
-    advance(out + gate + before)
+    dxi_sent.wait()
+    pump.add(conv)
+    pump.spend(3)
     dhn = finish()
     x = s.x[l]
     inv = rms(x)
     part = jnp.sum(dhn * x * inv, axis=0, keepdims=True)
     g0 = v0 + 8
+    wide = chans // 2
+    count = x.shape[1] // wide
     s.gg[l] = jnp.zeros_like(s.gg[l])
-    for j in range(x.shape[1] // chans):
-        s.gg[l, j : j + 1, :] = part[:, j * chans : (j + 1) * chans]
+    for j in range(count):
+        s.gg[l, j : j + 1, :] = part[:, j * wide : (j + 1) * wide]
     dr = dhn * s.gain[l : l + 1, :]
-    s.g[...] = s.g[...] + inv * dr - x * (inv * inv * inv) * jnp.mean(dr * x, axis=-1, keepdims=True)
+    s.tgrad[...] = s.tgrad[...] + inv * dr - x * (inv * inv * inv) * jnp.mean(dr * x, axis=-1, keepdims=True)
 
     @pl.when(me.dp > 0)
     def _():
         edge.wait_send()
 
-    s.small[g0 : g0 + 8, :] = sum_lanes(net, me, s.gg.at[l], s.gg1.at[l], s.gg2.at[l])()()
-    if s.small.shape[0] > g0 + 8:
-        s.small[g0 + 8 :, :] = jnp.zeros((s.small.shape[0] - g0 - 8, chans), F32)
-    s.small[v0 + taps + 3 : g0, :] = jnp.zeros((g0 - v0 - taps - 3, chans), F32)
-    advance(small)
-    return out + gate + conv + small
+    second = sum_lanes(net, me, s.gg.at[l], s.gg1.at[l], s.gg2.at[l])
+    pump.spend(2)
+    finish = second()
+    pump.spend(2)
+    total = finish()
+    for i in range(2):
+        s.small[i, g0 : g0 + count // 2, :] = total[i * count // 2 : (i + 1) * count // 2]
+        s.small[i, g0 + count // 2 :, :] = jnp.zeros((s.small.shape[1] - g0 - count // 2, wide), F32)
+        s.small[i, v0 + taps + 3 : g0, :] = jnp.zeros((g0 - v0 - taps - 3, wide), F32)
+    pump.add(small)
 
 
 class Refs:
@@ -724,7 +792,7 @@
     s = Refs()
     for name, ref in zip(names, refs, strict=True):
         setattr(s, name, ref)
-    s.seqs = seqs
+    s.seqs, s.pending = seqs, {}
     me = Place(blocks, lanes)
     net = Net(s.send, s.recv)
     entry_barrier(me)
@@ -733,18 +801,11 @@
     for l in range(layers):
         forward_layer(net, me, l, s)
     s.lout[...] = s.x[layers].astype(s.lout.dtype)
-    s.g[...] = s.g0[...]
-    before = []
+    s.tgrad[...] = s.g0[...]
+    pump = Pump()
     for l in reversed(range(layers)):
-        done = backward_layer(net, me, l, s, before)
-        if before:
-            for c in before:
-                for _ in c:
-                    pass
-        before = done
-    s.tgrad[...] = s.g[...]
-    for _ in range(6):
-        advance(before)
+        backward_layer(net, me, l, s, pump)
+    pump.drain()
 
 
 def layers_call(mesh, tokens, grad, gain, win, ck, cb, stt, stp, sb, dlog, skip, wout):
@@ -755,30 +816,29 @@
     layers, chans = skip.shape
     states, rank, xw, taps = dlog.shape[1], stp.shape[1], stt.shape[1], ck.shape[1]
     outers = blocks // 2
-    small = -(-(xw + rank + states + 16) // (EDGE * blocks)) * EDGE * blocks
-    grads = 3 * width + small
+    levels = blocks.bit_length() - 1
+    small = small_rows(xw + rank + states, blocks)
+    table, grads = chunk_table(width, chans, blocks, small)
+    chunks = len(table)
+    wide = chans // 2
     groups = rows // GRP
     slots = layers * (3 * 2 + 2 * 3 + 3 * 2 + lanes + blocks + 2 * (1 + outers) + 1)
-    chunks = 3 * (width // max(512, EDGE * blocks)) + 1
-    slots += layers * chunks * (3 + 3 * outers)
+    slots += layers * (chunks * 2 * levels + 6)
     two = 2 * layers
     ins = ["tok", "g0", "gain", "win", "ck", "cb", "stt", "stp", "sb", "dlog", "skip", "wout"]
     outs = {
         "lout": ((own_rows, width), BF16),
         "tgrad": ((own_rows, width), F32),
-        "gout": ((layers, grads, chans), BF16),
+        "gout": ((layers, grads, wide), BF16),
     }
     half = grads // 2
-    piece = half // outers
     scratch = {
         "x": ((layers + 1, own_rows, width), F32),
-        "g": ((own_rows, width), F32),
         "hn": ((layers, EDGE + rows, width), BF16),
         "xi": ((layers, EDGE + rows, chans), F32),
         "xc": ((layers, rows, chans), F32),
         "u": ((layers, rows, chans), BF16),
         "z": ((layers, rows, chans), F32),
-        "pre": ((layers, rows, chans), F32),
         "dt": ((layers, rows, chans), F32),
         "du": ((rows, chans), F32),
         "ys": ((layers, rows, chans), F32),
@@ -790,13 +850,13 @@
         "q": ((rows, states, chans), BF16),
         "w1": ((chans // 128, GRP * 8, 128), F32),
         "w2": ((chans // 128, GRP * 8, 128), F32),
-        "do": ((layers, rows, width), BF16),
+        "do": ((rows, width), BF16),
         "dy": ((rows, chans), F32),
-        "dz": ((layers, rows, chans), BF16),
+        "tail": ((layers, 8, chans), F32),
+        "dz": ((rows, chans), BF16),
         "s1": ((rows, chans), F32),
         "s2": ((rows, chans), F32),
-        "dxc": ((layers, rows + 8, chans), F32),
-        "dxi": ((rows, chans), BF16),
+        "dxc": ((rows + 8, chans), F32),
         "part": ((rows, width), F32),
         "rs1": ((2, own_rows, width), BF16),
         "rs2": ((two, 2, own_rows, width), BF16),
@@ -806,20 +866,27 @@
         "xd1": ((two, xw, rows), F32),
         "xd2": ((two, xw, rows), F32),
         "sums": ((layers, blocks, seqs * chans // 128, 128), F32),
-        "st1": ((two, seqs, states, chans), BF16),
+        "st1": ((seqs, states, chans), BF16),
         "got1": ((two, seqs, states, chans), BF16),
-        "st2": ((two, seqs, states, chans), BF16),
+        "st2": ((seqs, states, chans), BF16),
         "got2": ((two, outers, seqs, states, chans), BF16),
-        "small": ((small, chans), F32),
-        "gg": ((layers, 8, chans), F32),
-        "gg1": ((layers, 8, chans), F32),
-        "gg2": ((layers, 8, chans), F32),
-        "gs": ((half, chans), BF16),
-        "gm": ((half, chans), F32),
-        "zs": ((half, chans), BF16),
-        "sh": ((piece, chans), BF16),
-        "xr": ((layers, half, chans), BF16),
-        "zr": ((layers, outers, piece, chans), BF16),
+        "small": ((2, small, wide), F32),
+        "smalls": ((small, wide), BF16),
+        "smallr": ((layers, small, wide), BF16),
+        "gg": ((layers, 8, wide), F32),
+        "gg1": ((layers, 8, wide), F32),
+        "gg2": ((layers, 8, wide), F32),
+        "hnt": ((layers, rows, width), BF16),
+        "got": ((layers, rows, chans), BF16),
+        "dor": ((layers, rows, width // 2), BF16),
+        "dzh": ((2, rows, wide), BF16),
+        "dzr": ((layers, rows, wide), BF16),
+        "dxh": ((2, rows, wide), BF16),
+        "dxr": ((layers, rows, wide), BF16),
+        "gm": ((half, wide), F32),
+        "zs": ((levels - 1, half // 2, wide), BF16),
+        "zr": ((layers, levels - 1, half // 2, wide), BF16),
+        "sh": ((half // 2 ** (levels - 1), wide), BF16),
     }
     names = ins + list(outs) + list(scratch) + ["local", "send", "recv"]
     any_space = pl.BlockSpec(memory_space=pl.ANY)
@@ -835,6 +902,75 @@
             collective_id=0, has_side_effects=True, vmem_limit_bytes=63 * 2**20
         ),
     )(tokens.reshape(own_rows, width), grad, gain, win, ck, cb, stt, stp, sb, dlog, skip, wout)
+
+
+def unpack_kernel(names, table, *refs):
+    s = Refs()
+    for name, ref in zip(names, refs, strict=True):
+        setattr(s, name, ref)
+    l = pl.program_id(0)
+    layers, chans = s.cb.shape
+    width = s.gain.shape[1]
+    wide = chans // 2
+    taps, xw, rank, states = s.ck.shape[1], s.sp.shape[2], s.stp.shape[1], s.dlog.shape[1]
+    v0 = xw + rank + states
+
+    @pl.when(l == 0)
+    def _():
+        seg, seqs, _ = s.lout.shape
+        for p in range(seg):
+            s.lout[p] = s.lo[p * seqs : (p + 1) * seqs, :]
+            s.tgrad[p] = s.tg[p * seqs : (p + 1) * seqs, :]
+
+    row = lax.broadcasted_iota(jnp.int32, (layers, wide), 0) == l
+
+    def put(ref, at, value):
+        ref[:, at : at + wide] = jnp.where(row, value, ref[:, at : at + wide])
+
+    for kind, first, place, base, half in table:
+        for i in range(2):
+            block = s.grads[0, base + i * half : base + (i + 1) * half, :].astype(F32)
+            if kind == "out":
+                at = i * (width // 2) + place
+                s.wout[0, first : first + half, at : at + wide] = block
+            elif kind == "small":
+                cols = slice(i * wide, (i + 1) * wide)
+                s.sp[0, cols, :] = block[:xw].T
+                s.stp[0, :, cols] = block[xw : xw + rank]
+                s.dlog[0, :, cols] = block[xw + rank : v0]
+                s.ck[0, :, cols] = block[v0 : v0 + taps]
+                for j, ref in enumerate((s.cb, s.skip, s.sb)):
+                    put(ref, i * wide, block[v0 + taps + j : v0 + taps + j + 1])
+                for j in range(width // chans):
+                    put(s.gain, i * (width // 2) + j * wide, block[v0 + 8 + j : v0 + 9 + j])
+            else:
+                s.win[0, 0 if kind == "conv" else 1, first : first + half, i * wide : (i + 1) * wide] = block
+
+
+def unpack_call(table, lout, tgrad, gout, shape, gain, win, ck, sp, stp, dlog, wout):
+    layers, _, width, chans = win.shape
+    ins = ["lo", "tg", "grads"]
+    outs = {
+        "lout": (shape, BF16), "tgrad": (shape, F32), "gain": (gain.shape, F32), "win": (win.shape, F32), "ck": (ck.shape, F32),
+        "cb": ((layers, chans), F32), "sp": (sp.shape, F32), "stp": (stp.shape, F32), "sb": ((layers, chans), F32),
+        "dlog": (dlog.shape, F32), "skip": ((layers, chans), F32), "wout": (wout.shape, F32),
+    }
+
+    def whole(a):
+        return pl.BlockSpec(a, lambda l: (0,) * len(a))
+
+    def layer(a):
+        return pl.BlockSpec((1,) + a[1:], lambda l: (l,) + (0,) * (len(a) - 1))
+
+    once = {"lout", "tgrad", "gain", "cb", "sb", "skip"}
+    return pl.pallas_call(
+        functools.partial(unpack_kernel, ins + list(outs), table),
+        grid=(layers,),
+        out_shape=[jax.ShapeDtypeStruct(a, t) for a, t in outs.values()],
+        in_specs=[whole(lout.shape), whole(tgrad.shape), layer(gout.shape)],
+        out_specs=[whole(a) if name in once else layer(a) for name, (a, _) in outs.items()],
+        compiler_params=pltpu.CompilerParams(vmem_limit_bytes=50 * 2**20),
+    )(lout, tgrad, gout)
 
 
 def body(
@@ -864,25 +1000,10 @@
     )
     layers, chans = skip_gain.shape
     xw, rank, states, taps = state_proj.shape[2], step_proj.shape[1], decay_log.shape[1], conv_kernel.shape[1]
-    gout = gout.astype(F32)
-    out = gout[:, :width].reshape(layers, width // chans, chans, chans).transpose(0, 2, 1, 3).reshape(layers, chans, width)
-    inp = gout[:, width : 3 * width].reshape(layers, 2, width, chans)
-    rest = gout[:, 3 * width :]
-    v0 = xw + rank + states
-    return (
-        lout.reshape(tokens.shape),
-        tgrad.reshape(tokens.shape),
-        rest[:, v0 + 8 : v0 + 8 + width // chans].reshape(layers, width),
-        inp,
-        rest[:, v0 : v0 + taps],
-        rest[:, v0 + taps],
-        rest[:, :xw].transpose(0, 2, 1),
-        rest[:, xw : xw + rank],
-        rest[:, v0 + taps + 2],
-        rest[:, xw + rank : v0],
-        rest[:, v0 + taps + 1],
-        out,
-    )
+    xw, rank, states = state_proj.shape[2], step_proj.shape[1], decay_log.shape[1]
+    blocks = mesh.shape["dp"]
+    table, _ = chunk_table(width, skip_gain.shape[1], blocks, small_rows(xw + rank + states, blocks))
+    return unpack_call(table, lout, tgrad, gout, tokens.shape, norm_gain, input_proj, conv_kernel, state_proj, step_proj, decay_log, output_proj)
 
 
 def solution(mesh):

time: 332 us -> 268 us (0.81)
  Pallas kernels: 300 us -> 260 us
  local copies, waits for them, and re-layouts: 19.1 us -> 5.37 us
  other arithmetic: 11.7 us -> 1.8 us
    pallas_call x1, Pallas kernels: 300 us -> 253 us  [layers_call(): pl.pallas_call(functools.partial(kernel, names, seqs, blocks, lanes), out...]
    convert_element_type x1 -> x0, other arithmetic: 9.92 us -> none  [body(): gout = gout.astype(F32)]
    slice x6 -> x0, local copies, waits for them, and re-layouts: 7.98 us -> none  [the longest x1 4.59 us: body(): inp = gout[:, width:3 * width].reshape(layers, 2, width, chans)]
    pallas_call x0 -> x1, Pallas kernels: none -> 7.31 us  [unpack_call(): pl.pallas_call(functools.partial(unpack_kernel, ins + list(outs), table),...]
    reshape x3 -> x0, local copies, waits for them, and re-layouts: 4.22 us -> none  [the longest x1 2.66 us: body(): gout[:, :width].reshape(layers, width // chans, chans, chans)]
where the time goes in v2:
time: 268 us
  Pallas kernels  260 us (97%)
  local copies, waits for them, and re-layouts  5.37 us (2%)
    pallas_call x1, Pallas kernels, layers_call(): pl.pallas_call(functools.partial(kernel, names, seqs, blocks, lanes), out...  253 us
    pallas_call x1, Pallas kernels, unpack_call(): pl.pallas_call(functools.partial(unpack_kernel, ins + list(outs), table),...  7.31 us

profile of v2, /device:TPU:0, one launch (start us, length us, event | category | flops | bytes accessed | tf_op | source)
XLA Modules:
  0.0 267.8 jit_solution(10084258800837820505)
XLA Ops:
  0.7 0.8 compare_select_fusion
  1.4 0.1 copy.26
  1.5 1.6 reshape.32.refs_0_
  3.1 1.0 convert_multiply_fusion
  4.2 0.9 reshape.33.refs_1_
  5.0 252.7 %shard_map.229 = (bf16[64,1024]{1,0:T(8,128)(2,1)}, f32[64,1024]{1,0:T(8,128)}, bf16[2,6528,256]{2,1,0:T(8,128)(2,1)}) custom-call(bf16[64,1024]{1,0:T(8,128)(2,1)} %reshape.32.refs_0_, f32[64,1024]{1,0:T(8,128)} %reshape.33.refs_1_, f32[2,1024]{1,0:T(2,128)} %refs_2_.1, bf16[2,2,1024,512]{3,2,1,0:T(8,128)(2,1)} %refs_3_.1, bf16[2,4,512]{2,1,0:T(4,128)(2,1)} %refs_4_.1, ...), custom_call_target="tpu_custom_call" | custom-call | tf_op jit(solution)/shard_map/pallas_call | solution.py:895
  257.7 0.0 copy-start
  257.7 0.9 copy-done
  258.7 0.0 copy-start.1
  258.7 0.9 copy-done.1
  259.6 7.3 %shard_map.230 = (bf16[32,2,1024]{2,1,0:T(2,128)(2,1)}, f32[32,2,1024]{2,1,0:T(2,128)}, f32[2,1024]{1,0:T(2,128)}, f32[2,2,1024,512]{3,2,1,0:T(8,128)}, f32[2,4,...) custom-call(bf16[64,1024]{1,0:T(8,128)(2,1)S(1)} %copy-done.1, ...), custom_call_target="tpu_custom_call" | custom-call | tf_op jit(solution)/shard_map/pallas_call | solution.py:966
  266.9 0.9 copy.27
  (1 shorter events, 0.0 us)
Async XLA Ops:
  257.7 1.0 copy-start
  258.7 0.9 copy-start.1

commit v3 on v2

--- a/solution.py
+++ b/solution.py
@@ -14,6 +14,8 @@
 LOG2E = math.log2(math.e)
 MESH = pl.DeviceIdType.MESH
 VMEM = pltpu.VMEM
+HALF = 512
+GSPACE = [False]
 EDGE = 16
 
 GRP = 16
@@ -214,7 +216,7 @@
         greet(me.dp - 1, top)
 
     greeted = jnp.where(me.mp == top, jnp.where(me.dp < me.blocks - 1, top, 0), jnp.where(me.dp > 0, 1, 0))
-    pl.semaphore_wait(sem, 2 + me.blocks - 1 + greeted)
+    return lambda: pl.semaphore_wait(sem, 2 + me.blocks - 1 + greeted)
 
 
 def gather_rows(net, me, full, base, rows):
@@ -238,18 +240,19 @@
     return finish
 
 
-def sum_lanes(net, me, own, got1, got2):
+def sum_lanes(net, me, own, got1, far, got2):
     slot = net.slots(2)
     near = start(net.copy(own, got1, me.at(mp=me.core), slot))
 
     def second():
         near.wait()
-        own[...] = own[...] + got1[...]
-        far = start(net.copy(own, got2, me.at(mp=me.chip), slot + 1))
+        total = own[...] + got1[...]
+        far[...] = total.astype(far.dtype)
+        copy = start(net.copy(far, got2, me.at(mp=me.chip), slot + 1))
 
         def finish():
-            far.wait()
-            return own[...] + got2[...]
+            copy.wait()
+            return total + got2[...].astype(F32)
 
         return finish
 
@@ -374,43 +377,54 @@
 
 
 class Pump:
+    latency, cost, early, scale = 2.0, 0.3, 1.0, 1.0
+
     def __init__(self):
         self.now, self.free, self.active = 0.0, {}, []
 
     def add(self, chunks):
-        self.active += [[c, self.now] for c in chunks]
+        self.active += [[gen, self.now, list(plan)] for gen, plan in chunks]
         self.poll()
+
+    def when(self, entry):
+        links = entry[2][0] if entry[2] else []
+        return max([entry[1]] + [self.free.get(link, 0.0) - self.early for link, _ in links])
 
     def spend(self, us):
         self.now += us
         self.poll()
 
     def poll(self):
-        for entry in list(self.active):
-            if entry[1] <= self.now:
-                self.step(entry)
+        while True:
+            ready = [e for e in self.active if self.when(e) <= self.now]
+            if not ready:
+                return
+            self.step(ready[0])
 
     def step(self, entry):
-        issued = next(entry[0], None)
-        if issued is None:
+        links = entry[2].pop(0) if entry[2] else []
+        if next(entry[0], None) is None:
             self.active.remove(entry)
             return
-        link, us = issued
-        begin = max(self.now, self.free.get(link, 0.0))
-        self.free[link] = begin + us
-        entry[1] = begin + us + 2.0
-        self.now += 0.4
+        done = self.now
+        for link, us in links:
+            self.free[link] = max(self.now, self.free.get(link, 0.0)) + us * self.scale
+            done = max(done, self.free[link])
+        entry[1] = done + (self.latency if links else 0.0)
+        self.now += self.cost
 
     def drain(self):
         while self.active:
-            entry = min(self.active, key=lambda e: e[1])
-            self.now = max(self.now, entry[1])
+            entry = min(self.active, key=self.when)
+            self.now = max(self.now, self.when(entry))
             self.step(entry)
 
 
-def transfer(bit, ref):
-    us = 2e-5 * math.prod(ref.shape) * 2
-    return ("x", us) if bit == 0 else ("z", us * bit)
+def transfer(bit, values):
+    us = 2e-5 * values * 2
+    if bit == 0:
+        return [("x", us)]
+    return [("z", us)] if bit == 1 else [("z", us), ("middle", us * bit)]
 
 
 def reduce_chunk(net, me, local, out, row, half, fill, bufs):
@@ -418,6 +432,7 @@
     levels = len(sends) + 1
     slot = net.slots(2 * levels)
     yield from fill(gm)
+    yield True
     off, size = 0, half
 
     def bit_of(b):
@@ -433,7 +448,7 @@
         size //= 2
         sends[b - 1][...] = part(gm, off + (1 - bit_of(b)) * size, size)[...].astype(BF16)
         copy = start(net.copy(sends[b - 1], gots[b - 1], peer(b), slot + b))
-        yield transfer(b, sends[b - 1])
+        yield True
         copy.wait()
         off = off + bit_of(b) * size
         mine = part(gm, off, size)
@@ -446,7 +461,7 @@
     source = sh
     for b in reversed(range(levels)):
         copy = start(net.copy(source, held, peer(b), slot + levels + b))
-        yield transfer(b, held)
+        yield True
         copy.wait()
         if b == levels - 1:
             keep.wait()
@@ -456,11 +471,41 @@
             source = held = part(out, base + off, size)
 
 
+def chunk_plan(levels, values, first):
+    plan = first + [[]]
+    for b in range(1, levels):
+        plan.append(transfer(b, values >> b))
+    for b in reversed(range(levels)):
+        plan.append(transfer(b, values >> b))
+    return plan
+
+
 def rms(x):
     return lax.rsqrt(jnp.mean(x * x, axis=-1, keepdims=True) + EPS)
 
 
-def forward_layer(net, me, l, s):
+def load_weights(s):
+    layers = s.gain.shape[0]
+    copies = {}
+    names = ["win", "stt", "stp", "wout"]
+    for l in range(layers):
+        for i, name in enumerate(names):
+            hbm, vmem = getattr(s, name + "_hbm"), getattr(s, name)
+            copies[name, l] = start(pltpu.make_async_copy(hbm.at[l], vmem.at[l], s.loaded.at[l, i]))
+    return copies
+
+
+def first_gradient(me, s):
+    seg, seqs, _ = s.cot.shape
+    begin = (me.dp * me.lanes + me.mp) * seg
+    position = begin + lax.broadcasted_iota(jnp.int32, (1, seg), 1)
+    for q in range(seqs):
+        weight = jnp.where(position < s.lengths[q], 0.5 + s.starts[q : q + 1, :].astype(F32), 0.0)
+        for p in range(seg):
+            s.tgrad[p * seqs + q : p * seqs + q + 1, :] = weight[:, p : p + 1] * s.cot[p, q : q + 1, :].astype(F32)
+
+
+def forward_layer(net, me, l, s, loads, arrived):
     own_rows = s.x.shape[1]
     rows = s.dt.shape[1]
     seqs = s.seqs
@@ -475,6 +520,8 @@
     s.hn[l, pl.ds(at, own_rows), :] = hn
     edge_slot = net.slots(me.lanes)
     last = me.mp == me.lanes - 1
+    if l == 0:
+        arrived()
 
     def edge(t):
         src = s.hn.at[l, pl.ds(rows, EDGE)]
@@ -489,7 +536,9 @@
     def _():
         s.hn[l, 0:EDGE, :] = jnp.zeros((EDGE, s.hn.shape[2]), BF16)
 
-    gather_rows(net, me, s.hn.at[l], EDGE, own_rows)()
+    gathered = gather_rows(net, me, s.hn.at[l], EDGE, own_rows)
+    loads["win", l].wait()
+    gathered()
 
     @pl.when(me.dp > 0)
     def _():
@@ -503,8 +552,6 @@
     def _():
         for t in range(me.lanes):
             edge(t).wait_send()
-
-    s.pending[l] = [start(net.copy(s.hn.at[l, pl.ds(EDGE, rows)], s.hnt.at[l], me.at(dp=me.twin), net.slots()))]
 
     s.xi[l] = dot(s.hn[l], s.win[l, 0], 1, 0).astype(BF16).astype(F32)
     conv = s.cb[l : l + 1, :]
@@ -516,10 +563,15 @@
     s.u[l] = u
 
     p = 2 * l
+    loads["stt", l].wait()
     s.xd[p] = dot(s.stt[l], u, 1, 1)
-    second = sum_lanes(net, me, s.xd.at[p], s.xd1.at[p], s.xd2.at[p])
+    second = sum_lanes(net, me, s.xd.at[p], s.xd1.at[p], s.xdf, s.xd2.at[p])
     s.z[l] = dot(s.hn[l, EDGE : EDGE + rows, :], s.win[l, 1], 1, 0)
-    xd = second()()
+    finish = second()
+    if l == 0:
+        first_gradient(me, s)
+    loads["stp", l].wait()
+    xd = finish()
     s.dtr[l] = xd[:rank].astype(BF16)
     spread(s.bg.at[l], xd[rank : rank + states])
     spread(s.cg.at[l], xd[rank + states :])
@@ -539,9 +591,11 @@
     zero = jnp.zeros_like(a2)
     own = totals_scan(s.dt.at[l], s.du, s.bg.at[l], a2, (zero,) * seqs)
     shared()
-    first = entering_state(
+    finish = entering_state(
         net, me, own, s.sums.at[l], a2, s.st1, s.got1.at[p], s.st2, s.got2.at[p], True
-    )()()
+    )()
+    s.pending[l] = [start(net.copy(s.hn.at[l, pl.ds(EDGE, rows)], s.hnt.at[l], me.at(dp=me.twin), net.slots()))]
+    first = finish()
     for q in range(seqs):
         s.h[l, q] = first[q].astype(s.h.dtype)
     output_scan(
@@ -553,6 +607,7 @@
     z = s.z[l]
     s.go[l] = (ys * z * jax.nn.sigmoid(z)).astype(BF16)
     s.pending[l].append(start(net.copy(s.go.at[l], s.got.at[l], me.at(dp=me.twin), net.slots())))
+    loads["wout", l].wait()
     s.part[...] = dot(s.go[l], s.wout[l], 1, 0)
     total = scatter_sum(net, me, s.part, own_rows, s.rs1, s.rs2.at[p], s.rs3, s.rs4.at[p])()()
     s.x[l + 1] = s.x[l] + total
@@ -564,7 +619,7 @@
 
 def chunk_table(width, chans, blocks, small):
     wide = chans // 2
-    half = max(512, 8 * blocks)
+    half = max(HALF, 8 * blocks)
     table, base = [], 0
     for kind, rows, places in (("out", chans, width // chans), ("gate", width, 1), ("conv", width, 1), ("small", small, 1)):
         step = min(half, rows)
@@ -612,19 +667,21 @@
         slot = net.slots()
         s.smalls[...] = s.small[1 - me.inner].astype(BF16)
         pair = start(net.copy(s.smalls, s.smallr.at[l], me.at(dp=me.twin), slot))
-        yield transfer(0, s.smalls)
+        yield True
         pair.wait()
         gm[...] = s.small[me.inner] + s.smallr[l].astype(F32)
 
     made = {"out": [], "gate": [], "conv": [], "small": []}
-    for i, (kind, first, place, base, half) in enumerate(table):
+    for i, (kind, begin, place, base, half) in enumerate(table):
         fill = {
-            "out": lambda: out_fill(first, place, half),
-            "gate": lambda: in_fill(first, half, s.dzh, s.dzr.at[l]),
-            "conv": lambda: in_fill(first, half, s.dxh, s.dxr.at[l]),
+            "out": lambda: out_fill(begin, place, half),
+            "gate": lambda: in_fill(begin, half, s.dzh, s.dzr.at[l]),
+            "conv": lambda: in_fill(begin, half, s.dxh, s.dxr.at[l]),
             "small": lambda: small_fill,
         }[kind]()
-        made[kind].append(reduce_chunk(net, me, s.local.at[l, i], s.gout.at[l], base, half, fill, bufs(base, half)))
+        first = [transfer(0, half * wide)] if kind == "small" else []
+        chunk = reduce_chunk(net, me, s.local.at[l, i], s.gout.at[l], base, half, fill, bufs(base, half))
+        made[kind].append((chunk, chunk_plan(levels, half * wide, first)))
     return made["out"], made["gate"], made["conv"], made["small"]
 
 
@@ -656,7 +713,6 @@
     s.dz[...] = dz
     for i in range(2):
         s.dzh[i] = dz[:, i * chans // 2 : (i + 1) * chans // 2]
-    dz_sent = start(net.copy(s.dzh.at[1 - me.inner], s.dzr.at[l], me.at(dp=me.twin), net.slots()))
     pump.spend(1.5)
 
     s.du[...] = s.dt[l] * s.u[l].astype(F32)
@@ -667,6 +723,7 @@
     second = entering_state(
         net, me, own, s.sums.at[l], a2, s.st1, s.got1.at[p], s.st2, s.got2.at[p], False
     )
+    dz_sent = start(net.copy(s.dzh.at[1 - me.inner], s.dzr.at[l], me.at(dp=me.twin), net.slots()))
     pump.spend(2.8)
     hn_sent, go_sent = s.pending[l]
     do_sent.wait()
@@ -693,7 +750,7 @@
     dpre = ((s.s1[...] + s.s2[...] * u) * softplus_slope(s.dt[l])).astype(BF16)
     s.s2[...] = s.s2[...] * s.dt[l] + s.skip[l : l + 1, :] * s.dy[...]
     s.xd[p, 0:rank, :] = dot(s.stp[l], dpre, 1, 1)
-    second = sum_lanes(net, me, s.xd.at[p], s.xd1.at[p], s.xd2.at[p])
+    second = sum_lanes(net, me, s.xd.at[p], s.xd1.at[p], s.xdf, s.xd2.at[p])
     xw = s.xd.shape[1]
     v0 = xw + rank + states
 
@@ -762,9 +819,8 @@
     g0 = v0 + 8
     wide = chans // 2
     count = x.shape[1] // wide
-    s.gg[l] = jnp.zeros_like(s.gg[l])
     for j in range(count):
-        s.gg[l, j : j + 1, :] = part[:, j * wide : (j + 1) * wide]
+        s.gg[l * count + j : l * count + j + 1, :] = part[:, j * wide : (j + 1) * wide]
     dr = dhn * s.gain[l : l + 1, :]
     s.tgrad[...] = s.tgrad[...] + inv * dr - x * (inv * inv * inv) * jnp.mean(dr * x, axis=-1, keepdims=True)
 
@@ -772,15 +828,21 @@
     def _():
         edge.wait_send()
 
-    second = sum_lanes(net, me, s.gg.at[l], s.gg1.at[l], s.gg2.at[l])
-    pump.spend(2)
+    for i in range(2):
+        s.small[i, v0 + taps + 3 :, :] = jnp.zeros((s.small.shape[1] - v0 - taps - 3, wide), F32)
+    if l > 0:
+        pump.add(small)
+        return
+    second = sum_lanes(net, me, s.gg, s.gg1, s.ggf, s.gg2)
+    pump.spend(1.5)
     finish = second()
-    pump.spend(2)
+    pump.spend(2.5)
     total = finish()
-    for i in range(2):
-        s.small[i, g0 : g0 + count // 2, :] = total[i * count // 2 : (i + 1) * count // 2]
-        s.small[i, g0 + count // 2 :, :] = jnp.zeros((s.small.shape[1] - g0 - count // 2, wide), F32)
-        s.small[i, v0 + taps + 3 : g0, :] = jnp.zeros((g0 - v0 - taps - 3, wide), F32)
+    layers = s.gain.shape[0]
+    for k in range(layers):
+        for i in range(2):
+            at, of = g0 + k * (count // 2), k * count + i * (count // 2)
+            s.small[i, at : at + count // 2, :] = total[of : of + count // 2]
     pump.add(small)
 
 
@@ -795,20 +857,22 @@
     s.seqs, s.pending = seqs, {}
     me = Place(blocks, lanes)
     net = Net(s.send, s.recv)
-    entry_barrier(me)
+    arrived = entry_barrier(me)
+    loads = load_weights(s)
+    seg = s.tok.shape[0]
+    for p in range(seg):
+        s.x[0, p * seqs : (p + 1) * seqs, :] = s.tok[p].astype(F32)
     layers = s.gain.shape[0]
-    s.x[0] = s.tok[...].astype(F32)
     for l in range(layers):
-        forward_layer(net, me, l, s)
+        forward_layer(net, me, l, s, loads, arrived)
     s.lout[...] = s.x[layers].astype(s.lout.dtype)
-    s.tgrad[...] = s.g0[...]
     pump = Pump()
     for l in reversed(range(layers)):
         backward_layer(net, me, l, s, pump)
     pump.drain()
 
 
-def layers_call(mesh, tokens, grad, gain, win, ck, cb, stt, stp, sb, dlog, skip, wout):
+def layers_call(mesh, tokens, cotangent, starts, lengths, gain, win, ck, cb, stt, stp, sb, dlog, skip, wout):
     blocks, lanes = mesh.shape["dp"], mesh.shape["mp"]
     seg, seqs, width = tokens.shape
     own_rows = seg * seqs
@@ -825,7 +889,7 @@
     slots = layers * (3 * 2 + 2 * 3 + 3 * 2 + lanes + blocks + 2 * (1 + outers) + 1)
     slots += layers * (chunks * 2 * levels + 6)
     two = 2 * layers
-    ins = ["tok", "g0", "gain", "win", "ck", "cb", "stt", "stp", "sb", "dlog", "skip", "wout"]
+    ins = ["tok", "cot", "starts", "lengths", "gain", "win_hbm", "ck", "cb", "stt_hbm", "stp_hbm", "sb", "dlog", "skip", "wout_hbm"]
     outs = {
         "lout": ((own_rows, width), BF16),
         "tgrad": ((own_rows, width), F32),
@@ -833,6 +897,10 @@
     }
     half = grads // 2
     scratch = {
+        "win": (win.shape, BF16),
+        "stt": (stt.shape, BF16),
+        "stp": (stp.shape, BF16),
+        "wout": (wout.shape, BF16),
         "x": ((layers + 1, own_rows, width), F32),
         "hn": ((layers, EDGE + rows, width), BF16),
         "xi": ((layers, EDGE + rows, chans), F32),
@@ -864,7 +932,8 @@
         "rs4": ((two, own_rows, width), BF16),
         "xd": ((two, xw, rows), F32),
         "xd1": ((two, xw, rows), F32),
-        "xd2": ((two, xw, rows), F32),
+        "xdf": ((xw, rows), BF16),
+        "xd2": ((two, xw, rows), BF16),
         "sums": ((layers, blocks, seqs * chans // 128, 128), F32),
         "st1": ((seqs, states, chans), BF16),
         "got1": ((two, seqs, states, chans), BF16),
@@ -873,9 +942,10 @@
         "small": ((2, small, wide), F32),
         "smalls": ((small, wide), BF16),
         "smallr": ((layers, small, wide), BF16),
-        "gg": ((layers, 8, wide), F32),
-        "gg1": ((layers, 8, wide), F32),
-        "gg2": ((layers, 8, wide), F32),
+        "gg": ((layers * width // wide, wide), F32),
+        "gg1": ((layers * width // wide, wide), F32),
+        "ggf": ((layers * width // wide, wide), F32),
+        "gg2": ((layers * width // wide, wide), F32),
         "hnt": ((layers, rows, width), BF16),
         "got": ((layers, rows, chans), BF16),
         "dor": ((layers, rows, width // 2), BF16),
@@ -888,20 +958,20 @@
         "zr": ((layers, levels - 1, half // 2, wide), BF16),
         "sh": ((half // 2 ** (levels - 1), wide), BF16),
     }
-    names = ins + list(outs) + list(scratch) + ["local", "send", "recv"]
+    names = ins + list(outs) + list(scratch) + ["loaded", "local", "send", "recv"]
     any_space = pl.BlockSpec(memory_space=pl.ANY)
-    vmem = pl.BlockSpec(memory_space=VMEM)
-    sems = [pltpu.SemaphoreType.DMA((layers, chunks)), pltpu.SemaphoreType.DMA((slots,)), pltpu.SemaphoreType.DMA((slots,))]
+    vmem, smem = pl.BlockSpec(memory_space=VMEM), pl.BlockSpec(memory_space=pltpu.SMEM)
+    sems = [pltpu.SemaphoreType.DMA((layers, 4)), pltpu.SemaphoreType.DMA((layers, chunks)), pltpu.SemaphoreType.DMA((slots,)), pltpu.SemaphoreType.DMA((slots,))]
     return pl.pallas_call(
         functools.partial(kernel, names, seqs, blocks, lanes),
         out_shape=[jax.ShapeDtypeStruct(a, t) for a, t in outs.values()],
-        in_specs=[vmem] * len(ins),
-        out_specs=[vmem, vmem, any_space],
+        in_specs=[any_space if n.endswith("_hbm") else smem if n == "lengths" else vmem for n in ins],
+        out_specs=[vmem, vmem, GSPACE[0] and vmem or any_space],
         scratch_shapes=[VMEM(a, t) for a, t in scratch.values()] + sems,
         compiler_params=pltpu.CompilerParams(
             collective_id=0, has_side_effects=True, vmem_limit_bytes=63 * 2**20
         ),
-    )(tokens.reshape(own_rows, width), grad, gain, win, ck, cb, stt, stp, sb, dlog, skip, wout)
+    )(tokens, cotangent, starts, lengths, gain, win, ck, cb, stt, stp, sb, dlog, skip, wout)
 
 
 def unpack_kernel(names, table, *refs):
@@ -912,15 +982,15 @@
     layers, chans = s.cb.shape
     width = s.gain.shape[1]
     wide = chans // 2
-    taps, xw, rank, states = s.ck.shape[1], s.sp.shape[2], s.stp.shape[1], s.dlog.shape[1]
+    taps, xw, rank, states = s.ck.shape[1], s.sp.shape[1], s.stp.shape[1], s.dlog.shape[1]
     v0 = xw + rank + states
+
+    fetch = [pltpu.make_async_copy(s.lo, s.lov, s.sem.at[0]), pltpu.make_async_copy(s.tg, s.tgv, s.sem.at[1])]
 
     @pl.when(l == 0)
     def _():
-        seg, seqs, _ = s.lout.shape
-        for p in range(seg):
-            s.lout[p] = s.lo[p * seqs : (p + 1) * seqs, :]
-            s.tgrad[p] = s.tg[p * seqs : (p + 1) * seqs, :]
+        for copy in fetch:
+            copy.start()
 
     row = lax.broadcasted_iota(jnp.int32, (layers, wide), 0) == l
 
@@ -935,16 +1005,31 @@
                 s.wout[0, first : first + half, at : at + wide] = block
             elif kind == "small":
                 cols = slice(i * wide, (i + 1) * wide)
-                s.sp[0, cols, :] = block[:xw].T
+                s.sp[0, :, cols] = block[:xw]
                 s.stp[0, :, cols] = block[xw : xw + rank]
                 s.dlog[0, :, cols] = block[xw + rank : v0]
                 s.ck[0, :, cols] = block[v0 : v0 + taps]
                 for j, ref in enumerate((s.cb, s.skip, s.sb)):
                     put(ref, i * wide, block[v0 + taps + j : v0 + taps + j + 1])
-                for j in range(width // chans):
-                    put(s.gain, i * (width // 2) + j * wide, block[v0 + 8 + j : v0 + 9 + j])
+                count = width // chans
+
+                @pl.when(l == 0)
+                def _():
+                    for k in range(layers):
+                        for j in range(count):
+                            at, of = i * (width // 2) + j * wide, v0 + 8 + k * count + j
+                            s.gain[k : k + 1, at : at + wide] = block[of : of + 1]
             else:
                 s.win[0, 0 if kind == "conv" else 1, first : first + half, i * wide : (i + 1) * wide] = block
+
+    @pl.when(l == 0)
+    def _():
+        seg, seqs, _ = s.lout.shape
+        for copy in fetch:
+            copy.wait()
+        for p in range(seg):
+            s.lout[p] = s.lov[p * seqs : (p + 1) * seqs, :]
+            s.tgrad[p] = s.tgv[p * seqs : (p + 1) * seqs, :]
 
 
 def unpack_call(table, lout, tgrad, gout, shape, gain, win, ck, sp, stp, dlog, wout):
@@ -952,7 +1037,7 @@
     ins = ["lo", "tg", "grads"]
     outs = {
         "lout": (shape, BF16), "tgrad": (shape, F32), "gain": (gain.shape, F32), "win": (win.shape, F32), "ck": (ck.shape, F32),
-        "cb": ((layers, chans), F32), "sp": (sp.shape, F32), "stp": (stp.shape, F32), "sb": ((layers, chans), F32),
+        "cb": ((layers, chans), F32), "sp": ((layers, sp.shape[2], chans), F32), "stp": (stp.shape, F32), "sb": ((layers, chans), F32),
         "dlog": (dlog.shape, F32), "skip": ((layers, chans), F32), "wout": (wout.shape, F32),
     }
 
@@ -964,11 +1049,12 @@
 
     once = {"lout", "tgrad", "gain", "cb", "sb", "skip"}
     return pl.pallas_call(
-        functools.partial(unpack_kernel, ins + list(outs), table),
+        functools.partial(unpack_kernel, ins + list(outs) + ["lov", "tgv", "sem"], table),
         grid=(layers,),
         out_shape=[jax.ShapeDtypeStruct(a, t) for a, t in outs.values()],
-        in_specs=[whole(lout.shape), whole(tgrad.shape), layer(gout.shape)],
+        in_specs=[pl.BlockSpec(memory_space=pl.ANY), pl.BlockSpec(memory_space=pl.ANY), layer(gout.shape)],
         out_specs=[whole(a) if name in once else layer(a) for name, (a, _) in outs.items()],
+        scratch_shapes=[VMEM(lout.shape, BF16), VMEM(tgrad.shape, F32), pltpu.SemaphoreType.DMA((2,))],
         compiler_params=pltpu.CompilerParams(vmem_limit_bytes=50 * 2**20),
     )(lout, tgrad, gout)
 
@@ -990,20 +1076,18 @@
     skip_gain,
     output_proj,
 ):
-    seg, seqs, width = tokens.shape
-    position = lax.axis_index(("dp", "mp")) * seg + lax.broadcasted_iota(jnp.int32, (seg, seqs), 0)
-    weight = jnp.where(position < lengths[None, :], 0.5 + char_start.astype(F32), 0.0)
-    grad = (cotangent.astype(F32) * weight[:, :, None]).reshape(seg * seqs, width)
+    width = tokens.shape[2]
     lout, tgrad, gout = layers_call(
-        mesh, tokens, grad, norm_gain, input_proj, conv_kernel, conv_bias,
+        mesh, tokens, cotangent, char_start.T, lengths, norm_gain, input_proj, conv_kernel, conv_bias,
         state_proj.transpose(0, 2, 1), step_proj, step_bias, decay_log, skip_gain, output_proj,
     )
-    layers, chans = skip_gain.shape
-    xw, rank, states, taps = state_proj.shape[2], step_proj.shape[1], decay_log.shape[1], conv_kernel.shape[1]
     xw, rank, states = state_proj.shape[2], step_proj.shape[1], decay_log.shape[1]
     blocks = mesh.shape["dp"]
     table, _ = chunk_table(width, skip_gain.shape[1], blocks, small_rows(xw + rank + states, blocks))
-    return unpack_call(table, lout, tgrad, gout, tokens.shape, norm_gain, input_proj, conv_kernel, state_proj, step_proj, decay_log, output_proj)
+    outs = unpack_call(table, lout, tgrad, gout, tokens.shape, norm_gain, input_proj, conv_kernel, state_proj, step_proj, decay_log, output_proj)
+    outs = list(outs)
+    outs[6] = outs[6].transpose(0, 2, 1)
+    return tuple(outs)
 
 
 def solution(mesh):

time: 268 us -> 243 us (0.907)
  Pallas kernels: 260 us -> 240 us
  local copies, waits for them, and re-layouts: 5.37 us -> 1.85 us
    pallas_call x1, Pallas kernels: 253 us -> 232 us  [layers_call(): pl.pallas_call(functools.partial(kernel, names, seqs, blocks, lanes), out...]
where the time goes in v3:
time: 243 us; the launch traced here: 242 us
  Pallas kernels  240 us (99%)
    pallas_call x1, Pallas kernels, layers_call(): pl.pallas_call(functools.partial(kernel, names, seqs, blocks, lanes), out...  232 us
    pallas_call x1, Pallas kernels, unpack_call(): pl.pallas_call(functools.partial(unpack_kernel, ins + list(outs) + ['lov'...  7.68 us

profile of v3, /device:TPU:0, one launch (start us, length us, event | category | flops | bytes accessed | tf_op | source)
XLA Modules:
  0.0 242.5 jit_solution(5899447480833569263)
XLA Ops:
  0.6 232.1 %shard_map.229 = (bf16[64,1024]{1,0:T(8,128)(2,1)}, f32[64,1024]{1,0:T(8,128)}, bf16[2,6528,256]{2,1,0:T(8,128)(2,1)}) custom-call(bf16[32,2,1024]{2,1,0:T(2,128)(2,1)} %refs_0_.1, bf16[32,2,1024]{2,1,0:T(2,128)(2,1)} %refs_1_.1, s32[2,32]{1,0:T(2,128)} %bitcast.4, s32[2]{0:T(128)} %refs_3_.1, f32[2,1024]{1,0:T(2,128)} %refs_4_.1, ...), custom_call_target="tpu_custom_call" | custom-call | tf_op jit(solution)/shard_map/pallas_call | solution.py:965
  232.8 0.0 copy-start
  232.8 0.9 copy-done
  233.7 0.0 copy-start.1
  233.7 0.9 copy-done.1
  234.6 7.7 %shard_map.230 = (bf16[32,2,1024]{2,1,0:T(2,128)(2,1)}, f32[32,2,1024]{2,1,0:T(2,128)}, f32[2,1024]{1,0:T(2,128)}, f32[2,2,1024,512]{3,2,1,0:T(8,128)}, f32[2,4,...) custom-call(bf16[64,1024]{1,0:T(8,128)(2,1)S(1)} %copy-done.1, ...), custom_call_target="tpu_custom_call" | custom-call | tf_op jit(solution)/shard_map/pallas_call | solution.py:1051
Async XLA Ops:
  232.8 1.0 copy-start
  233.7 0.9 copy-start.1

commit v4 on v3

--- a/solution.py
+++ b/solution.py
@@ -228,16 +228,20 @@
     mine = block(me.mp)
     far = start(net.copy(mine, mine, me.at(mp=me.chip), slot))
     near = start(net.copy(mine, mine, me.at(mp=me.core), slot + 1))
-    far.wait_recv()
-    theirs = block(me.chip)
-    passed = start(net.copy(theirs, theirs, me.at(mp=me.core), slot + 2))
-
-    def finish():
-        near.wait()
-        passed.wait()
-        far.wait_send()
-
-    return finish
+
+    def second():
+        far.wait_recv()
+        theirs = block(me.chip)
+        passed = start(net.copy(theirs, theirs, me.at(mp=me.core), slot + 2))
+
+        def finish():
+            near.wait()
+            passed.wait()
+            far.wait_send()
+
+        return finish
+
+    return second
 
 
 def sum_lanes(net, me, own, got1, far, got2):
@@ -304,41 +308,34 @@
     return finish
 
 
-def entering_state(net, me, own, sums, a2, send1, got1, send2, got2, forward):
-    seqs = len(own)
+def entering_state(net, me, own, sums, q, a2, send1, got1, send2, got2, forward):
     slot = net.slots(1 + me.outers)
     early = 0 if forward else 1
     am_early = me.inner == early
-
-    def decay(dp, s):
+    width = a2.shape[1] // 128
+
+    def total(dp):
         tile = sums[dp]
-        width = a2.shape[1] // 128
-        row = jnp.concatenate([tile[s * width + j : s * width + j + 1, :] for j in range(width)], axis=1)
-        return row
-
-    for s in range(seqs):
-        send1[s] = own[s].astype(send1.dtype)
+        return jnp.concatenate([tile[q * width + j : q * width + j + 1, :] for j in range(width)], axis=1)
+
+    send1[...] = own.astype(send1.dtype)
     pair = start(net.copy(send1, got1, me.at(dp=me.twin), slot))
 
     def to(k):
         return me.outer + k if forward else me.outer - k
 
     def copy(k):
-        dp = to(k) * 2 + me.inner
-        return net.copy(send2, got2.at[me.outer], me.at(dp=dp), slot + k)
+        return net.copy(send2, got2.at[me.outer], me.at(dp=to(k) * 2 + me.inner), slot + k)
 
     def reaches(k):
         return (to(k) < me.outers) if forward else (to(k) >= 0)
 
     def second():
         pair.wait()
-        late_block = me.outer * 2 + 1 - early
-        for s in range(seqs):
-            theirs = got1[s].astype(F32)
-            mine = own[s]
-            first = jnp.where(am_early, mine, theirs)
-            last = jnp.where(am_early, theirs, mine)
-            send2[s] = (last + jnp.exp2(a2 * decay(late_block, s)) * first).astype(send2.dtype)
+        theirs = got1[...].astype(F32)
+        first = jnp.where(am_early, own, theirs)
+        last = jnp.where(am_early, theirs, own)
+        send2[...] = (last + jnp.exp2(a2 * total(me.outer * 2 + 1 - early)) * first).astype(send2.dtype)
 
         def send(k):
             @pl.when(reaches(k))
@@ -354,14 +351,11 @@
                 source = i if forward else me.outers - 1 - i
                 away = me.outer - source if forward else source - me.outer
                 net.copy(send2, got2.at[source], me.at(dp=me.twin), slot + away).wait_recv()
-                both = [decay(2 * source, s) + decay(2 * source + 1, s) for s in range(seqs)]
-                return tuple(got2[source, s].astype(F32) + jnp.exp2(a2 * both[s]) * state[s] for s in range(seqs))
-
-            state = lax.fori_loop(0, count, add, tuple(jnp.zeros_like(own[s]) for s in range(seqs)))
-            result = []
-            for s in range(seqs):
-                after = got1[s].astype(F32) + jnp.exp2(a2 * decay(me.twin, s)) * state[s]
-                result.append(jnp.where(am_early, state[s], after))
+                both = total(2 * source) + total(2 * source + 1)
+                return got2[source].astype(F32) + jnp.exp2(a2 * both) * state
+
+            state = lax.fori_loop(0, count, add, jnp.zeros_like(own))
+            after = got1[...].astype(F32) + jnp.exp2(a2 * total(me.twin)) * state
 
             def sent(k):
                 @pl.when(reaches(k))
@@ -369,7 +363,7 @@
                     copy(k).wait_send()
 
             others(me.outers, sent)
-            return tuple(result)
+            return jnp.where(am_early, state, after)
 
         return finish
 
@@ -380,10 +374,16 @@
     latency, cost, early, scale = 2.0, 0.3, 1.0, 1.0
 
     def __init__(self):
-        self.now, self.free, self.active = 0.0, {}, []
+        self.now, self.free, self.active, self.quiet = 0.0, {}, [], False
 
     def add(self, chunks):
-        self.active += [[gen, self.now, list(plan)] for gen, plan in chunks]
+        for gen, plan, key in chunks:
+            for old in [e for e in self.active if e[3] == key]:
+                while old in self.active:
+                    self.step(old)
+            entry = [gen, self.now, list(plan), key]
+            self.active.append(entry)
+            self.step(entry)
         self.poll()
 
     def when(self, entry):
@@ -395,7 +395,7 @@
         self.poll()
 
     def poll(self):
-        while True:
+        while not self.quiet:
             ready = [e for e in self.active if self.when(e) <= self.now]
             if not ready:
                 return
@@ -420,20 +420,86 @@
             self.step(entry)
 
 
-def transfer(bit, values):
-    us = 2e-5 * values * 2
-    if bit == 0:
-        return [("x", us)]
-    return [("z", us)] if bit == 1 else [("z", us), ("middle", us * bit)]
+def transfer(link, values):
+    return [(link, 2e-5 * values * 2)]
+
+
+def chunk_plan(levels, values, first):
+    up = [transfer("out", values * 3 // 4), transfer("mid", values // 2), transfer("in", values // 4)]
+    down = [transfer("out", values // 4), transfer("mid", values // 2), transfer("in", values * 3 // 4)]
+    more = [transfer("far", values >> b) for b in range(3, levels)]
+    return first + [[]] + up + more + more[::-1] + down + [transfer("x", values)]
 
 
 def reduce_chunk(net, me, local, out, row, half, fill, bufs):
-    gm, sends, gots, sh = bufs
-    levels = len(sends) + 1
-    slot = net.slots(2 * levels)
+    gm, zs, zr, sh = bufs
+    levels = me.blocks.bit_length() - 1
+    slot = net.slots(7 + 2 * (levels - 3))
     yield from fill(gm)
     yield True
-    off, size = 0, half
+
+    q = (me.dp // 2) % 4
+    is_end = (q == 0) | (q == 3)
+    is_inner = (q == 1) | (q == 2)
+    left = q < 2
+    near = me.at(dp=me.dp + (1 - 2 * (q % 2)) * 2)
+    across = me.at(dp=me.dp + (3 - 2 * q) * 2)
+    piece = half // 4
+
+    def rows(ref, first, count):
+        return ref.at[pl.ds(pl.multiple_of(first, 16), count)]
+
+    def either(a, b):
+        return jnp.where(left, a * piece, b * piece)
+
+    def narrow(at, first, count):
+        rows(zs, at * piece, count * piece)[...] = rows(gm, first, count * piece)[...].astype(BF16)
+
+    def widen(first, at, count):
+        mine = rows(gm, first, count * piece)
+        mine[...] = mine[...] + rows(zr, at * piece, count * piece)[...].astype(F32)
+
+    def sent(i, at, to, count, device):
+        return net.copy(rows(zs, at * piece, count * piece), rows(zr, to * piece, count * piece), device, slot + i)
+
+    up = [sent(0, 0, 0, 3, near), sent(1, 0, 3, 2, across), sent(2, 2, 0, 1, near)]
+
+    @pl.when(is_end)
+    def _():
+        narrow(0, either(1, 0), 3)
+        up[0].start()
+
+    yield True
+
+    @pl.when(is_inner)
+    def _():
+        up[0].wait_recv()
+        widen(either(1, 0), 0, 3)
+        narrow(0, either(2, 0), 2)
+        up[1].start()
+
+    yield True
+
+    @pl.when(is_inner)
+    def _():
+        up[1].wait()
+        widen(either(0, 2), 3, 2)
+        narrow(2, either(0, 3), 1)
+        up[2].start()
+
+    yield True
+
+    @pl.when(is_end)
+    def _():
+        up[0].wait_send()
+        up[2].wait_recv()
+        widen(q * piece, 0, 1)
+
+    @pl.when(is_inner)
+    def _():
+        up[2].wait_send()
+
+    off, size = q * piece, piece
 
     def bit_of(b):
         return (me.dp // 2**b) % 2
@@ -441,43 +507,78 @@
     def peer(b):
         return me.at(dp=me.dp + (1 - 2 * bit_of(b)) * 2**b)
 
-    def part(ref, first, count):
-        return ref.at[pl.ds(pl.multiple_of(first, 16), count)]
-
-    for b in range(1, levels):
+    used = 5 * piece
+    for b in range(3, levels):
         size //= 2
-        sends[b - 1][...] = part(gm, off + (1 - bit_of(b)) * size, size)[...].astype(BF16)
-        copy = start(net.copy(sends[b - 1], gots[b - 1], peer(b), slot + b))
+        mine = rows(zs, 0, size)
+        got = rows(zr, used, size)
+        mine[...] = rows(gm, off + (1 - bit_of(b)) * size, size)[...].astype(BF16)
+        copy = start(net.copy(mine, got, peer(b), slot + 4 + b))
         yield True
         copy.wait()
         off = off + bit_of(b) * size
-        mine = part(gm, off, size)
-        mine[...] = mine[...] + gots[b - 1][...].astype(F32)
-    sh[...] = part(gm, off, size)[...].astype(BF16)
+        total = rows(gm, off, size)
+        total[...] = total[...] + got[...].astype(F32)
+        used += size
+    sh[...] = rows(gm, off, size)[...].astype(BF16)
     base = row + me.inner * half
-    held = part(out, base + off, size)
+    held = rows(out, base + off, size)
     keep = pltpu.make_async_copy(sh, held, local)
     keep.start()
-    source = sh
-    for b in reversed(range(levels)):
-        copy = start(net.copy(source, held, peer(b), slot + levels + b))
+    if levels > 3:
+        keep.wait()
+    for b in reversed(range(3, levels)):
+        copy = start(net.copy(held, held, peer(b), slot + levels + 1 + b))
         yield True
         copy.wait()
-        if b == levels - 1:
+        off = off - bit_of(b) * size
+        size *= 2
+        held = rows(out, base + off, size)
+
+    def shared(i, first, count, device):
+        place = rows(out, base + first, count * piece)
+        return net.copy(place, place, device, slot + i)
+
+    source = sh if levels == 3 else held
+    own = rows(out, base + q * piece, piece)
+    down = [net.copy(source, own, near, slot + 3), shared(4, either(0, 2), 2, across), shared(5, either(1, 0), 3, near)]
+
+    @pl.when(is_end)
+    def _():
+        down[0].start()
+
+    yield True
+
+    @pl.when(is_inner)
+    def _():
+        down[0].wait_recv()
+        if levels == 3:
             keep.wait()
-        if b > 0:
-            off = off - bit_of(b) * size
-            size *= 2
-            source = held = part(out, base + off, size)
-
-
-def chunk_plan(levels, values, first):
-    plan = first + [[]]
-    for b in range(1, levels):
-        plan.append(transfer(b, values >> b))
-    for b in reversed(range(levels)):
-        plan.append(transfer(b, values >> b))
-    return plan
+        down[1].start()
+
+    yield True
+
+    @pl.when(is_inner)
+    def _():
+        down[1].wait()
+        down[2].start()
+
+    yield True
+
+    @pl.when(is_end)
+    def _():
+        if levels == 3:
+            keep.wait()
+        down[0].wait_send()
+        down[2].wait_recv()
+
+    @pl.when(is_inner)
+    def _():
+        down[2].wait_send()
+
+    copy = start(shared(6, 0, 4, me.at(dp=me.twin)))
+    yield True
+    copy.wait()
 
 
 def rms(x):
@@ -487,63 +588,69 @@
 def load_weights(s):
     layers = s.gain.shape[0]
     copies = {}
-    names = ["win", "stt", "stp", "wout"]
     for l in range(layers):
-        for i, name in enumerate(names):
+        for i, name in enumerate(["win", "stt", "stp", "wout"]):
             hbm, vmem = getattr(s, name + "_hbm"), getattr(s, name)
             copies[name, l] = start(pltpu.make_async_copy(hbm.at[l], vmem.at[l], s.loaded.at[l, i]))
-    return copies
-
-
-def first_gradient(me, s):
+
+    def wait(name, l):
+        copy = copies.pop((name, l), None)
+        if copy is not None:
+            copy.wait()
+
+    return wait
+
+
+def first_gradient(me, s, q):
     seg, seqs, _ = s.cot.shape
     begin = (me.dp * me.lanes + me.mp) * seg
     position = begin + lax.broadcasted_iota(jnp.int32, (1, seg), 1)
-    for q in range(seqs):
-        weight = jnp.where(position < s.lengths[q], 0.5 + s.starts[q : q + 1, :].astype(F32), 0.0)
-        for p in range(seg):
-            s.tgrad[p * seqs + q : p * seqs + q + 1, :] = weight[:, p : p + 1] * s.cot[p, q : q + 1, :].astype(F32)
-
-
-def forward_layer(net, me, l, s, loads, arrived):
-    own_rows = s.x.shape[1]
-    rows = s.dt.shape[1]
-    seqs = s.seqs
+    weight = jnp.where(position < s.lengths[q], 0.5 + s.starts[q : q + 1, :].astype(F32), 0.0)
+    for p in range(seg):
+        s.tgrad[q * seg + p : q * seg + p + 1, :] = weight[:, p : p + 1] * s.cot[p, q : q + 1, :].astype(F32)
+
+
+def forward_layer(net, me, l, q, s, loads, arrived):
+    own_rows = s.x.shape[2]
+    rows = own_rows * me.lanes
     chans = s.dt.shape[2]
     states = s.dlog.shape[1]
     rank = s.stp.shape[1]
     taps = s.ck.shape[1]
-
-    x = s.x[l]
+    part = pl.ds(q * rows, rows)
+    block = slice(q * rows, (q + 1) * rows)
+
+    x = s.x[l, q]
     hn = (x * rms(x) * s.gain[l : l + 1, :]).astype(BF16)
-    at = pl.multiple_of(EDGE + me.mp * own_rows, 16)
-    s.hn[l, pl.ds(at, own_rows), :] = hn
+    s.hn[l, q, pl.ds(pl.multiple_of(EDGE + me.mp * own_rows, 16), own_rows), :] = hn
     edge_slot = net.slots(me.lanes)
     last = me.mp == me.lanes - 1
-    if l == 0:
-        arrived()
-
-    def edge(t):
-        src = s.hn.at[l, pl.ds(rows, EDGE)]
-        return net.copy(src, s.hn.at[l, pl.ds(0, EDGE)], me.at(dp=me.dp + 1, mp=t), edge_slot + t)
+    arrived()
+
+    def edge(t, dp):
+        src = s.hn.at[l, q, pl.ds(rows, EDGE)]
+        return net.copy(src, s.hn.at[l, q, pl.ds(0, EDGE)], me.at(dp=dp, mp=t), edge_slot + t)
 
     @pl.when(last & (me.dp < me.blocks - 1))
     def _():
         for t in range(me.lanes):
-            edge(t).start()
+            edge(t, me.dp + 1).start()
 
     @pl.when(me.dp == 0)
     def _():
-        s.hn[l, 0:EDGE, :] = jnp.zeros((EDGE, s.hn.shape[2]), BF16)
-
-    gathered = gather_rows(net, me, s.hn.at[l], EDGE, own_rows)
-    loads["win", l].wait()
-    gathered()
+        s.hn[l, q, 0:EDGE, :] = jnp.zeros((EDGE, s.hn.shape[3]), BF16)
+
+    second = gather_rows(net, me, s.hn.at[l, q], EDGE, own_rows)
+    yield
+    finish = second()
+    yield
+    loads("win", l)
+    finish()
 
     @pl.when(me.dp > 0)
     def _():
         pltpu.make_async_remote_copy(
-            src_ref=s.hn.at[l, pl.ds(rows, EDGE)], dst_ref=s.hn.at[l, pl.ds(0, EDGE)],
+            src_ref=s.hn.at[l, q, pl.ds(rows, EDGE)], dst_ref=s.hn.at[l, q, pl.ds(0, EDGE)],
             send_sem=net.send.at[edge_slot], recv_sem=net.recv.at[edge_slot + me.mp],
             device_id=me.at(dp=me.twin), device_id_type=MESH,
         ).wait_recv()
@@ -551,66 +658,70 @@
     @pl.when(last & (me.dp < me.blocks - 1))
     def _():
         for t in range(me.lanes):
-            edge(t).wait_send()
-
-    s.xi[l] = dot(s.hn[l], s.win[l, 0], 1, 0).astype(BF16).astype(F32)
+            edge(t, me.dp + 1).wait_send()
+
+    s.xi[l, q] = dot(s.hn[l, q], s.win[l, 0], 1, 0).astype(BF16).astype(F32)
     conv = s.cb[l : l + 1, :]
     for k in range(taps):
-        off = EDGE - seqs * (taps - 1 - k)
-        conv = conv + s.xi[l, off : off + rows, :] * s.ck[l, k : k + 1, :].astype(F32)
-    s.xc[l] = conv
+        off = EDGE - (taps - 1 - k)
+        conv = conv + s.xi[l, q, off : off + rows, :] * s.ck[l, k : k + 1, :].astype(F32)
+    s.xc[l, part] = conv
     u = (conv * jax.nn.sigmoid(conv)).astype(BF16)
-    s.u[l] = u
+    s.u[l, part] = u
 
     p = 2 * l
-    loads["stt", l].wait()
-    s.xd[p] = dot(s.stt[l], u, 1, 1)
-    second = sum_lanes(net, me, s.xd.at[p], s.xd1.at[p], s.xdf, s.xd2.at[p])
-    s.z[l] = dot(s.hn[l, EDGE : EDGE + rows, :], s.win[l, 1], 1, 0)
+    loads("stt", l)
+    s.xd[p, q] = dot(s.stt[l], u, 1, 1)
+    second = sum_lanes(net, me, s.xd.at[p, q], s.xd1.at[p, q], s.xdf.at[q], s.xd2.at[p, q])
+    s.z[l, part] = dot(s.hn[l, q, EDGE:, :], s.win[l, 1], 1, 0)
+    yield
     finish = second()
     if l == 0:
-        first_gradient(me, s)
-    loads["stp", l].wait()
+        first_gradient(me, s, q)
+    yield
+    loads("stp", l)
     xd = finish()
-    s.dtr[l] = xd[:rank].astype(BF16)
-    spread(s.bg.at[l], xd[rank : rank + states])
-    spread(s.cg.at[l], xd[rank + states :])
-    pre = dot(s.dtr[l], s.stp[l], 0, 0) + s.sb[l : l + 1, :]
-    dt = softplus(pre)
-    s.dt[l] = dt
-    s.du[...] = dt * s.u[l].astype(F32)
-
-    odd = lax.broadcasted_iota(jnp.int32, (rows, 1), 0) % seqs
-    for q in range(seqs):
-        total = jnp.sum(jnp.where(odd == q, dt, 0.0), axis=0, keepdims=True)
-        for j in range(chans // 128):
-            i = q * (chans // 128) + j
-            s.sums[l, me.dp, i : i + 1, :] = total[:, j * 128 : (j + 1) * 128]
-    shared = share_sums(net, me, s.sums.at[l])
+    s.dtr[l, q] = xd[:rank].astype(BF16)
+    spread(s.bg.at[l, q], xd[rank : rank + states])
+    spread(s.cg.at[l, q], xd[rank + states :])
+    dt = softplus(dot(s.dtr[l, q], s.stp[l], 0, 0) + s.sb[l : l + 1, :])
+    s.dt[l, part] = dt
+    s.du[part] = dt * s.u[l, part].astype(F32)
+
+    total = jnp.sum(dt, axis=0, keepdims=True)
+    for j in range(chans // 128):
+        i = q * (chans // 128) + j
+        s.sums[l, me.dp, i : i + 1, :] = total[:, j * 128 : (j + 1) * 128]
+    if q == s.seqs - 1:
+        s.shared[l] = share_sums(net, me, s.sums.at[l])
     a2 = -jnp.exp(s.dlog[l]) * LOG2E
-    zero = jnp.zeros_like(a2)
-    own = totals_scan(s.dt.at[l], s.du, s.bg.at[l], a2, (zero,) * seqs)
-    shared()
-    finish = entering_state(
-        net, me, own, s.sums.at[l], a2, s.st1, s.got1.at[p], s.st2, s.got2.at[p], True
-    )()
-    s.pending[l] = [start(net.copy(s.hn.at[l, pl.ds(EDGE, rows)], s.hnt.at[l], me.at(dp=me.twin), net.slots()))]
+    dt, du, bg, cg = s.dt.at[l, part], s.du.at[part], s.bg.at[l, q], s.cg.at[l, q]
+    own = totals_scan(dt, du, bg, a2, (jnp.zeros_like(a2),))[0]
+    second = entering_state(
+        net, me, own, s.sums.at[l], q, a2, s.st1.at[q], s.got1.at[p, q], s.st2.at[q], s.got2.at[p, q], True
+    )
+    yield
+    if q == 0:
+        s.shared[l]()
+    finish = second()
+    s.pending[l].append(start(net.copy(s.hn.at[l, q, pl.ds(EDGE, rows)], s.hnt.at[l, part], me.at(dp=me.twin), net.slots())))
+    yield
     first = finish()
-    for q in range(seqs):
-        s.h[l, q] = first[q].astype(s.h.dtype)
-    output_scan(
-        s.dt.at[l], s.du, s.bg.at[l], s.cg.at[l], a2, first, s.h.at[l, pl.ds(seqs, rows)], s.w1, s.ys.at[l]
-    )
-
-    ys = s.ys[l] + s.skip[l : l + 1, :] * s.u[l].astype(F32)
-    s.ys[l] = ys
-    z = s.z[l]
-    s.go[l] = (ys * z * jax.nn.sigmoid(z)).astype(BF16)
-    s.pending[l].append(start(net.copy(s.go.at[l], s.got.at[l], me.at(dp=me.twin), net.slots())))
-    loads["wout", l].wait()
-    s.part[...] = dot(s.go[l], s.wout[l], 1, 0)
-    total = scatter_sum(net, me, s.part, own_rows, s.rs1, s.rs2.at[p], s.rs3, s.rs4.at[p])()()
-    s.x[l + 1] = s.x[l] + total
+    s.h[l, q, 0] = first.astype(s.h.dtype)
+    output_scan(dt, du, bg, cg, a2, (first,), s.h.at[l, q, pl.ds(1, rows)], s.w1, s.ys.at[l, part])
+
+    ys = s.ys[l, part] + s.skip[l : l + 1, :] * s.u[l, part].astype(F32)
+    s.ys[l, part] = ys
+    z = s.z[l, part]
+    s.go[l, part] = (ys * z * jax.nn.sigmoid(z)).astype(BF16)
+    s.pending[l].append(start(net.copy(s.go.at[l, part], s.got.at[l, part], me.at(dp=me.twin), net.slots())))
+    loads("wout", l)
+    s.part[q] = dot(s.go[l, part], s.wout[l], 1, 0)
+    second = scatter_sum(net, me, s.part.at[q], own_rows, s.rs1.at[q], s.rs2.at[p, q], s.rs3.at[q], s.rs4.at[p, q])
+    yield
+    finish = second()
+    yield
+    s.x[l + 1, q] = s.x[l, q] + finish()
 
 
 def small_rows(rows, blocks):
@@ -633,20 +744,19 @@
 def gradient_chunks(net, me, l, s):
     rows = s.dt.shape[1]
     chans = s.dt.shape[2]
-    width = s.x.shape[2]
+    width = s.x.shape[3]
     wide = chans // 2
     table, _ = chunk_table(width, chans, me.blocks, s.small.shape[1])
     levels = me.blocks.bit_length() - 1
-    hn = s.hn.at[l, pl.ds(EDGE, rows)]
+    block = rows // s.seqs
+    copy = l % s.gm.shape[0]
 
     def bufs(base, half):
-        first, sends, gots, size = base // 2, [], [], half
-        for b in range(1, levels):
-            size //= 2
-            r = pl.ds((base // 2) // 2**b, size)
-            sends.append(s.zs.at[b - 1, r])
-            gots.append(s.zr.at[l, b - 1, r])
-        return s.gm.at[pl.ds(first, half)], sends, gots, s.sh.at[pl.ds((base // 2) // 2 ** (levels - 1), size)]
+        first, size = base // 2, half >> (levels - 1)
+        return (
+            s.gm.at[copy, pl.ds(first, half)], s.zs.at[copy, pl.ds(first * 3 // 4, half * 3 // 4)],
+            s.zr.at[l, pl.ds(first * 3 // 2, half * 3 // 2)], s.sh.at[copy, pl.ds(first >> (levels - 1), size)],
+        )
 
     def out_fill(first, place, half):
         def fill(gm):
@@ -658,8 +768,10 @@
 
     def in_fill(first, half, own, other):
         def fill(gm):
-            mine = dot(hn[:, first : first + half], own[me.inner], 0, 0)
-            gm[...] = mine + dot(s.hnt[l, :, first : first + half], other[...], 0, 0)
+            total = dot(s.hnt[l, :, first : first + half], other[...], 0, 0)
+            for q in range(s.seqs):
+                total = total + dot(s.hn[l, q, EDGE:, first : first + half], own[me.inner, q * block : (q + 1) * block, :], 0, 0)
+            gm[...] = total
             yield from ()
         return fill
 
@@ -679,101 +791,113 @@
             "conv": lambda: in_fill(begin, half, s.dxh, s.dxr.at[l]),
             "small": lambda: small_fill,
         }[kind]()
-        first = [transfer(0, half * wide)] if kind == "small" else []
+        first = [transfer("x", half * wide)] if kind == "small" else []
         chunk = reduce_chunk(net, me, s.local.at[l, i], s.gout.at[l], base, half, fill, bufs(base, half))
-        made[kind].append((chunk, chunk_plan(levels, half * wide, first)))
+        made[kind].append((chunk, chunk_plan(levels, half * wide, first), (copy, base)))
     return made["out"], made["gate"], made["conv"], made["small"]
 
 
-def backward_layer(net, me, l, s, pump):
-    own_rows = s.x.shape[1]
-    rows = s.dt.shape[1]
-    seqs = s.seqs
+def backward_layer(net, me, l, q, s, pump):
+    own_rows = s.x.shape[2]
+    rows = own_rows * me.lanes
     chans = s.dt.shape[2]
+    wide = chans // 2
+    width = s.x.shape[3]
     states = s.dlog.shape[1]
     rank = s.stp.shape[1]
     taps = s.ck.shape[1]
+    xw = s.xd.shape[2]
+    v0 = xw + rank + states
     p = 2 * l + 1
-    out, gate, conv, small = gradient_chunks(net, me, l, s)
-
-    at = pl.multiple_of(me.mp * own_rows, 16)
-    s.do[pl.ds(at, own_rows), :] = s.tgrad[...].astype(BF16)
-    gathered = gather_rows(net, me, s.do, 0, own_rows)
-    pump.spend(4)
-    gathered()
-    half = s.do.shape[1] // 2
-    theirs = pl.ds(pl.multiple_of((1 - me.inner) * half, 128), half)
-    do_sent = start(net.copy(s.do.at[:, theirs], s.dor.at[l], me.at(dp=me.twin), net.slots()))
+    part = pl.ds(q * rows, rows)
+    own = pl.ds(q * own_rows, own_rows)
+    final = q == s.seqs - 1
+    if q == 0:
+        s.chunks[l] = gradient_chunks(net, me, l, s)
+    out, gate, conv, small = s.chunks[l]
+    twin = me.at(dp=me.twin)
+
+    def keep(first, value):
+        for i in range(2):
+            place = (i, slice(first, first + value.shape[0]))
+            half = value[:, i * wide : (i + 1) * wide]
+            s.small[place] = half if q == 0 else s.small[place] + half
+
+    s.do[pl.ds(pl.multiple_of(q * rows + me.mp * own_rows, 16), own_rows), :] = s.tgrad[own, :].astype(BF16)
+    second = gather_rows(net, me, s.do, q * rows, own_rows)
+    pump.spend(0.5)
+    yield
+    finish = second()
     pump.spend(1.5)
-    dgo = dot(s.do[...], s.wout[l], 1, 1)
-    z = s.z[l]
+    yield
+    finish()
+    if final:
+        theirs = pl.ds(pl.multiple_of((1 - me.inner) * (width // 2), 128), width // 2)
+        do_sent = start(net.copy(s.do.at[:, theirs], s.dor.at[l], twin, net.slots()))
+    dgo = dot(s.do[part, :], s.wout[l], 1, 1)
+    z = s.z[l, part]
     sg = jax.nn.sigmoid(z)
-    s.dy[...] = dgo * z * sg
-    dz = (dgo * s.ys[l] * silu_slope(z, sg)).astype(BF16)
-    s.dz[...] = dz
+    s.dy[part, :] = dgo * z * sg
+    dz = (dgo * s.ys[l, part] * silu_slope(z, sg)).astype(BF16)
+    s.dz[part, :] = dz
     for i in range(2):
-        s.dzh[i] = dz[:, i * chans // 2 : (i + 1) * chans // 2]
-    pump.spend(1.5)
-
-    s.du[...] = s.dt[l] * s.u[l].astype(F32)
+        s.dzh[i, part, :] = dz[:, i * wide : (i + 1) * wide]
+
+    s.du[part, :] = s.dt[l, part] * s.u[l, part].astype(F32)
     an = -jnp.exp(s.dlog[l])
     a2 = an * LOG2E
-    zero = jnp.zeros_like(a2)
-    own = adjoint_totals(s.dt.at[l], s.dy, s.cg.at[l], a2, (zero,) * seqs)
+    dt, du, dy, bg, cg = s.dt.at[l, part], s.du.at[part], s.dy.at[part], s.bg.at[l, q], s.cg.at[l, q]
+    end = adjoint_totals(dt, dy, cg, a2, (jnp.zeros_like(a2),))[0]
     second = entering_state(
-        net, me, own, s.sums.at[l], a2, s.st1, s.got1.at[p], s.st2, s.got2.at[p], False
+        net, me, end, s.sums.at[l], q, a2, s.st1.at[q], s.got1.at[p, q], s.st2.at[q], s.got2.at[p, q], False
     )
-    dz_sent = start(net.copy(s.dzh.at[1 - me.inner], s.dzr.at[l], me.at(dp=me.twin), net.slots()))
-    pump.spend(2.8)
-    hn_sent, go_sent = s.pending[l]
-    do_sent.wait()
-    go_sent.wait()
-    pump.add(out)
+    if final:
+        dz_sent = start(net.copy(s.dzh.at[1 - me.inner], s.dzr.at[l], twin, net.slots()))
+    pump.spend(2.5)
+    yield
     finish = second()
-    hn_sent.wait()
-    dz_sent.wait()
-    pump.add(gate)
+    if final:
+        do_sent.wait()
+        for copy in s.pending[l]:
+            copy.wait()
+        pump.add(out)
+        dz_sent.wait()
+        pump.add(gate)
+    pump.spend(1.5)
+    yield
+    last = finish()
     pump.spend(1)
-    last = finish()
-    pump.spend(2.5)
     acc = adjoint_scan(
-        s.dt.at[l], s.du, s.dy, s.bg.at[l], s.cg.at[l], a2, an, last, s.h.at[l], s.q, s.w1, s.w2, s.s1, s.s2,
-        lambda: pump.spend(1.5), 4,
+        dt, du, dy, bg, cg, a2, an, (last,), s.h.at[l, q], s.q.at[q], s.w1, s.w2, s.s1.at[part], s.s2.at[part],
+        lambda: pump.spend(1.5), 2,
     )
-    x0 = s.xd.shape[1] - 2 * states
-    state_sums(s.q, 0, s.du, s.xd.at[p, pl.ds(x0, states)])
-    state_sums(s.h.at[l], seqs, s.dy, s.xd.at[p, pl.ds(x0 + states, states)])
-
-    pump.spend(2)
-
-    u = s.u[l].astype(F32)
-    dpre = ((s.s1[...] + s.s2[...] * u) * softplus_slope(s.dt[l])).astype(BF16)
-    s.s2[...] = s.s2[...] * s.dt[l] + s.skip[l : l + 1, :] * s.dy[...]
-    s.xd[p, 0:rank, :] = dot(s.stp[l], dpre, 1, 1)
-    second = sum_lanes(net, me, s.xd.at[p], s.xd1.at[p], s.xdf, s.xd2.at[p])
-    xw = s.xd.shape[1]
-    v0 = xw + rank + states
-
-    def keep(first, value):
-        for i in range(2):
-            s.small[i, first : first + value.shape[0], :] = value[:, i * chans // 2 : (i + 1) * chans // 2]
-
-    keep(xw, dot(s.dtr[l], dpre, 1, 0))
+    x0 = xw - 2 * states
+    state_sums(s.q.at[q], 0, du, s.xd.at[p, q, pl.ds(x0, states)])
+    state_sums(s.h.at[l, q], 1, dy, s.xd.at[p, q, pl.ds(x0 + states, states)])
+    pump.spend(0.7)
+
+    u = s.u[l, part].astype(F32)
+    dpre = ((s.s1[part, :] + s.s2[part, :] * u) * softplus_slope(s.dt[l, part])).astype(BF16)
+    s.s2[part, :] = s.s2[part, :] * s.dt[l, part] + s.skip[l : l + 1, :] * s.dy[part, :]
+    s.xd[p, q, 0:rank, :] = dot(s.stp[l], dpre, 1, 1)
+    second = sum_lanes(net, me, s.xd.at[p, q], s.xd1.at[p, q], s.xdf.at[q], s.xd2.at[p, q])
+    keep(xw, dot(s.dtr[l, q], dpre, 1, 0))
     keep(xw + rank, an * acc)
     keep(v0 + taps + 2, jnp.sum(dpre.astype(F32), axis=0, keepdims=True))
-    keep(v0 + taps + 1, jnp.sum(s.dy[...] * u, axis=0, keepdims=True))
-    pump.spend(1)
+    keep(v0 + taps + 1, jnp.sum(s.dy[part, :] * u, axis=0, keepdims=True))
+    pump.spend(0.7)
+    yield
     finish = second()
-    pump.spend(3.5)
+    pump.spend(1.5)
+    yield
     dxr = finish().astype(BF16)
-    pump.spend(0.5)
-    xc = s.xc[l]
-    du = s.s2[...] + dot(dxr, s.stt[l], 0, 0)
+    xc = s.xc[l, part]
+    du = s.s2[part, :] + dot(dxr, s.stt[l], 0, 0)
     dxc = du * silu_slope(xc, jax.nn.sigmoid(xc))
-    s.dxc[0:rows, :] = dxc
+    s.dxc[q, 0:rows, :] = dxc
 
     slot = net.slots()
-    edge = net.copy(s.dxc.at[pl.ds(0, 8)], s.tail.at[l], me.at(dp=me.dp - 1), slot)
+    edge = net.copy(s.dxc.at[q, pl.ds(0, 8)], s.tail.at[l, q], me.at(dp=me.dp - 1), slot)
 
     @pl.when(me.dp > 0)
     def _():
@@ -781,53 +905,60 @@
 
     @pl.when(me.dp == me.blocks - 1)
     def _():
-        s.tail[l] = jnp.zeros((8, chans), F32)
-
-    keep(0, dot(dxr, s.u[l], 1, 0))
+        s.tail[l, q] = jnp.zeros((8, chans), F32)
+
+    keep(0, dot(dxr, s.u[l, part], 1, 0))
     keep(v0 + taps, jnp.sum(dxc, axis=0, keepdims=True))
     for k in range(taps):
-        off = EDGE - seqs * (taps - 1 - k)
-        keep(v0 + k, jnp.sum(dxc * s.xi[l, off : off + rows, :], axis=0, keepdims=True))
-    s.part[...] = dot(s.dz[...], s.win[l, 1], 1, 1)
-    pump.spend(1.5)
+        off = EDGE - (taps - 1 - k)
+        keep(v0 + k, jnp.sum(dxc * s.xi[l, q, off : off + rows, :], axis=0, keepdims=True))
+    s.part[q] = dot(s.dz[part, :], s.win[l, 1], 1, 1)
+    pump.spend(1)
+    yield
 
     @pl.when(me.dp < me.blocks - 1)
     def _():
-        net.copy(s.dxc.at[pl.ds(0, 8)], s.tail.at[l], me.at(dp=me.twin), slot).wait_recv()
-
-    s.dxc[rows : rows + 8, :] = s.tail[l]
+        net.copy(s.dxc.at[q, pl.ds(0, 8)], s.tail.at[l, q], twin, slot).wait_recv()
+
+    s.dxc[q, rows : rows + 8, :] = s.tail[l, q]
     dxi = jnp.zeros((rows, chans), F32)
     for k in range(taps):
-        off = seqs * (taps - 1 - k)
-        dxi = dxi + s.ck[l, k : k + 1, :].astype(F32) * s.dxc[off : off + rows, :]
+        off = taps - 1 - k
+        dxi = dxi + s.ck[l, k : k + 1, :].astype(F32) * s.dxc[q, off : off + rows, :]
     dxi = dxi.astype(BF16)
     for i in range(2):
-        s.dxh[i] = dxi[:, i * chans // 2 : (i + 1) * chans // 2]
-    dxi_sent = start(net.copy(s.dxh.at[1 - me.inner], s.dxr.at[l], me.at(dp=me.twin), net.slots()))
-
-    s.part[...] = s.part[...] + dot(dxi, s.win[l, 0], 1, 1)
-    second = scatter_sum(net, me, s.part, own_rows, s.rs1, s.rs2.at[p], s.rs3, s.rs4.at[p])
-    pump.spend(2)
+        s.dxh[i, part, :] = dxi[:, i * wide : (i + 1) * wide]
+    if final:
+        dxi_sent = start(net.copy(s.dxh.at[1 - me.inner], s.dxr.at[l], twin, net.slots()))
+
+    s.part[q] = s.part[q] + dot(dxi, s.win[l, 0], 1, 1)
+    second = scatter_sum(net, me, s.part.at[q], own_rows, s.rs1.at[q], s.rs2.at[p, q], s.rs3.at[q], s.rs4.at[p, q])
+    pump.spend(1)
+    yield
     finish = second()
-    dxi_sent.wait()
-    pump.add(conv)
-    pump.spend(3)
+    if final:
+        dxi_sent.wait()
+        pump.add(conv)
+    pump.spend(1.5)
+    yield
     dhn = finish()
-    x = s.x[l]
+    x = s.x[l, q]
     inv = rms(x)
-    part = jnp.sum(dhn * x * inv, axis=0, keepdims=True)
-    g0 = v0 + 8
-    wide = chans // 2
-    count = x.shape[1] // wide
+    gain = jnp.sum(dhn * x * inv, axis=0, keepdims=True)
+    count = width // wide
     for j in range(count):
-        s.gg[l * count + j : l * count + j + 1, :] = part[:, j * wide : (j + 1) * wide]
+        place = slice(l * count + j, l * count + j + 1)
+        piece = gain[:, j * wide : (j + 1) * wide]
+        s.gg[place, :] = piece if q == 0 else s.gg[place, :] + piece
     dr = dhn * s.gain[l : l + 1, :]
-    s.tgrad[...] = s.tgrad[...] + inv * dr - x * (inv * inv * inv) * jnp.mean(dr * x, axis=-1, keepdims=True)
+    s.tgrad[own, :] = s.tgrad[own, :] + inv * dr - x * (inv * inv * inv) * jnp.mean(dr * x, axis=-1, keepdims=True)
 
     @pl.when(me.dp > 0)
     def _():
         edge.wait_send()
 
+    if not final:
+        return
     for i in range(2):
         s.small[i, v0 + taps + 3 :, :] = jnp.zeros((s.small.shape[1] - v0 - taps - 3, wide), F32)
     if l > 0:
@@ -838,12 +969,19 @@
     finish = second()
     pump.spend(2.5)
     total = finish()
-    layers = s.gain.shape[0]
-    for k in range(layers):
+    for k in range(s.gain.shape[0]):
         for i in range(2):
-            at, of = g0 + k * (count // 2), k * count + i * (count // 2)
+            at, of = v0 + 8 + k * (count // 2), k * count + i * (count // 2)
             s.small[i, at : at + count // 2, :] = total[of : of + count // 2]
     pump.add(small)
+
+
+def side_by_side(streams):
+    while streams:
+        streams = [stream for stream in streams if next(stream, s_end) is not s_end]
+
+
+s_end = object()
 
 
 class Refs:
@@ -854,21 +992,31 @@
     s = Refs()
     for name, ref in zip(names, refs, strict=True):
         setattr(s, name, ref)
-    s.seqs, s.pending = seqs, {}
     me = Place(blocks, lanes)
     net = Net(s.send, s.recv)
-    arrived = entry_barrier(me)
+    arrive = [entry_barrier(me)]
     loads = load_weights(s)
-    seg = s.tok.shape[0]
-    for p in range(seg):
-        s.x[0, p * seqs : (p + 1) * seqs, :] = s.tok[p].astype(F32)
     layers = s.gain.shape[0]
-    for l in range(layers):
-        forward_layer(net, me, l, s, loads, arrived)
-    s.lout[...] = s.x[layers].astype(s.lout.dtype)
+    s.seqs, s.pending, s.shared, s.chunks = seqs, {l: [] for l in range(layers)}, {}, {}
+    for p in range(s.tok.shape[0]):
+        row = s.tok[p].astype(F32)
+        for q in range(seqs):
+            s.x[0, q, p : p + 1, :] = row[q : q + 1, :]
+
+    def arrived():
+        if arrive:
+            arrive.pop()()
+
     pump = Pump()
-    for l in reversed(range(layers)):
-        backward_layer(net, me, l, s, pump)
+
+    def stream(q):
+        for l in range(layers):
+            yield from forward_layer(net, me, l, q, s, loads, arrived)
+        s.lout[pl.ds(q * s.tok.shape[0], s.tok.shape[0]), :] = s.x[layers, q]
+        for l in reversed(range(layers)):
+            yield from backward_layer(net, me, l, q, s, pump)
+
+    side_by_side([stream(q) for q in range(seqs)])
     pump.drain()
 
 
@@ -885,25 +1033,27 @@
     table, grads = chunk_table(width, chans, blocks, small)
     chunks = len(table)
     wide = chans // 2
-    groups = rows // GRP
-    slots = layers * (3 * 2 + 2 * 3 + 3 * 2 + lanes + blocks + 2 * (1 + outers) + 1)
-    slots += layers * (chunks * 2 * levels + 6)
+    block = rows // seqs
+    groups = block // GRP
+    slots = layers * (seqs * (3 * 2 + 2 * 3 + 3 * 2 + lanes + 2 * (1 + outers) + 3) + blocks + 4)
+    slots += layers * (chunks * (2 * levels + 2) + 6)
     two = 2 * layers
     ins = ["tok", "cot", "starts", "lengths", "gain", "win_hbm", "ck", "cb", "stt_hbm", "stp_hbm", "sb", "dlog", "skip", "wout_hbm"]
     outs = {
-        "lout": ((own_rows, width), BF16),
+        "lout": ((own_rows, width), F32),
         "tgrad": ((own_rows, width), F32),
         "gout": ((layers, grads, wide), BF16),
     }
     half = grads // 2
+    copies = layers if blocks <= 16 else 1
     scratch = {
         "win": (win.shape, BF16),
         "stt": (stt.shape, BF16),
         "stp": (stp.shape, BF16),
         "wout": (wout.shape, BF16),
-        "x": ((layers + 1, own_rows, width), F32),
-        "hn": ((layers, EDGE + rows, width), BF16),
-        "xi": ((layers, EDGE + rows, chans), F32),
+        "x": ((layers + 1, seqs, seg, width), F32),
+        "hn": ((layers, seqs, EDGE + block, width), BF16),
+        "xi": ((layers, seqs, EDGE + block, chans), F32),
         "xc": ((layers, rows, chans), F32),
         "u": ((layers, rows, chans), BF16),
         "z": ((layers, rows, chans), F32),
@@ -911,34 +1061,34 @@
         "du": ((rows, chans), F32),
         "ys": ((layers, rows, chans), F32),
         "go": ((layers, rows, chans), BF16),
-        "dtr": ((layers, rank, rows), BF16),
-        "bg": ((layers, groups, states, GRP), F32),
-        "cg": ((layers, groups, states, GRP), F32),
-        "h": ((layers, rows + seqs, states, chans), BF16),
-        "q": ((rows, states, chans), BF16),
+        "dtr": ((layers, seqs, rank, block), BF16),
+        "bg": ((layers, seqs, groups, states, GRP), F32),
+        "cg": ((layers, seqs, groups, states, GRP), F32),
+        "h": ((layers, seqs, block + 1, states, chans), BF16),
+        "q": ((seqs, block, states, chans), BF16),
         "w1": ((chans // 128, GRP * 8, 128), F32),
         "w2": ((chans // 128, GRP * 8, 128), F32),
         "do": ((rows, width), BF16),
         "dy": ((rows, chans), F32),
-        "tail": ((layers, 8, chans), F32),
+        "tail": ((layers, seqs, 8, chans), F32),
         "dz": ((rows, chans), BF16),
         "s1": ((rows, chans), F32),
         "s2": ((rows, chans), F32),
-        "dxc": ((rows + 8, chans), F32),
-        "part": ((rows, width), F32),
-        "rs1": ((2, own_rows, width), BF16),
-        "rs2": ((two, 2, own_rows, width), BF16),
-        "rs3": ((own_rows, width), BF16),
-        "rs4": ((two, own_rows, width), BF16),
-        "xd": ((two, xw, rows), F32),
-        "xd1": ((two, xw, rows), F32),
-        "xdf": ((xw, rows), BF16),
-        "xd2": ((two, xw, rows), BF16),
+        "dxc": ((seqs, block + 8, chans), F32),
+        "part": ((seqs, block, width), F32),
+        "rs1": ((seqs, 2, seg, width), BF16),
+        "rs2": ((two, seqs, 2, seg, width), BF16),
+        "rs3": ((seqs, seg, width), BF16),
+        "rs4": ((two, seqs, seg, width), BF16),
+        "xd": ((two, seqs, xw, block), F32),
+        "xd1": ((two, seqs, xw, block), F32),
+        "xdf": ((seqs, xw, block), BF16),
+        "xd2": ((two, seqs, xw, block), BF16),
         "sums": ((layers, blocks, seqs * chans // 128, 128), F32),
         "st1": ((seqs, states, chans), BF16),
         "got1": ((two, seqs, states, chans), BF16),
         "st2": ((seqs, states, chans), BF16),
-        "got2": ((two, outers, seqs, states, chans), BF16),
+        "got2": ((two, seqs, outers, states, chans), BF16),
         "small": ((2, small, wide), F32),
         "smalls": ((small, wide), BF16),
         "smallr": ((layers, small, wide), BF16),
@@ -953,10 +1103,10 @@
         "dzr": ((layers, rows, wide), BF16),
         "dxh": ((2, rows, wide), BF16),
         "dxr": ((layers, rows, wide), BF16),
-        "gm": ((half, wide), F32),
-        "zs": ((levels - 1, half // 2, wide), BF16),
-        "zr": ((layers, levels - 1, half // 2, wide), BF16),
-        "sh": ((half // 2 ** (levels - 1), wide), BF16),
+        "gm": ((copies, half, wide), F32),
+        "zs": ((copies, half * 3 // 4, wide), BF16),
+        "zr": ((layers, half * 3 // 2, wide), BF16),
+        "sh": ((copies, half // 2 ** (levels - 1), wide), BF16),
     }
     names = ins + list(outs) + list(scratch) + ["loaded", "local", "send", "recv"]
     any_space = pl.BlockSpec(memory_space=pl.ANY)
@@ -1028,8 +1178,9 @@
         for copy in fetch:
             copy.wait()
         for p in range(seg):
-            s.lout[p] = s.lov[p * seqs : (p + 1) * seqs, :]
-            s.tgrad[p] = s.tgv[p * seqs : (p + 1) * seqs, :]
+            for to, of in ((s.lout, s.lov), (s.tgrad, s.tgv)):
+                both = [of[q * seg + p : q * seg + p + 1, :] for q in range(seqs)]
+                to[p] = jnp.concatenate(both, axis=0).astype(to.dtype)
 
 
 def unpack_call(table, lout, tgrad, gout, shape, gain, win, ck, sp, stp, dlog, wout):
@@ -1054,7 +1205,7 @@
         out_shape=[jax.ShapeDtypeStruct(a, t) for a, t in outs.values()],
         in_specs=[pl.BlockSpec(memory_space=pl.ANY), pl.BlockSpec(memory_space=pl.ANY), layer(gout.shape)],
         out_specs=[whole(a) if name in once else layer(a) for name, (a, _) in outs.items()],
-        scratch_shapes=[VMEM(lout.shape, BF16), VMEM(tgrad.shape, F32), pltpu.SemaphoreType.DMA((2,))],
+        scratch_shapes=[VMEM(lout.shape, F32), VMEM(tgrad.shape, F32), pltpu.SemaphoreType.DMA((2,))],
         compiler_params=pltpu.CompilerParams(vmem_limit_bytes=50 * 2**20),
     )(lout, tgrad, gout)
 

time: 243 us -> 232 us (0.955)
  Pallas kernels: 240 us -> 229 us
    pallas_call x1, Pallas kernels: 232 us -> 221 us  [layers_call(): pl.pallas_call(functools.partial(kernel, names, seqs, blocks, lanes), out...]
where the time goes in v4:
time: 232 us
  Pallas kernels  229 us (99%)
    pallas_call x1, Pallas kernels, layers_call(): pl.pallas_call(functools.partial(kernel, names, seqs, blocks, lanes), out...  221 us
    pallas_call x1, Pallas kernels, unpack_call(): pl.pallas_call(functools.partial(unpack_kernel, ins + list(outs) + ['lov'...  7.76 us

profile of v4, /device:TPU:0, one launch (start us, length us, event | category | flops | bytes accessed | tf_op | source)
XLA Modules:
  0.0 231.8 jit_solution(1750550483900357827)
XLA Ops:
  0.6 221.3 %shard_map.229 = (f32[64,1024]{1,0:T(8,128)}, f32[64,1024]{1,0:T(8,128)}, bf16[2,6528,256]{2,1,0:T(8,128)(2,1)}) custom-call(bf16[32,2,1024]{2,1,0:T(2,128)(2,1)} %refs_0_.1, bf16[32,2,1024]{2,1,0:T(2,128)(2,1)} %refs_1_.1, s32[2,32]{1,0:T(2,128)} %bitcast.4, s32[2]{0:T(128)} %refs_3_.1, f32[2,1024]{1,0:T(2,128)} %refs_4_.1, ...), custom_call_target="tpu_custom_call" | custom-call | tf_op jit(solution)/shard_map/pallas_call | solution.py:1115
  221.9 0.0 copy-start
  221.9 0.9 copy-done
  222.9 0.0 copy-start.1
  222.9 0.9 copy-done.1
  223.8 7.8 %shard_map.230 = (bf16[32,2,1024]{2,1,0:T(2,128)(2,1)}, f32[32,2,1024]{2,1,0:T(2,128)}, f32[2,1024]{1,0:T(2,128)}, f32[2,2,1024,512]{3,2,1,0:T(8,128)}, f32[2,4,...) custom-call(f32[64,1024]{1,0:T(8,128)S(1)} %copy-done, ...), custom_call_target="tpu_custom_call" | custom-call | tf_op jit(solution)/shard_map/pallas_call | solution.py:1202
Async XLA Ops:
  221.9 1.0 copy-start
  222.9 0.9 copy-start.1

commit v5 on v4

--- a/solution.py
+++ b/solution.py
@@ -15,7 +15,7 @@
 MESH = pl.DeviceIdType.MESH
 VMEM = pltpu.VMEM
 HALF = 512
-GSPACE = [False]
+
 EDGE = 16
 
 GRP = 16
@@ -371,7 +371,7 @@
 
 
 class Pump:
-    latency, cost, early, scale = 2.0, 0.3, 1.0, 1.0
+    latency, cost, early, scale = 3.0, 0.3, 1.0, 1.2
 
     def __init__(self):
         self.now, self.free, self.active, self.quiet = 0.0, {}, [], False
@@ -1116,7 +1116,7 @@
         functools.partial(kernel, names, seqs, blocks, lanes),
         out_shape=[jax.ShapeDtypeStruct(a, t) for a, t in outs.values()],
         in_specs=[any_space if n.endswith("_hbm") else smem if n == "lengths" else vmem for n in ins],
-        out_specs=[vmem, vmem, GSPACE[0] and vmem or any_space],
+        out_specs=[vmem, vmem, any_space],
         scratch_shapes=[VMEM(a, t) for a, t in scratch.values()] + sems,
         compiler_params=pltpu.CompilerParams(
             collective_id=0, has_side_effects=True, vmem_limit_bytes=63 * 2**20

time: 232 us -> 223 us (0.961)
  Pallas kernels: 229 us -> 220 us
    pallas_call x1, Pallas kernels: 221 us -> 212 us  [layers_call(): pl.pallas_call(functools.partial(kernel, names, seqs, blocks, lanes), out...]
where the time goes in v5:
time: 223 us
  Pallas kernels  220 us (99%)
    pallas_call x1, Pallas kernels, layers_call(): pl.pallas_call(functools.partial(kernel, names, seqs, blocks, lanes), out...  212 us
    pallas_call x1, Pallas kernels, unpack_call(): pl.pallas_call(functools.partial(unpack_kernel, ins + list(outs) + ['lov'...  7.76 us

profile of v5, /device:TPU:0, one launch (start us, length us, event | category | flops | bytes accessed | tf_op | source)
XLA Modules:
  0.0 222.8 jit_solution(7832827312804488165)
XLA Ops:
  0.6 212.3 %shard_map.229 = (f32[64,1024]{1,0:T(8,128)}, f32[64,1024]{1,0:T(8,128)}, bf16[2,6528,256]{2,1,0:T(8,128)(2,1)}) custom-call(bf16[32,2,1024]{2,1,0:T(2,128)(2,1)} %refs_0_.1, bf16[32,2,1024]{2,1,0:T(2,128)(2,1)} %refs_1_.1, s32[2,32]{1,0:T(2,128)} %bitcast.4, s32[2]{0:T(128)} %refs_3_.1, f32[2,1024]{1,0:T(2,128)} %refs_4_.1, ...), custom_call_target="tpu_custom_call" | custom-call | tf_op jit(solution)/shard_map/pallas_call | solution.py:1115
  213.0 0.0 copy-start
  213.0 0.9 copy-done
  213.9 0.0 copy-start.1
  213.9 0.9 copy-done.1
  214.9 7.8 %shard_map.230 = (bf16[32,2,1024]{2,1,0:T(2,128)(2,1)}, f32[32,2,1024]{2,1,0:T(2,128)}, f32[2,1024]{1,0:T(2,128)}, f32[2,2,1024,512]{3,2,1,0:T(8,128)}, f32[2,4,...) custom-call(f32[64,1024]{1,0:T(8,128)S(1)} %copy-done, ...), custom_call_target="tpu_custom_call" | custom-call | tf_op jit(solution)/shard_map/pallas_call | solution.py:1202
Async XLA Ops:
  213.0 1.0 copy-start
  213.9 0.9 copy-start.1
